TPU v7x, 512 devices: a whole 4x8x8 slice. The times are simulated.
512 devices in a mesh: ctx: 64 (over y, z_lo, core), grp: 8 (over z_hi, x).
Axes of the slice: x: 4, y: 8, z: 8 (z_hi: 2, z_lo: 4; z = z_hi * 4 + z_lo), core: 2. Of those that a mesh axis runs over, the one named last changes fastest.
Arguments:
- queries: bfloat16 [128, 8192], P('ctx', 'grp'), may hold values from -100 to 100
- fresh_keys: bfloat16 [128, 1024], P('ctx', 'grp'), may hold values from -5 to 5
- fresh_values: bfloat16 [128, 1024], P('ctx', 'grp'), may hold values from -5 to 5
- key_cache: bfloat16 [1536, 128, 1024], P('ctx', None, 'grp'), may hold values from -5 to 5
- value_cache: bfloat16 [1536, 128, 1024], P('ctx', None, 'grp'), may hold values from -5 to 5
- lengths: int32 [128], replicated, may hold values from 1 to 16384, as said below
- block_table: int32 [128, 128], replicated, may hold values from 0 to 1535, as said below
- resid: bfloat16 [128, 8192], P(None, 'ctx'), may hold values from -0.1796875 to 0.1796875
- out_weight: bfloat16 [8192, 8192], P('grp', 'ctx'), may hold values from -0.0625 to 0.0625
- norm_gain: bfloat16 [8192], P('ctx'), may hold values from 0.099609375 to 1.8984375
- gate_weight: bfloat16 [8192, 28672], P('ctx', 'grp'), may hold values from -0.0625 to 0.0625
- up_weight: bfloat16 [8192, 28672], P('ctx', 'grp'), may hold values from -0.0625 to 0.0625
- down_weight: bfloat16 [28672, 8192], P('grp', 'ctx'), may hold values from -0.03125 to 0.03125
- row_order: int32 [128], replicated, may hold values from 0 to 127, each once
Outputs:
- mixed: bfloat16 [128, 8192], P('grp', 'ctx')
Inputs may be any that keep to these rules, and one draw needn't show every extreme that they name: Page j of request r lies in slot block_table[r, j], which is row block_table[r, j] % 24 of the cache on ctx index block_table[r, j] // 24. The live pages j < ceil(lengths[r] / 128) of all requests together name every slot exactly once; entries at or beyond a request's last live page repeat that page's slot. At most 16384 tokens a request, reached by one request in every draw; the live pages of all requests, ceil(lengths[r] / 128) each, add up to 1536.
All inputs are finite; a program needn't handle non-finite values.
Results may differ from a plain program's by a relative error of at most 0.025.
Values may be sent and summed in bfloat16 or wider, within the bound.
No kernel may reach another device: no remote copies, remote signals or barrier semaphores. Data moves between devices by JAX's collectives and lax.ppermute only.
A program may use at most 128 MiB of HBM per device.

v0:
```python
import jax
import jax.numpy as jnp
from jax import lax
from jax.sharding import PartitionSpec as P

H = 64
KVH = 8
HD = 128


EPS = 1e-05


def passed_along(block, axis, distance):
    devices = range(lax.axis_size(axis))
    route = [((i - distance) % len(devices), i) for i in devices]
    return lax.ppermute(block, axis, route)


def slot_layout(block_table, lengths, first_slot, slots_dev, page_len):
    slot_ids = first_slot + jnp.arange(slots_dev, dtype=jnp.int32)
    page_ids = jnp.arange(block_table.shape[1], dtype=jnp.int32)
    page_count = (lengths + page_len - 1) // page_len
    live_page = page_ids[None, :] < page_count[:, None]
    matches = (block_table[None, :, :] == slot_ids[:, None, None]) & live_page[None, :, :]
    owned_rows = jnp.any(matches, axis=2)
    request_ids = jnp.arange(block_table.shape[0], dtype=jnp.int32)
    owner_row = jnp.sum(jnp.where(owned_rows, request_ids[None, :], 0), axis=1)
    page_no = jnp.sum(jnp.where(matches, page_ids[None, None, :], 0), axis=(1, 2))
    live_count = jnp.sum(jnp.where(owned_rows, lengths[None, :], 0), axis=1) - page_no * page_len
    live_mask = jnp.arange(page_len, dtype=jnp.int32)[None, :] < live_count[:, None]
    return (owner_row, live_mask)


def own_partial(query_heads, fresh_keys, fresh_values, inv_root):
    req_dev, kv_local, group_size, head_size = query_heads.shape
    key_heads = fresh_keys.reshape(req_dev, kv_local, head_size)
    own_max = (
        jnp.einsum("rkgd,rkd->rkg", query_heads, key_heads, preferred_element_type=jnp.float32)
        * inv_root
    )
    own_sum = jnp.ones_like(own_max)
    value_heads = fresh_values.reshape(req_dev, kv_local, 1, head_size).astype(jnp.float32)
    own_acc = jnp.broadcast_to(value_heads, (req_dev, kv_local, group_size, head_size))
    return (own_max, own_sum, own_acc)


def absorb(partial_value, home_dev, key_rows, value_rows, token_owner, token_live, inv_root):
    query_wide, running_max, weight_sum, weighted = partial_value
    req_dev = query_wide.shape[0]
    row_ids = home_dev * req_dev + jnp.arange(req_dev, dtype=jnp.int32)
    allowed = (token_owner[None, :] == row_ids[:, None]) & token_live[None, :]
    scores = (
        jnp.einsum(
            "rkgd,tkd->rkgt",
            query_wide.astype(jnp.bfloat16),
            key_rows,
            preferred_element_type=jnp.float32,
        )
        * inv_root
    )
    scores = jnp.where(allowed[:, None, None, :], scores, -jnp.inf)
    new_max = jnp.maximum(running_max, jnp.max(scores, axis=3))
    weights = jnp.exp(scores - new_max[..., None])
    factor = jnp.exp(running_max - new_max)
    weight_sum = weight_sum * factor + jnp.sum(weights, axis=3)
    weighted = weighted * factor[..., None] + jnp.einsum(
        "rkgt,tkd->rkgd",
        weights.astype(jnp.bfloat16),
        value_rows,
        preferred_element_type=jnp.float32,
    )
    return (query_wide, new_max, weight_sum, weighted)


def shards(
    queries,
    fresh_keys,
    fresh_values,
    key_cache,
    value_cache,
    lengths,
    block_table,
    resid,
    out_weight,
    norm_gain,
    gate_weight,
    up_weight,
    down_weight,
    row_order,
):
    req_dev = queries.shape[0]
    kv_local = fresh_keys.shape[1] // HD
    group_size = H // KVH
    slots_dev = key_cache.shape[0]
    page_len = key_cache.shape[1]
    ctx_size = lax.axis_size("ctx")
    ctx_index = lax.axis_index("ctx")
    inv_root = HD ** (-0.5)
    owner_row, live_mask = slot_layout(
        block_table, lengths, ctx_index * slots_dev, slots_dev, page_len
    )
    query_heads = queries.reshape(req_dev, kv_local, group_size, HD)
    own_max, own_sum, own_acc = own_partial(query_heads, fresh_keys, fresh_values, inv_root)
    key_rows = key_cache.reshape(slots_dev * page_len, kv_local, HD)
    value_rows = value_cache.reshape(slots_dev * page_len, kv_local, HD)
    token_owner = jnp.repeat(owner_row, page_len)
    token_live = live_mask.reshape(-1)
    query_wide = query_heads.astype(jnp.float32)

    def visit(partial_value, home_dev):
        return absorb(
            partial_value, home_dev, key_rows, value_rows, token_owner, token_live, inv_root
        )

    def cycle_turn(step_no, partial_value):
        partial_value = visit(partial_value, (ctx_index - step_no) % ctx_size)
        moved = passed_along(
            (partial_value[0], partial_value[1], partial_value[2], partial_value[3]), "ctx", 1
        )
        return tuple(moved)

    final_state = lax.fori_loop(0, ctx_size, cycle_turn, (query_wide, own_max, own_sum, own_acc))
    local_out = (
        (final_state[3] / final_state[2][..., None]).astype(jnp.bfloat16).reshape(req_dev, -1)
    )
    attended = lax.all_gather(local_out, "ctx", axis=0, tiled=True)
    projected = lax.psum(jnp.dot(attended, out_weight, preferred_element_type=jnp.float32), "grp")
    hidden = (resid.astype(jnp.float32) + projected).astype(jnp.bfloat16)
    hidden_wide = hidden.astype(jnp.float32)
    squares = jnp.sum(hidden_wide * hidden_wide, axis=1)
    gained = (hidden_wide * norm_gain.astype(jnp.float32)[None, :]).astype(jnp.bfloat16)
    gate_part = jnp.dot(gained, gate_weight, preferred_element_type=jnp.float32)
    up_part = jnp.dot(gained, up_weight, preferred_element_type=jnp.float32)
    model_width = resid.shape[1] * ctx_size
    gate_sum, up_sum, square_sum = lax.psum((gate_part, up_part, squares), "ctx")
    inv_rms = lax.rsqrt(square_sum / model_width + EPS)[:, None]
    activated = (jax.nn.silu(gate_sum * inv_rms) * (up_sum * inv_rms)).astype(jnp.bfloat16)
    rows_out = row_order.shape[0] // lax.axis_size("grp")
    my_rows = lax.psum_scatter(
        jnp.dot(activated[row_order], down_weight, preferred_element_type=jnp.float32),
        "grp",
        scatter_dimension=0,
        tiled=True,
    )
    picked_rows = lax.dynamic_slice_in_dim(row_order, lax.axis_index("grp") * rows_out, rows_out)
    return (hidden_wide[picked_rows] + my_rows).astype(jnp.bfloat16)


def solution(mesh):
    in_specs = (
        P("ctx", "grp"),
        P("ctx", "grp"),
        P("ctx", "grp"),
        P("ctx", None, "grp"),
        P("ctx", None, "grp"),
        P(),
        P(),
        P(None, "ctx"),
        P("grp", "ctx"),
        P("ctx"),
        P("ctx", "grp"),
        P("ctx", "grp"),
        P("grp", "ctx"),
        P(),
    )
    out_specs = P("grp", "ctx")
    return jax.shard_map(shards, mesh=mesh, in_specs=in_specs, out_specs=out_specs, check_vma=False)
```

profile of v0, /device:TPU:1, one launch (start us, length us, event | category | flops | bytes accessed | tf_op | source)
XLA Modules:
  0.0 2015.0 jit_solution(481631204598213813)
XLA Ops:
  13.3 1153.3 %while.22 = (s32[]{:T(128)}, bf16[2,1,8,128]{3,2,0,1:T(8,128)(2,1)S(1)}, f32[2,1,8]{2,0,1:T(2,128)S(1)}, f32[2,1,8]{2,0,1:T(2,128)S(1)}, f32[2,1,8,128]{3,2,0,1:...) while((s32[]{:T(128)}, ...), condition=%wide.region_7.8_spmd.clone, body=%wide.region_4.7_spmd.clone.sunk | while | flops 25529408 | bytes 2285702 | solution.py:123
  13.3 5.5 collective-permute-start
  80.6 5.5 collective-permute-done.2
  116.6 5.5 collective-permute-done.2
  134.6 5.5 collective-permute-done.2
  152.6 5.5 collective-permute-done.2
  188.6 5.5 collective-permute-done.2
  206.6 5.5 collective-permute-done.2
  260.7 5.5 collective-permute-done.2
  278.7 5.5 collective-permute-done.2
  332.7 5.5 collective-permute-done.2
  350.7 5.5 collective-permute-done.2
  404.7 5.5 collective-permute-done.2
  422.7 5.5 collective-permute-done.2
  458.8 5.5 collective-permute-done.2
  476.8 5.5 collective-permute-done.2
  494.8 5.5 collective-permute-done.2
  530.8 5.5 collective-permute-done.2
  548.8 5.5 collective-permute-done.2
  602.8 5.5 collective-permute-done.2
  620.8 5.5 collective-permute-done.2
  674.9 5.5 collective-permute-done.2
  692.9 5.5 collective-permute-done.2
  746.9 5.5 collective-permute-done.2
  764.9 5.5 collective-permute-done.2
  800.9 5.5 collective-permute-done.2
  818.9 5.5 collective-permute-done.2
  1166.6 82.5 %all-gather = bf16[64,2,1024]{2,1,0:T(2,128)(2,1)S(1)} all-gather(bf16[1,2,1024]{2,1,0:T(2,128)(2,1)S(1)} %reshape.233), channel_id=1, replica_groups=mesh['ctx'=64,'grp'=8] {'ctx'}, dimensions={0}, use_global_device_ids=true | all-gather | bytes 266240 | tf_op jit(solution)/shard_map/all_gather | solution.py:127
  1250.2 106.5 %all-reduce.4.cloned.1.call-done = f32[128,128]{1,0:T(8,128)} async-done(((f32[128,128]{1,0:T(8,128)}), f32[128,128]{1,0:T(8,128)}) %all-reduce.4.cloned.1.call-update) | async-done | bytes 65552 | tf_op jit(solution)/shard_map/psum | solution.py:128
  1361.7 139.3 %psum.30 = f32[128]{0:T(128)S(1)} all-reduce(f32[128]{0:T(128)S(1)} %get-tuple-element.302), channel_id=1, replica_groups=mesh['ctx'=64,'grp'=8] {'ctx'}, use_global_device_ids=true, to_apply=%region_11.12 | all-reduce | flops 128 | bytes 1024 | tf_op jit(solution)/shard_map/psum | solution.py:136
  1500.9 412.8 %all-reduce.6.cloned.1.call-done = (f32[128,3584]{1,0:T(8,128)}, f32[128,3584]{1,0:T(8,128)}) async-done(((f32[128,3584]{1,0:T(8,128)}, f32[128,3584]{1,0:T(8,128)}), (f32[128,3584]{1,0:T(8,128)}, f32[128,3584]{1,0:T(8,128)})) %all-reduce.6.cloned.1.call-update) | async-done | bytes 3670032 | tf_op jit(solution)/shard_map/psum | solution.py:136
  1920.3 86.8 %reduce-scatter.2.cloned.1.call-done = f32[16,128]{1,0:T(8,128)} async-done(((f32[128,128]{1,0:T(8,128)}), f32[16,128]{1,0:T(8,128)}) %reduce-scatter.2.cloned.1.call-update) | async-done | bytes 8208 | tf_op jit(solution)/shard_map/reduce_scatter | solution.py:140
  (1238 shorter events, 1027.3 us)
Async XLA Ops:
  6.5 1350.2 %all-reduce.4.cloned.1.call-start = ((), (), s32[]{:S(2)}) async-start(), calls=%async_computation.1 | async-start | bytes 131072 | tf_op jit(solution)/shard_map/psum | solution.py:128
  13.3 18.7 collective-permute-start
  32.0 18.0 collective-permute-start
  50.1 18.0 collective-permute-start
  104.1 18.0 collective-permute-start
  122.1 18.0 collective-permute-start
  158.1 18.0 collective-permute-start
  176.1 18.0 collective-permute-start
  194.1 18.0 collective-permute-start
  230.1 18.0 collective-permute-start
  248.1 18.0 collective-permute-start
  266.1 18.0 collective-permute-start
  302.2 18.0 collective-permute-start
  320.2 18.0 collective-permute-start
  338.2 18.0 collective-permute-start
  374.2 18.0 collective-permute-start
  392.2 18.0 collective-permute-start
  446.2 18.0 collective-permute-start
  464.2 18.0 collective-permute-start
  500.2 18.0 collective-permute-start
  518.3 18.0 collective-permute-start
  536.3 18.0 collective-permute-start
  572.3 18.0 collective-permute-start
  590.3 18.0 collective-permute-start
  608.3 18.0 collective-permute-start
  644.3 18.0 collective-permute-start
  662.3 18.0 collective-permute-start
  680.3 18.0 collective-permute-start
  716.3 18.0 collective-permute-start
  734.4 18.0 collective-permute-start
  1250.1 663.6 %all-reduce.6.cloned.1.call-start = ((), (), s32[]{:S(2)}) async-start(), calls=%async_computation.3 | async-start | bytes 7340032 | tf_op jit(solution)/shard_map/psum | solution.py:136
  1361.0 646.1 %reduce-scatter.2.cloned.1.call-start = ((), (), s32[]{:S(2)}) async-start(), calls=%async_computation.2 | async-start | bytes 73728 | tf_op jit(solution)/shard_map/reduce_scatter | solution.py:140
  (233 other events, 7718.5 us)
Sparse Core Ops, SparseCore 0:
  1250.3 106.4 all-reduce.3
  1361.1 552.5 all-reduce.5
  1919.8 87.3 reduce-scatter.1
where the time goes:
time: 2030 us; the launch traced here: 2010 us
  waiting for transfers between devices  1030 us (51%)
  starting transfers between devices  505 us (25%)
  blocking collectives  222 us (11%)
  matrix products  195 us (10%)
  other arithmetic  33.9 us (2%)
    ppermute x256, starting transfers between devices, passed_along(): return lax.ppermute(block, axis, route)  505 us
    ppermute x256, waiting for transfers between devices, passed_along(): return lax.ppermute(block, axis, route)  427 us
    psum x1, waiting for transfers between devices, shards(): lax.psum((gate_part, up_part, squares), 'ctx')  413 us
    psum x1, blocking collectives, shards(): lax.psum((gate_part, up_part, squares), 'ctx')  139 us
    psum x1, waiting for transfers between devices, shards(): lax.psum(jnp.dot(attended, out_weight, preferred_element_type=jnp.float32...  107 us
    dot_general x64, matrix products, absorb(): jnp.einsum('rkgd,tkd->rkgt', query_wide.astype(jnp.bfloat16), key_rows, p...  98.1 us
    dot_general x64, matrix products, absorb(): jnp.einsum('rkgt,tkd->rkgd', weights.astype(jnp.bfloat16), value_rows, pr...  90.2 us
    reduce_scatter x1, waiting for transfers between devices, shards(): lax.psum_scatter(jnp.dot(activated[row_order], down_weight, preferred_ele...  86.8 us
  transfers between devices with their start and end apart: 259, of which 127 were waited for; matrix products, arithmetic and copies ran while one was open for 11% of the time, Pallas kernels for 0%

commit v1 on v0

v1 whole, which is shorter than its diff:
```python
import jax
import jax.numpy as jnp
from jax import lax
from jax.experimental import pallas as pl
from jax.experimental.pallas import tpu as pltpu
from jax.sharding import Mesh
from jax.sharding import PartitionSpec as P

HD = 128
GROUP = 8
LANES = 128
EPS = 1e-05
NEG = -1e30
CTX = ("y", "zl", "core")
RING = ("y", "zl")
GRP = ("zh", "x")
F32 = jnp.float32
BF16 = jnp.bfloat16
VMEM = pl.BlockSpec(memory_space=pltpu.VMEM)
SMEM = pl.BlockSpec(memory_space=pltpu.SMEM)


def exchange(x, axes):
    return lax.all_to_all(x, axes, 0, 0, tiled=True)


def lane_ids(shape):
    return lax.broadcasted_iota(jnp.int32, shape, len(shape) - 1)


def call(body, out_shape, in_specs, scratch=()):
    return pl.pallas_call(
        body,
        out_shape=out_shape,
        in_specs=in_specs,
        out_specs=jax.tree.map(lambda _: VMEM, out_shape),
        scratch_shapes=list(scratch),
    )


def attend_body(len_ref, table_ref, q_ref, k_ref, v_ref, out_ref, top_ref, sum_ref, acc_ref):
    slots, page = k_ref.shape[0], k_ref.shape[1]
    first = lax.axis_index(CTX) * slots
    table = table_ref[...] - first
    rows, cols = table.shape
    code = lax.broadcasted_iota(jnp.int32, (rows, cols), 0) * cols + lane_ids((rows, cols))
    top_ref[...] = jnp.full(top_ref.shape, NEG, F32)
    sum_ref[...] = jnp.zeros(sum_ref.shape, F32)
    acc_ref[...] = jnp.zeros(acc_ref.shape, F32)
    lane = lane_ids((GROUP, page))
    owners, scores = [], []
    for s in range(slots):
        found = jnp.min(jnp.where(table == s, code, rows * cols - 1))
        owner, page_no = found // cols, found % cols
        live = len_ref[owner] - page_no * page
        pair = q_ref[owner // 2].astype(F32)
        q = jnp.where(owner % 2 == 1, pair[GROUP:], pair[:GROUP]).astype(BF16)
        score = lax.dot_general(q, k_ref[s], (((1,), (1,)), ((), ())), preferred_element_type=F32)
        score = jnp.where(lane < live, score * HD ** (-0.5), NEG)
        best = jnp.max(score, axis=1, keepdims=True)
        top_ref[owner] = jnp.maximum(top_ref[owner], jnp.broadcast_to(best, (GROUP, LANES)))
        owners.append(owner)
        scores.append(score)
    for s in range(slots):
        owner = owners[s]
        shift = top_ref[owner].astype(BF16).astype(F32)
        weight = jnp.exp(scores[s] - shift)
        total = jnp.sum(weight, axis=1, keepdims=True)
        sum_ref[owner] = sum_ref[owner] + jnp.broadcast_to(total, (GROUP, LANES))
        acc_ref[owner] = acc_ref[owner] + jnp.dot(
            weight.astype(BF16), v_ref[s], preferred_element_type=F32
        )
    lane = lane_ids((GROUP, LANES))
    for d in range(out_ref.shape[0]):
        stats = jnp.zeros((GROUP, LANES), F32)
        for par in range(2):
            total = sum_ref[2 * d + par]
            high = total.astype(BF16).astype(F32)
            base = par * 64
            stats = jnp.where(lane == base, top_ref[2 * d + par], stats)
            stats = jnp.where(lane == base + 1, high, stats)
            stats = jnp.where(lane == base + 2, total - high, stats)
        block = jnp.concatenate([acc_ref[2 * d], acc_ref[2 * d + 1], stats], axis=0)
        out_ref[d] = block.astype(BF16)


def combine_body(part_ref, q_ref, fk_ref, fv_ref, out_ref):
    count = part_ref.shape[0]
    fk, fv = fk_ref[...].astype(F32), fv_ref[...].astype(F32)
    q = q_ref[...].astype(F32)
    done = []
    for par in range(2):
        base = par * 64
        mine = slice(par * GROUP, (par + 1) * GROUP)
        own = jnp.sum(q[mine] * fk[par : par + 1], axis=1, keepdims=True) * HD ** (-0.5)
        best = own
        for d in range(count):
            stats = part_ref[d].astype(F32)[2 * GROUP :]
            best = jnp.maximum(best, stats[:, base : base + 1])
        own_weight = jnp.exp(own - best)
        total = own_weight
        acc = own_weight.astype(BF16).astype(F32) * fv[par : par + 1]
        for d in range(count):
            block = part_ref[d].astype(F32)
            stats = block[2 * GROUP :]
            factor = jnp.exp(stats[:, base : base + 1] - best)
            total = total + factor * (stats[:, base + 1 : base + 2] + stats[:, base + 2 : base + 3])
            acc = acc + factor * block[mine]
        done.append(acc / total)
    rows = jnp.concatenate(done, axis=0).astype(BF16)
    for d in range(count):
        out_ref[d] = rows


def project_body(att_ref, w_ref, out_ref, rows_ref):
    count, per, _ = att_ref.shape
    rows_ref[...] = att_ref[...].astype(F32).reshape(count * per, HD)
    reqs = count * per // GROUP
    total = jnp.zeros((reqs, w_ref.shape[1]), F32)
    for h in range(GROUP):
        head = rows_ref[pl.ds(h, reqs, stride=GROUP), :].astype(BF16)
        total = total + jnp.dot(head, w_ref[h * HD : (h + 1) * HD, :], preferred_element_type=F32)
    total = total.astype(BF16)
    for g in range(out_ref.shape[0]):
        out_ref[g] = total


def hidden_body(part_ref, resid_ref, gain_ref, hidden_ref, pay_ref):
    total = resid_ref[...].astype(F32)
    projected = part_ref[0].astype(F32)
    for g in range(1, part_ref.shape[0]):
        projected = projected + part_ref[g].astype(F32)
    hidden = (total + projected).astype(BF16)
    hidden_ref[...] = hidden
    wide = hidden.astype(F32)
    pay_ref[0] = (wide * gain_ref[...].astype(F32)).astype(BF16)
    square = jnp.sum(wide * wide, axis=1, keepdims=True)
    high = square.astype(BF16).astype(F32)
    lane = lane_ids(wide.shape)
    pay_ref[1] = jnp.where(lane == 0, high, jnp.where(lane == 1, square - high, 0.0)).astype(BF16)


def low_half(shape):
    return lax.broadcasted_iota(jnp.int32, shape, 0) % 8 < 4


def split_fours(first, second, low):
    rows = first.shape[0]
    even = jnp.where(low, first, pltpu.roll(second, 4, 0))
    odd = jnp.where(low, pltpu.roll(first, rows - 4, 0), second)
    return even.reshape(rows // 8, 8, LANES), odd.reshape(rows // 8, 8, LANES)


def join_fours(even, odd, low):
    rows = even.shape[0] * 8
    even, odd = even.reshape(rows, LANES), odd.reshape(rows, LANES)
    first = jnp.where(low, even, pltpu.roll(odd, 4, 0))
    second = jnp.where(low, pltpu.roll(even, rows - 4, 0), odd)
    return first, second


def widen_body(pay_ref, gate_ref, up_ref, met_ref, out_ref):
    core = lax.axis_index("core")
    mine, other = pay_ref[core, 0], pay_ref[1 - core, 0]
    square = pay_ref[0, 1].astype(F32) + pay_ref[1, 1].astype(F32)
    high = square.astype(BF16).astype(F32)
    rows = mine.shape[0]
    low = low_half((rows, LANES))
    half = met_ref.shape[2]
    pairs = half // (2 * LANES)

    def pair_tiles(p):
        ref, which, at = (gate_ref, 0, p) if p < pairs else (up_ref, 1, p - pairs)
        start = pl.multiple_of(core * half + at * 2 * LANES, LANES)
        x = jnp.dot(mine, ref[:, pl.ds(start, 2 * LANES)], preferred_element_type=F32)
        x = x + jnp.dot(
            other, met_ref[which, :, at * 2 * LANES : (at + 1) * 2 * LANES], preferred_element_type=F32
        )
        return split_fours(x[:, :LANES], x[:, LANES:], low)

    for g in range(pairs):
        even0, odd0 = pair_tiles(2 * g)
        even1, odd1 = pair_tiles(2 * g + 1)
        out_ref[:, 0, g * 16 : (g + 1) * 16, :] = jnp.concatenate([even0, even1], axis=1).astype(BF16)
        out_ref[:, 1, g * 16 : (g + 1) * 16, :] = jnp.concatenate([odd0, odd1], axis=1).astype(BF16)
    lane = lane_ids((rows, LANES))
    total = square + pltpu.roll(square, LANES - 1, 1)
    high = total.astype(BF16).astype(F32)
    rest = pltpu.roll(total - high, 1, 1)
    square = jnp.where(lane == 0, high, jnp.where(lane == 1, rest, 0.0))
    zero = jnp.zeros((rows, LANES), F32)
    even, odd = split_fours(square, zero, low)
    blank = zero.reshape(rows // 8, 8, LANES)
    g = pairs
    out_ref[:, 0, g * 16 : (g + 1) * 16, :] = jnp.concatenate([even, blank], axis=1).astype(BF16)
    out_ref[:, 1, g * 16 : (g + 1) * 16, :] = jnp.concatenate([odd, blank], axis=1).astype(BF16)


def activate_body(width, part_ref, out_ref):
    total = part_ref[0].astype(F32)
    for d in range(1, part_ref.shape[0]):
        total = total + part_ref[d].astype(F32)
    units = (total.shape[0] - 16) // 2
    square = total[2 * units : 2 * units + 8]
    square = square[:, 0:1] + square[:, 1:2]
    square = jnp.broadcast_to(square, (8, LANES))
    square = square + pltpu.roll(square, 4, 0)
    inv_rms = lax.rsqrt(square / width + EPS)[None]
    gate = total[:units].reshape(units // 8, 8, LANES) * inv_rms
    up = total[units : 2 * units].reshape(units // 8, 8, LANES) * inv_rms
    active = (gate / (1.0 + jnp.exp(-gate)) * up).reshape(units, LANES)
    pad = jnp.zeros((out_ref.shape[1] - units, LANES), F32)
    active = jnp.concatenate([active, pad], axis=0).astype(BF16)
    for d in range(out_ref.shape[0]):
        out_ref[d] = active


def down_body(act_ref, w_ref, order_ref, hidden_ref, out_ref, kept_ref):
    halves, dests = act_ref.shape[0], act_ref.shape[1]
    rows = dests * 8
    low = low_half((rows, LANES))
    half = w_ref.shape[0] // halves
    pairs = half // (2 * LANES)
    total = jnp.zeros((rows, LANES), F32)
    for c in range(halves):
        for g in range((pairs + 1) // 2):
            even = act_ref[c, :, 0, g * 16 : (g + 1) * 16, :].astype(F32)
            odd = act_ref[c, :, 1, g * 16 : (g + 1) * 16, :].astype(F32)
            for k in range(2):
                p = 2 * g + k
                if p >= pairs:
                    continue
                first, second = join_fours(even[:, k * 8 : k * 8 + 8], odd[:, k * 8 : k * 8 + 8], low)
                block = jnp.concatenate([first, second], axis=1).astype(BF16)
                start = c * half + p * 2 * LANES
                total = total + jnp.dot(
                    block, w_ref[start : start + 2 * LANES, :], preferred_element_type=F32
                )
    reqs = order_ref.shape[1]
    pick = lax.broadcasted_iota(jnp.int32, (reqs, reqs), 0) == order_ref[...]
    pick = pick.astype(F32).astype(BF16)
    first_dim = (((0,), (0,)), ((), ()))
    out = lax.dot_general(pick, total.astype(BF16), first_dim, preferred_element_type=F32)
    out_ref[...] = out.astype(BF16)
    kept = lax.dot_general(pick, hidden_ref[...], first_dim, preferred_element_type=F32)
    kept_ref[...] = kept.astype(BF16)


def shards(
    queries,
    fresh_keys,
    fresh_values,
    key_cache,
    value_cache,
    lengths,
    block_table,
    resid,
    out_weight,
    norm_gain,
    gate_weight,
    up_weight,
    down_weight,
    row_order,
):
    ctx, ring, grp = lax.axis_size(CTX), lax.axis_size(RING), lax.axis_size(GRP)
    core = lax.axis_index("core")
    reqs, width = resid.shape
    shape = jax.ShapeDtypeStruct

    half = gate_weight.shape[1] // 2
    given = jnp.stack(
        [lax.dynamic_slice_in_dim(w, (1 - core) * half, half, 1) for w in (gate_weight, up_weight)]
    )
    met = lax.ppermute(given, "core", [(0, 1), (1, 0)])

    my_queries = queries.reshape(2 * GROUP, HD)
    all_queries = exchange(jnp.broadcast_to(my_queries[None], (ctx, 2 * GROUP, HD)), CTX)
    scratch = [pltpu.VMEM((reqs, GROUP, LANES), F32)] * 3
    parts = call(attend_body, shape((ctx, 3 * GROUP, HD), BF16), [SMEM] + [VMEM] * 4, scratch)(
        lengths, block_table, all_queries, key_cache, value_cache
    )
    parts = exchange(parts, CTX)
    local = call(combine_body, shape((ctx, 2 * GROUP, HD), BF16), [VMEM] * 4)(
        parts, my_queries, fresh_keys, fresh_values
    )
    attended = exchange(local, CTX)
    projected = call(
        project_body,
        shape((grp, reqs, width), BF16),
        [VMEM] * 2,
        [pltpu.VMEM((reqs * GROUP, HD), F32)],
    )(attended, out_weight)
    projected = exchange(projected, GRP)
    hidden, pay = call(
        hidden_body,
        (shape((reqs, width), BF16), shape((2, reqs, width), BF16)),
        [VMEM] * 3,
    )(projected, resid, norm_gain.reshape(1, width))
    pay = lax.all_gather(pay, "core", axis=0, tiled=False)
    blocks = 2 * half // LANES
    wide = call(widen_body, shape((ring // 2, 2, blocks * 4 + 16, LANES), BF16), [VMEM] * 4)(
        pay, gate_weight, up_weight, met
    )
    wide = exchange(wide.reshape(ring, blocks * 4 + 16, LANES), RING)
    units = blocks * 2
    padded = -(-units // 16) * 16
    model_width = width * ctx

    def activate(part_ref, out_ref):
        activate_body(model_width, part_ref, out_ref)

    active = call(activate, shape((ring, padded, LANES), BF16), [VMEM])(wide)
    active = exchange(active, RING)
    active = lax.all_gather(active, "core", axis=0, tiled=False)
    rows, kept = call(
        down_body,
        (shape((reqs, width), BF16), shape((reqs, width), BF16)),
        [VMEM] * 4,
    )(
        active.reshape(2, ring // 2, 2, padded, LANES),
        down_weight,
        row_order.reshape(1, reqs),
        hidden,
    )
    share = reqs // grp
    rows = exchange(rows.reshape(grp, share, width), GRP)
    kept = lax.dynamic_index_in_dim(kept.reshape(grp, share, width), lax.axis_index(GRP), 0, False)
    return (kept.astype(F32) + jnp.sum(rows.astype(F32), axis=0)).astype(BF16)


def solution(mesh, sizes=(8, 4, 2, 2, 4)):
    inner = Mesh(mesh.devices.reshape(sizes), ("y", "zl", "core", "zh", "x"))
    in_specs = (
        P(CTX, GRP),
        P(CTX, GRP),
        P(CTX, GRP),
        P(CTX, None, GRP),
        P(CTX, None, GRP),
        P(),
        P(),
        P(None, CTX),
        P(GRP, CTX),
        P(CTX),
        P(CTX, GRP),
        P(CTX, GRP),
        P(GRP, CTX),
        P(),
    )
    out_specs = P(GRP, CTX)
    return jax.shard_map(shards, mesh=inner, in_specs=in_specs, out_specs=out_specs, check_vma=False)
```

time: 2030 us -> 214 us (0.11)
  waiting for transfers between devices: 1030 us -> 44.9 us
  starting transfers between devices: 505 us -> 21.4 us
  matrix products: 195 us -> 0 us
  blocking collectives: 222 us -> 110 us
  other arithmetic: 33.9 us -> 1.38 us
    psum x2 -> x0, waiting for transfers between devices: 519 us -> none  [the longest x1 413 us: shards(): lax.psum((gate_part, up_part, squares), 'ctx')]
    ppermute x256 -> x1, starting transfers between devices: 505 us -> 2.36 us  [shards(): met = lax.ppermute(given, 'core', [(0, 1), (1, 0)])]
    ppermute x256 -> x1, waiting for transfers between devices: 427 us -> 0.01 us  [shards(): met = lax.ppermute(given, 'core', [(0, 1), (1, 0)])]
    dot_general x133 -> x0, matrix products: 195 us -> none  [the longest x64 98.1 us: absorb(): jnp.einsum('rkgd,tkd->rkgt', query_wide.astype(jnp.bfloat16), key_rows, p...]
    psum x1 -> x0, blocking collectives: 139 us -> none  [shards(): lax.psum((gate_part, up_part, squares), 'ctx')]
    all_to_all x0 -> x4, blocking collectives: none -> 104 us  [exchange(): return lax.all_to_all(x, axes, 0, 0, tiled=True)]
    reduce_scatter x1 -> x0, waiting for transfers between devices: 86.8 us -> none  [shards(): lax.psum_scatter(jnp.dot(activated[row_order], down_weight, preferred_ele...]
    all_gather x1, blocking collectives: 82.5 us -> 5.56 us  [shards(): pay = lax.all_gather(pay, 'core', axis=0, tiled=False)]
  transfers between devices with their start and end apart: 259 -> 5, of which waited for: 127 -> 4; matrix products, arithmetic and copies ran while one was open for 11% -> 0% of each run, Pallas kernels for 0% -> 2%
where the time goes in v1:
time: 214 us; the launch traced here: 213 us
  blocking collectives  110 us (51%)
  waiting for transfers between devices  44.9 us (21%)
  starting transfers between devices  21.4 us (10%)
  Pallas kernels  18.5 us (9%)
  between operations  13.5 us (6%)
  local copies, waits for them, and re-layouts  3.78 us (2%)
    all_to_all x4, blocking collectives, exchange(): return lax.all_to_all(x, axes, 0, 0, tiled=True)  104 us
    all_to_all x3, waiting for transfers between devices, exchange(): return lax.all_to_all(x, axes, 0, 0, tiled=True)  34 us
    all_to_all x3, starting transfers between devices, exchange(): return lax.all_to_all(x, axes, 0, 0, tiled=True)  19 us
    all_gather x1, waiting for transfers between devices, shards(): active = lax.all_gather(active, 'core', axis=0, tiled=False)  10.8 us
    all_gather x1, blocking collectives, shards(): pay = lax.all_gather(pay, 'core', axis=0, tiled=False)  5.56 us
  transfers between devices with their start and end apart: 5, of which 4 were waited for; matrix products, arithmetic and copies ran while one was open for 0% of the time, Pallas kernels for 2%

profile of v1, /device:TPU:1, one launch (start us, length us, event | category | flops | bytes accessed | tf_op | source)
XLA Modules:
  0.0 213.1 jit_solution(6896587836087346231)
XLA Ops:
  6.5 0.7 broadcast_in_dim.7.q_ref
  7.3 0.6 copy-done.5
  7.8 27.1 %all_to_all.35.q_ref = bf16[64,16,128]{2,1,0:T(8,128)(2,1)} all-to-all(bf16[64,16,128]{2,1,0:T(8,128)(2,1)S(1)} %broadcast_in_dim.8), channel_id=1, replica_groups=mesh['y'=8,'zl'=4,'core'=2,'zh'=2,'x'=4] {'y','zl','core'}, dimensions={0} | all-to-all | bytes 524288 | tf_op jit(solution)/shard_map/all_to_all | solution.py:24
  34.9 3.7 %shard_map.136 = bf16[64,24,128]{2,1,0:T(8,128)(2,1)} custom-call(s32[128]{0:T(128)} %len_ref.1, s32[128,128]{1,0:T(8,128)} %table_ref.1, bf16[64,16,128]{2,1,0:T(8,128)(2,1)} %all_to_all.35.q_ref, bf16[24,128,128]{2,1,0:T(8,128)(2,1)} %k_ref.1, bf16[24,128,128]{2,1,0:T(8,128)(2,1)} %v_ref.1), custom_call_target="tpu_custom_call" | custom-call | tf_op jit(solution)/shard_map/pallas_call | solution.py:279
  38.6 5.1 %all-to-all-start.1 = ((bf16[64,24,128]{2,1,0:T(8,128)(2,1)}), bf16[64,24,128]{2,1,0:T(8,128)(2,1)S(1)}, u32[]{:S(2)}, u32[]{:S(2)}) async-start(bf16[64,24,128]{2,1,0:T(8,128)(2,1)} %shard_map.136), calls=%async_computation.1 | async-start | bytes 786432 | tf_op jit(solution)/shard_map/all_to_all | solution.py:24
  43.7 0.0 copy-done
  43.7 0.1 dynamic-slice_bitcast_fusion
  43.8 15.0 %all-to-all-done.1.part_ref = bf16[64,24,128]{2,1,0:T(8,128)(2,1)S(1)} async-done(((bf16[64,24,128]{2,1,0:T(8,128)(2,1)}), bf16[64,24,128]{2,1,0:T(8,128)(2,1)S(1)}, u32[]{:S(2)}, u32[]{:S(2)}) %all-to-all-start.1) | async-done | bytes 393248 | tf_op jit(solution)/shard_map/all_to_all | solution.py:24
  58.7 0.8 copy-done.2
  59.5 2.7 %shard_map.137 = bf16[64,16,128]{2,1,0:T(8,128)(2,1)} custom-call(bf16[64,24,128]{2,1,0:T(8,128)(2,1)} %copy-done.2, bf16[16,128]{1,0:T(8,128)(2,1)} %copy-done.5, bf16[2,128]{1,0:T(2,128)(2,1)} %fk_ref.1, bf16[2,128]{1,0:T(2,128)(2,1)} %fv_ref.1), custom_call_target="tpu_custom_call" | custom-call | tf_op jit(solution)/shard_map/pallas_call | solution.py:283
  62.2 5.4 %all-to-all-start.2 = ((bf16[64,16,128]{2,1,0:T(8,128)(2,1)}), bf16[64,16,128]{2,1,0:T(8,128)(2,1)S(1)}, u32[]{:S(2)}, u32[]{:S(2)}) async-start(bf16[64,16,128]{2,1,0:T(8,128)(2,1)} %shard_map.137), calls=%async_computation.2 | async-start | bytes 524288 | tf_op jit(solution)/shard_map/all_to_all | solution.py:24
  67.6 0.0 all-gather.4.cloned.1.call-start
  67.7 0.1 pad_maximum_fusion
  67.8 2.4 %collective-permute-start = (bf16[2,128,1792]{2,1,0:T(8,128)(2,1)S(1)}, bf16[2,128,1792]{2,1,0:T(8,128)(2,1)S(1)}, u32[]{:S(2)}, u32[]{:S(2)}) collective-permute-start(bf16[2,128,1792]{2,1,0:T(8,128)(2,1)S(1)} %pad_maximum_fusion), channel_id=1, source_target_pairs={{0,8},{8,0},{1,9},{9,1},{2,10},{10,2},{3,11},{11,3},{4,12},{12,4},... | collective-permute-start | bytes 2752520 | tf_op jit(solution)/shard_map/ppermute | solution.py:274
  70.1 10.1 %all-to-all-done.2.att_ref = bf16[64,16,128]{2,1,0:T(8,128)(2,1)S(1)} async-done(((bf16[64,16,128]{2,1,0:T(8,128)(2,1)}), bf16[64,16,128]{2,1,0:T(8,128)(2,1)S(1)}, u32[]{:S(2)}, u32[]{:S(2)}) %all-to-all-start.2) | async-done | bytes 262176 | tf_op jit(solution)/shard_map/all_to_all | solution.py:24
  80.2 0.7 copy-done.3
  80.9 2.0 shard_map.138
  82.9 20.0 %all_to_all.36.part_ref = bf16[8,128,128]{2,1,0:T(8,128)(2,1)} all-to-all(bf16[8,128,128]{2,1,0:T(8,128)(2,1)} %shard_map.138), channel_id=1, replica_groups=mesh['y'=8,'zl'=4,'core'=2,'zh'=2,'x'=4] {'zh','x'}, dimensions={0} | all-to-all | bytes 524288 | tf_op jit(solution)/shard_map/all_to_all | solution.py:24
  102.8 1.7 shard_map.139
  104.6 5.6 %all-gather = bf16[4,128,128]{2,1,0:T(8,128)(2,1)} all-gather(bf16[2,128,128]{2,1,0:T(8,128)(2,1)} %get-tuple-element.9), channel_id=2, replica_groups=mesh['y'=8,'zl'=4,'core'=2,'zh'=2,'x'=4] {'core'}, dimensions={0}, use_global_device_ids=true | all-gather | bytes 196608 | tf_op jit(solution)/shard_map/all_gather | solution.py:299
  110.1 0.0 collective-permute-done.met_ref
  110.1 1.0 copy-done.4
  111.1 3.4 %shard_map.140 = bf16[16,2,128,128]{3,2,1,0:T(8,128)(2,1)} custom-call(bf16[2,2,128,128]{3,2,1,0:T(8,128)(2,1)} %bitcast.16, bf16[128,3584]{1,0:T(8,128)(2,1)} %gate_ref.1, bf16[128,3584]{1,0:T(8,128)(2,1)} %up_ref.1, bf16[2,128,1792]{2,1,0:T(8,128)(2,1)} %copy-done.4), custom_call_target="tpu_custom_call" | custom-call | tf_op jit(solution)/shard_map/pallas_call | solution.py:301
  114.5 33.9 %all_to_all.37.part_ref = bf16[32,128,128]{2,1,0:T(8,128)(2,1)} all-to-all(bf16[32,128,128]{2,1,0:T(8,128)(2,1)} %bitcast.14), channel_id=1, replica_groups=mesh['y'=8,'zl'=4,'core'=2,'zh'=2,'x'=4] {'y','zl'}, dimensions={0} | all-to-all | bytes 2097152 | tf_op jit(solution)/shard_map/all_to_all | solution.py:24
  148.4 2.3 %shard_map.141 = bf16[32,64,128]{2,1,0:T(8,128)(2,1)} custom-call(bf16[32,128,128]{2,1,0:T(8,128)(2,1)} %all_to_all.37.part_ref), custom_call_target="tpu_custom_call" | custom-call | tf_op jit(solution)/shard_map/pallas_call | solution.py:312
  150.7 23.1 %all_to_all.38 = bf16[32,64,128]{2,1,0:T(8,128)(2,1)} all-to-all(bf16[32,64,128]{2,1,0:T(8,128)(2,1)} %shard_map.141), channel_id=1, replica_groups=mesh['y'=8,'zl'=4,'core'=2,'zh'=2,'x'=4] {'y','zl'}, dimensions={0} | all-to-all | bytes 1048576 | tf_op jit(solution)/shard_map/all_to_all | solution.py:24
  173.8 0.0 all-gather.4.cloned.1.call-update
  173.8 10.8 %all-gather.4.cloned.1.call-done = bf16[64,64,128]{2,1,0:T(8,128)(2,1)} async-done(((bf16[32,64,128]{2,1,0:T(8,128)(2,1)}), bf16[64,64,128]{2,1,0:T(8,128)(2,1)}) %all-gather.4.cloned.1.call-update) | async-done | bytes 1048592 | tf_op jit(solution)/shard_map/all_gather | solution.py:314
  184.7 2.7 %shard_map.142 = (bf16[128,128]{1,0:T(8,128)(2,1)}, bf16[128,128]{1,0:T(8,128)(2,1)}) custom-call(bf16[2,16,2,64,128]{4,3,2,1,0:T(8,128)(2,1)} %bitcast.15, bf16[3584,128]{1,0:T(8,128)(2,1)} %w_ref.3, s32[1,128]{1,0:T(1,128)} %bitcast.19, bf16[128,128]{1,0:T(8,128)(2,1)} %get-tuple-element.10.hidden_ref), custom_call_target="tpu_custom_call" | custom-call | tf_op jit(solution)/shard_map/pallas_call | solution.py:315
  187.4 8.5 %all-to-all-start.6 = ((bf16[8,16,128]{2,1,0:T(8,128)(2,1)}), bf16[8,16,128]{2,1,0:T(8,128)(2,1)S(1)}, u32[]{:S(2)}, u32[]{:S(2)}) async-start(bf16[8,16,128]{2,1,0:T(8,128)(2,1)} %bitcast.17), calls=%async_computation.6 | async-start | bytes 65536 | tf_op jit(solution)/shard_map/all_to_all | solution.py:24
  195.9 9.0 %all-to-all-done.6 = bf16[8,16,128]{2,1,0:T(8,128)(2,1)S(1)} async-done(((bf16[8,16,128]{2,1,0:T(8,128)(2,1)}), bf16[8,16,128]{2,1,0:T(8,128)(2,1)S(1)}, u32[]{:S(2)}, u32[]{:S(2)}) %all-to-all-start.6) | async-done | bytes 32800 | tf_op jit(solution)/shard_map/all_to_all | solution.py:24
  204.9 1.3 fusion
  (9 shorter events, 0.1 us)
Async XLA Ops:
  7.2 0.6 copy-start.5
  34.9 8.8 %copy-start = (bf16[128,3584]{1,0:T(8,128)(2,1)S(1)}, bf16[128,3584]{1,0:T(8,128)(2,1)}, u32[]{:S(2)}) copy-start(bf16[128,3584]{1,0:T(8,128)(2,1)} %gate_ref.1) | copy-start | bytes 2752516
  34.9 8.8 %copy-start.1 = (bf16[128,3584]{1,0:T(8,128)(2,1)S(1)}, bf16[128,3584]{1,0:T(8,128)(2,1)}, u32[]{:S(2)}) copy-start(bf16[128,3584]{1,0:T(8,128)(2,1)} %up_ref.1) | copy-start | bytes 2752516
  38.6 20.2 %all-to-all-start.1 = ((bf16[64,24,128]{2,1,0:T(8,128)(2,1)}), bf16[64,24,128]{2,1,0:T(8,128)(2,1)S(1)}, u32[]{:S(2)}, u32[]{:S(2)}) async-start(bf16[64,24,128]{2,1,0:T(8,128)(2,1)} %shard_map.136), calls=%async_computation.1 | async-start | bytes 786432 | tf_op jit(solution)/shard_map/all_to_all | solution.py:24
  58.7 0.8 copy-start.2
  62.2 18.0 %all-to-all-start.2 = ((bf16[64,16,128]{2,1,0:T(8,128)(2,1)}), bf16[64,16,128]{2,1,0:T(8,128)(2,1)S(1)}, u32[]{:S(2)}, u32[]{:S(2)}) async-start(bf16[64,16,128]{2,1,0:T(8,128)(2,1)} %shard_map.137), calls=%async_computation.2 | async-start | bytes 524288 | tf_op jit(solution)/shard_map/all_to_all | solution.py:24
  67.6 117.1 %all-gather.4.cloned.1.call-start = ((), (), s32[]{:S(2)}) async-start(), calls=%async_computation.7 | async-start | bytes 1572864 | tf_op jit(solution)/shard_map/all_gather | solution.py:314
  67.8 42.4 %collective-permute-start = (bf16[2,128,1792]{2,1,0:T(8,128)(2,1)S(1)}, bf16[2,128,1792]{2,1,0:T(8,128)(2,1)S(1)}, u32[]{:S(2)}, u32[]{:S(2)}) collective-permute-start(bf16[2,128,1792]{2,1,0:T(8,128)(2,1)S(1)} %pad_maximum_fusion), channel_id=1, source_target_pairs={{0,8},{8,0},{1,9},{9,1},{2,10},{10,2},{3,11},{11,3},{4,12},{12,4},... | collective-permute-start | bytes 2752520 | tf_op jit(solution)/shard_map/ppermute | solution.py:274
  80.2 0.7 copy-start.3
  110.1 1.0 copy-start.4
  187.4 17.5 %all-to-all-start.6 = ((bf16[8,16,128]{2,1,0:T(8,128)(2,1)}), bf16[8,16,128]{2,1,0:T(8,128)(2,1)S(1)}, u32[]{:S(2)}, u32[]{:S(2)}) async-start(bf16[8,16,128]{2,1,0:T(8,128)(2,1)} %bitcast.17), calls=%async_computation.6 | async-start | bytes 65536 | tf_op jit(solution)/shard_map/all_to_all | solution.py:24
Sparse Core Ops, SparseCore 0:
  174.0 10.6 all-gather.3

commit v2 on v1

--- a/solution.py
+++ b/solution.py
@@ -190,17 +190,15 @@
     square = jnp.where(lane == 0, high, jnp.where(lane == 1, rest, 0.0))
     zero = jnp.zeros((rows, LANES), F32)
     even, odd = split_fours(square, zero, low)
-    blank = zero.reshape(rows // 8, 8, LANES)
-    g = pairs
-    out_ref[:, 0, g * 16 : (g + 1) * 16, :] = jnp.concatenate([even, blank], axis=1).astype(BF16)
-    out_ref[:, 1, g * 16 : (g + 1) * 16, :] = jnp.concatenate([odd, blank], axis=1).astype(BF16)
+    out_ref[:, 0, pairs * 16 :, :] = even.astype(BF16)
+    out_ref[:, 1, pairs * 16 :, :] = odd.astype(BF16)
 
 
 def activate_body(width, part_ref, out_ref):
     total = part_ref[0].astype(F32)
     for d in range(1, part_ref.shape[0]):
         total = total + part_ref[d].astype(F32)
-    units = (total.shape[0] - 16) // 2
+    units = (total.shape[0] - 8) // 2
     square = total[2 * units : 2 * units + 8]
     square = square[:, 0:1] + square[:, 1:2]
     square = jnp.broadcast_to(square, (8, LANES))
@@ -215,26 +213,26 @@
         out_ref[d] = active
 
 
-def down_body(act_ref, w_ref, order_ref, hidden_ref, out_ref, kept_ref):
-    halves, dests = act_ref.shape[0], act_ref.shape[1]
-    rows = dests * 8
+def down_body(mine_ref, met_ref, w_ref, order_ref, hidden_ref, out_ref, kept_ref):
+    core = lax.axis_index("core")
+    rows = mine_ref.shape[0] * 8
     low = low_half((rows, LANES))
-    half = w_ref.shape[0] // halves
+    half = w_ref.shape[0] // 2
     pairs = half // (2 * LANES)
     total = jnp.zeros((rows, LANES), F32)
-    for c in range(halves):
+    for act_ref, c in ((mine_ref, core), (met_ref, 1 - core)):
         for g in range((pairs + 1) // 2):
-            even = act_ref[c, :, 0, g * 16 : (g + 1) * 16, :].astype(F32)
-            odd = act_ref[c, :, 1, g * 16 : (g + 1) * 16, :].astype(F32)
+            even = act_ref[:, 0, g * 16 : (g + 1) * 16, :].astype(F32)
+            odd = act_ref[:, 1, g * 16 : (g + 1) * 16, :].astype(F32)
             for k in range(2):
                 p = 2 * g + k
                 if p >= pairs:
                     continue
                 first, second = join_fours(even[:, k * 8 : k * 8 + 8], odd[:, k * 8 : k * 8 + 8], low)
                 block = jnp.concatenate([first, second], axis=1).astype(BF16)
-                start = c * half + p * 2 * LANES
+                start = pl.multiple_of(c * half + p * 2 * LANES, LANES)
                 total = total + jnp.dot(
-                    block, w_ref[start : start + 2 * LANES, :], preferred_element_type=F32
+                    block, w_ref[pl.ds(start, 2 * LANES), :], preferred_element_type=F32
                 )
     reqs = order_ref.shape[1]
     pick = lax.broadcasted_iota(jnp.int32, (reqs, reqs), 0) == order_ref[...]
@@ -298,10 +296,10 @@
     )(projected, resid, norm_gain.reshape(1, width))
     pay = lax.all_gather(pay, "core", axis=0, tiled=False)
     blocks = 2 * half // LANES
-    wide = call(widen_body, shape((ring // 2, 2, blocks * 4 + 16, LANES), BF16), [VMEM] * 4)(
+    wide = call(widen_body, shape((ring // 2, 2, blocks * 4 + 8, LANES), BF16), [VMEM] * 4)(
         pay, gate_weight, up_weight, met
     )
-    wide = exchange(wide.reshape(ring, blocks * 4 + 16, LANES), RING)
+    wide = exchange(wide.reshape(ring, blocks * 4 + 8, LANES), RING)
     units = blocks * 2
     padded = -(-units // 16) * 16
     model_width = width * ctx
@@ -311,13 +309,14 @@
 
     active = call(activate, shape((ring, padded, LANES), BF16), [VMEM])(wide)
     active = exchange(active, RING)
-    active = lax.all_gather(active, "core", axis=0, tiled=False)
+    met_active = lax.ppermute(active, "core", [(0, 1), (1, 0)])
     rows, kept = call(
         down_body,
         (shape((reqs, width), BF16), shape((reqs, width), BF16)),
-        [VMEM] * 4,
+        [VMEM] * 5,
     )(
-        active.reshape(2, ring // 2, 2, padded, LANES),
+        active.reshape(ring // 2, 2, padded, LANES),
+        met_active.reshape(ring // 2, 2, padded, LANES),
         down_weight,
         row_order.reshape(1, reqs),
         hidden,

time: 214 us -> 190 us (0.89)
  between operations: 13.5 us -> 0.11 us
  waiting for transfers between devices: 44.9 us -> 35.5 us
    all_gather x1 -> x0, waiting for transfers between devices: 10.8 us -> none  [shards(): active = lax.all_gather(active, 'core', axis=0, tiled=False)]
    all_to_all x3, starting transfers between devices: 19 us -> 13.8 us  [exchange(): return lax.all_to_all(x, axes, 0, 0, tiled=True)]
    ppermute x0 -> x1, starting transfers between devices: none -> 4.21 us  [shards(): met_active = lax.ppermute(active, 'core', [(0, 1), (1, 0)])]
where the time goes in v2:
time: 190 us; the launch traced here: 189 us
  blocking collectives  108 us (57%)
  waiting for transfers between devices  35.5 us (19%)
  starting transfers between devices  20.4 us (11%)
  Pallas kernels  18.5 us (10%)
  local copies, waits for them, and re-layouts  4.57 us (2%)
    all_to_all x4, blocking collectives, exchange(): return lax.all_to_all(x, axes, 0, 0, tiled=True)  103 us
    all_to_all x3, waiting for transfers between devices, exchange(): return lax.all_to_all(x, axes, 0, 0, tiled=True)  34 us
    all_to_all x3, starting transfers between devices, exchange(): return lax.all_to_all(x, axes, 0, 0, tiled=True)  13.8 us
    all_gather x1, blocking collectives, shards(): pay = lax.all_gather(pay, 'core', axis=0, tiled=False)  5.56 us
    ppermute x1, starting transfers between devices, shards(): met_active = lax.ppermute(active, 'core', [(0, 1), (1, 0)])  4.21 us
  transfers between devices with their start and end apart: 5, of which 4 were waited for; matrix products, arithmetic and copies ran while one was open for 0% of the time, Pallas kernels for 2%

profile of v2, /device:TPU:1, one launch (start us, length us, event | category | flops | bytes accessed | tf_op | source)
XLA Modules:
  0.0 188.6 jit_solution(5819273059856817036)
XLA Ops:
  0.0 0.7 broadcast_in_dim.7.q_ref
  0.7 0.6 copy-done.7
  1.3 27.1 %all_to_all.35.q_ref = bf16[64,16,128]{2,1,0:T(8,128)(2,1)} all-to-all(bf16[64,16,128]{2,1,0:T(8,128)(2,1)S(1)} %broadcast_in_dim.8), channel_id=1, replica_groups=mesh['y'=8,'zl'=4,'core'=2,'zh'=2,'x'=4] {'y','zl','core'}, dimensions={0} | all-to-all | bytes 524288 | tf_op jit(solution)/shard_map/all_to_all | solution.py:24
  28.4 3.7 %shard_map.136 = bf16[64,24,128]{2,1,0:T(8,128)(2,1)} custom-call(s32[128]{0:T(128)} %len_ref.1, s32[128,128]{1,0:T(8,128)} %table_ref.1, bf16[64,16,128]{2,1,0:T(8,128)(2,1)} %all_to_all.35.q_ref, bf16[24,128,128]{2,1,0:T(8,128)(2,1)} %k_ref.1, bf16[24,128,128]{2,1,0:T(8,128)(2,1)} %v_ref.1), custom_call_target="tpu_custom_call" | custom-call | tf_op jit(solution)/shard_map/pallas_call | solution.py:277
  32.0 5.1 %all-to-all-start.1 = ((bf16[64,24,128]{2,1,0:T(8,128)(2,1)}), bf16[64,24,128]{2,1,0:T(8,128)(2,1)S(1)}, u32[]{:S(2)}, u32[]{:S(2)}) async-start(bf16[64,24,128]{2,1,0:T(8,128)(2,1)} %shard_map.136), calls=%async_computation.1 | async-start | bytes 786432 | tf_op jit(solution)/shard_map/all_to_all | solution.py:24
  37.2 0.1 dynamic-slice_bitcast_fusion
  37.2 15.0 %all-to-all-done.1.part_ref = bf16[64,24,128]{2,1,0:T(8,128)(2,1)S(1)} async-done(((bf16[64,24,128]{2,1,0:T(8,128)(2,1)}), bf16[64,24,128]{2,1,0:T(8,128)(2,1)S(1)}, u32[]{:S(2)}, u32[]{:S(2)}) %all-to-all-start.1) | async-done | bytes 393248 | tf_op jit(solution)/shard_map/all_to_all | solution.py:24
  52.2 0.8 copy-done.3
  53.0 2.7 %shard_map.137 = bf16[64,16,128]{2,1,0:T(8,128)(2,1)} custom-call(bf16[64,24,128]{2,1,0:T(8,128)(2,1)} %copy-done.3, bf16[16,128]{1,0:T(8,128)(2,1)} %copy-done.7, bf16[2,128]{1,0:T(2,128)(2,1)} %fk_ref.1, bf16[2,128]{1,0:T(2,128)(2,1)} %fv_ref.1), custom_call_target="tpu_custom_call" | custom-call | tf_op jit(solution)/shard_map/pallas_call | solution.py:281
  55.6 5.4 %all-to-all-start.2 = ((bf16[64,16,128]{2,1,0:T(8,128)(2,1)}), bf16[64,16,128]{2,1,0:T(8,128)(2,1)S(1)}, u32[]{:S(2)}, u32[]{:S(2)}) async-start(bf16[64,16,128]{2,1,0:T(8,128)(2,1)} %shard_map.137), calls=%async_computation.2 | async-start | bytes 524288 | tf_op jit(solution)/shard_map/all_to_all | solution.py:24
  61.1 0.1 pad_maximum_fusion
  61.2 2.4 %collective-permute-start = (bf16[2,128,1792]{2,1,0:T(8,128)(2,1)S(1)}, bf16[2,128,1792]{2,1,0:T(8,128)(2,1)S(1)}, u32[]{:S(2)}, u32[]{:S(2)}) collective-permute-start(bf16[2,128,1792]{2,1,0:T(8,128)(2,1)S(1)} %pad_maximum_fusion), channel_id=1, source_target_pairs={{0,8},{8,0},{1,9},{9,1},{2,10},{10,2},{3,11},{11,3},{4,12},{12,4},... | collective-permute-start | bytes 2752520 | tf_op jit(solution)/shard_map/ppermute | solution.py:272
  63.5 10.1 %all-to-all-done.2.att_ref = bf16[64,16,128]{2,1,0:T(8,128)(2,1)S(1)} async-done(((bf16[64,16,128]{2,1,0:T(8,128)(2,1)}), bf16[64,16,128]{2,1,0:T(8,128)(2,1)S(1)}, u32[]{:S(2)}, u32[]{:S(2)}) %all-to-all-start.2) | async-done | bytes 262176 | tf_op jit(solution)/shard_map/all_to_all | solution.py:24
  73.7 0.7 copy-done.4
  74.4 2.0 %shard_map.138 = bf16[8,128,128]{2,1,0:T(8,128)(2,1)} custom-call(bf16[64,16,128]{2,1,0:T(8,128)(2,1)} %copy-done.4, bf16[1024,128]{1,0:T(8,128)(2,1)} %w_ref.2), custom_call_target="tpu_custom_call" | custom-call | tf_op jit(solution)/shard_map/pallas_call | solution.py:285
  76.3 20.0 %all_to_all.36.part_ref = bf16[8,128,128]{2,1,0:T(8,128)(2,1)} all-to-all(bf16[8,128,128]{2,1,0:T(8,128)(2,1)} %shard_map.138), channel_id=1, replica_groups=mesh['y'=8,'zl'=4,'core'=2,'zh'=2,'x'=4] {'zh','x'}, dimensions={0} | all-to-all | bytes 524288 | tf_op jit(solution)/shard_map/all_to_all | solution.py:24
  96.3 1.7 shard_map.139
  98.0 5.6 %all-gather = bf16[4,128,128]{2,1,0:T(8,128)(2,1)} all-gather(bf16[2,128,128]{2,1,0:T(8,128)(2,1)} %get-tuple-element.9), channel_id=2, replica_groups=mesh['y'=8,'zl'=4,'core'=2,'zh'=2,'x'=4] {'core'}, dimensions={0}, use_global_device_ids=true | all-gather | bytes 196608 | tf_op jit(solution)/shard_map/all_gather | solution.py:297
  103.6 0.0 collective-permute-done.met_ref
  103.6 1.0 copy-done.5
  104.6 3.4 %shard_map.140 = bf16[16,2,120,128]{3,2,1,0:T(8,128)(2,1)} custom-call(bf16[2,2,128,128]{3,2,1,0:T(8,128)(2,1)} %bitcast.18, bf16[128,3584]{1,0:T(8,128)(2,1)} %gate_ref.1, bf16[128,3584]{1,0:T(8,128)(2,1)} %up_ref.1, bf16[2,128,1792]{2,1,0:T(8,128)(2,1)} %copy-done.5), custom_call_target="tpu_custom_call" | custom-call | tf_op jit(solution)/shard_map/pallas_call | solution.py:299
  107.9 32.7 %all_to_all.37.part_ref = bf16[32,120,128]{2,1,0:T(8,128)(2,1)} all-to-all(bf16[32,120,128]{2,1,0:T(8,128)(2,1)} %bitcast.15), channel_id=1, replica_groups=mesh['y'=8,'zl'=4,'core'=2,'zh'=2,'x'=4] {'y','zl'}, dimensions={0} | all-to-all | bytes 1966080 | tf_op jit(solution)/shard_map/all_to_all | solution.py:24
  140.6 2.3 %shard_map.141 = bf16[32,64,128]{2,1,0:T(8,128)(2,1)} custom-call(bf16[32,120,128]{2,1,0:T(8,128)(2,1)} %all_to_all.37.part_ref), custom_call_target="tpu_custom_call" | custom-call | tf_op jit(solution)/shard_map/pallas_call | solution.py:310
  142.9 22.9 %all_to_all.38 = bf16[32,64,128]{2,1,0:T(8,128)(2,1)S(1)} all-to-all(bf16[32,64,128]{2,1,0:T(8,128)(2,1)} %shard_map.141), channel_id=1, replica_groups=mesh['y'=8,'zl'=4,'core'=2,'zh'=2,'x'=4] {'y','zl'}, dimensions={0} | all-to-all | bytes 1048576 | tf_op jit(solution)/shard_map/all_to_all | solution.py:24
  165.7 4.2 %collective-permute-start.1 = (bf16[32,64,128]{2,1,0:T(8,128)(2,1)S(1)}, bf16[32,64,128]{2,1,0:T(8,128)(2,1)S(1)}, u32[]{:S(2)}, u32[]{:S(2)}) collective-permute-start(bf16[32,64,128]{2,1,0:T(8,128)(2,1)S(1)} %all_to_all.38), channel_id=1, source_target_pairs={{0,8},{8,0},{1,9},{9,1},{2,10},{10,2},{3,11},{11,3},{4,12},{12,4},... | collective-permute-start | bytes 1572872 | tf_op jit(solution)/shard_map/ppermute | solution.py:312
  170.0 1.5 collective-permute-done.1
  171.5 0.0 copy-done
  171.5 0.8 copy-done.6
  172.3 2.7 %shard_map.142 = (bf16[128,128]{1,0:T(8,128)(2,1)}, bf16[128,128]{1,0:T(8,128)(2,1)}) custom-call(bf16[16,2,64,128]{3,2,1,0:T(8,128)(2,1)} %bitcast.16, bf16[16,2,64,128]{3,2,1,0:T(8,128)(2,1)} %bitcast.17, bf16[3584,128]{1,0:T(8,128)(2,1)} %w_ref.3, s32[1,128]{1,0:T(1,128)} %bitcast.21, bf16[128,128]{1,0:T(8,128)(2,1)} %get-tuple-element.10.hidden_ref), custom_call_target="tpu_custom_call" | custom-call | tf_op jit(solution)/shard_map/pallas_call | solution.py:313
  175.0 3.3 %all-to-all-start.6 = ((bf16[8,16,128]{2,1,0:T(8,128)(2,1)}), bf16[8,16,128]{2,1,0:T(8,128)(2,1)S(1)}, u32[]{:S(2)}, u32[]{:S(2)}) async-start(bf16[8,16,128]{2,1,0:T(8,128)(2,1)} %bitcast.19), calls=%async_computation.6 | async-start | bytes 65536 | tf_op jit(solution)/shard_map/all_to_all | solution.py:24
  178.3 8.9 %all-to-all-done.6 = bf16[8,16,128]{2,1,0:T(8,128)(2,1)S(1)} async-done(((bf16[8,16,128]{2,1,0:T(8,128)(2,1)}), bf16[8,16,128]{2,1,0:T(8,128)(2,1)S(1)}, u32[]{:S(2)}, u32[]{:S(2)}) %all-to-all-start.6) | async-done | bytes 32800 | tf_op jit(solution)/shard_map/all_to_all | solution.py:24
  187.3 1.3 fusion
  (12 shorter events, 0.1 us)
Async XLA Ops:
  0.7 0.6 copy-start.7
  28.4 8.8 %copy-start.1 = (bf16[128,3584]{1,0:T(8,128)(2,1)S(1)}, bf16[128,3584]{1,0:T(8,128)(2,1)}, u32[]{:S(2)}) copy-start(bf16[128,3584]{1,0:T(8,128)(2,1)} %gate_ref.1) | copy-start | bytes 2752516
  28.4 8.8 %copy-start.2 = (bf16[128,3584]{1,0:T(8,128)(2,1)S(1)}, bf16[128,3584]{1,0:T(8,128)(2,1)}, u32[]{:S(2)}) copy-start(bf16[128,3584]{1,0:T(8,128)(2,1)} %up_ref.1) | copy-start | bytes 2752516
  32.0 20.2 %all-to-all-start.1 = ((bf16[64,24,128]{2,1,0:T(8,128)(2,1)}), bf16[64,24,128]{2,1,0:T(8,128)(2,1)S(1)}, u32[]{:S(2)}, u32[]{:S(2)}) async-start(bf16[64,24,128]{2,1,0:T(8,128)(2,1)} %shard_map.136), calls=%async_computation.1 | async-start | bytes 786432 | tf_op jit(solution)/shard_map/all_to_all | solution.py:24
  52.2 0.8 copy-start.3
  55.6 18.0 %all-to-all-start.2 = ((bf16[64,16,128]{2,1,0:T(8,128)(2,1)}), bf16[64,16,128]{2,1,0:T(8,128)(2,1)S(1)}, u32[]{:S(2)}, u32[]{:S(2)}) async-start(bf16[64,16,128]{2,1,0:T(8,128)(2,1)} %shard_map.137), calls=%async_computation.2 | async-start | bytes 524288 | tf_op jit(solution)/shard_map/all_to_all | solution.py:24
  61.2 42.4 %collective-permute-start = (bf16[2,128,1792]{2,1,0:T(8,128)(2,1)S(1)}, bf16[2,128,1792]{2,1,0:T(8,128)(2,1)S(1)}, u32[]{:S(2)}, u32[]{:S(2)}) collective-permute-start(bf16[2,128,1792]{2,1,0:T(8,128)(2,1)S(1)} %pad_maximum_fusion), channel_id=1, source_target_pairs={{0,8},{8,0},{1,9},{9,1},{2,10},{10,2},{3,11},{11,3},{4,12},{12,4},... | collective-permute-start | bytes 2752520 | tf_op jit(solution)/shard_map/ppermute | solution.py:272
  73.7 0.7 copy-start.4
  103.6 1.0 copy-start.5
  165.7 5.7 %copy-start = (bf16[32,64,128]{2,1,0:T(8,128)(2,1)}, bf16[32,64,128]{2,1,0:T(8,128)(2,1)S(1)}, u32[]{:S(2)}) copy-start(bf16[32,64,128]{2,1,0:T(8,128)(2,1)S(1)} %all_to_all.38) | copy-start | bytes 1572868
  165.7 5.7 %collective-permute-start.1 = (bf16[32,64,128]{2,1,0:T(8,128)(2,1)S(1)}, bf16[32,64,128]{2,1,0:T(8,128)(2,1)S(1)}, u32[]{:S(2)}, u32[]{:S(2)}) collective-permute-start(bf16[32,64,128]{2,1,0:T(8,128)(2,1)S(1)} %all_to_all.38), channel_id=1, source_target_pairs={{0,8},{8,0},{1,9},{9,1},{2,10},{10,2},{3,11},{11,3},{4,12},{12,4},... | collective-permute-start | bytes 1572872 | tf_op jit(solution)/shard_map/ppermute | solution.py:312
  171.5 0.8 copy-start.6
  175.0 12.3 %all-to-all-start.6 = ((bf16[8,16,128]{2,1,0:T(8,128)(2,1)}), bf16[8,16,128]{2,1,0:T(8,128)(2,1)S(1)}, u32[]{:S(2)}, u32[]{:S(2)}) async-start(bf16[8,16,128]{2,1,0:T(8,128)(2,1)} %bitcast.19), calls=%async_computation.6 | async-start | bytes 65536 | tf_op jit(solution)/shard_map/all_to_all | solution.py:24

commit v3 on v2

--- a/solution.py
+++ b/solution.py
@@ -11,6 +11,7 @@
 LANES = 128
 EPS = 1e-05
 NEG = -1e30
+VMEM_LIMIT = 16 * 2**20
 CTX = ("y", "zl", "core")
 RING = ("y", "zl")
 GRP = ("zh", "x")
@@ -35,6 +36,7 @@
         in_specs=in_specs,
         out_specs=jax.tree.map(lambda _: VMEM, out_shape),
         scratch_shapes=list(scratch),
+        compiler_params=pltpu.CompilerParams(vmem_limit_bytes=VMEM_LIMIT),
     )
 
 

time: 190 us -> 174 us (0.916)
  Pallas kernels: 18.5 us -> 6.75 us
  blocking collectives: 108 us -> 106 us
    pallas_call x1, Pallas kernels: 3.36 us -> 0.63 us  [shards(): call(widen_body, shape((ring // 2, 2, blocks * 4 + 8, LANES), BF16), [VME...]
    pallas_call x1, Pallas kernels: 2.27 us -> 0.27 us  [shards(): active = call(activate, shape((ring, padded, LANES), BF16), [VMEM])(wide)]
  transfers between devices with their start and end apart: 5 -> 5, of which waited for: 4 -> 4; matrix products, arithmetic and copies ran while one was open for 0% -> 1% of each run, Pallas kernels for 2% -> 0%
where the time goes in v3:
time: 174 us; the launch traced here: 173 us
  blocking collectives  106 us (61%)
  waiting for transfers between devices  33.8 us (19%)
  starting transfers between devices  20.5 us (12%)
  Pallas kernels  6.75 us (4%)
  local copies, waits for them, and re-layouts  4.98 us (3%)
    all_to_all x4, blocking collectives, exchange(): return lax.all_to_all(x, axes, 0, 0, tiled=True)  102 us
    all_to_all x3, waiting for transfers between devices, exchange(): return lax.all_to_all(x, axes, 0, 0, tiled=True)  32.3 us
    all_to_all x3, starting transfers between devices, exchange(): return lax.all_to_all(x, axes, 0, 0, tiled=True)  14 us
    ppermute x1, starting transfers between devices, shards(): met_active = lax.ppermute(active, 'core', [(0, 1), (1, 0)])  4.21 us
    all_gather x1, blocking collectives, shards(): pay = lax.all_gather(pay, 'core', axis=0, tiled=False)  3.91 us
  transfers between devices with their start and end apart: 5, of which 4 were waited for; matrix products, arithmetic and copies ran while one was open for 1% of the time, Pallas kernels for 0%

profile of v3, /device:TPU:1, one launch (start us, length us, event | category | flops | bytes accessed | tf_op | source)
XLA Modules:
  0.0 173.5 jit_solution(8281887211492354287)
XLA Ops:
  0.0 0.8 broadcast_in_dim.7.q_ref
  0.8 0.0 copy-start.8
  0.8 27.0 %all_to_all.35.q_ref = bf16[64,16,128]{2,1,0:T(8,128)(2,1)S(1)} all-to-all(bf16[64,16,128]{2,1,0:T(8,128)(2,1)S(1)} %broadcast_in_dim.8), channel_id=1, replica_groups=mesh['y'=8,'zl'=4,'core'=2,'zh'=2,'x'=4] {'y','zl','core'}, dimensions={0} | all-to-all | bytes 524288 | tf_op jit(solution)/shard_map/all_to_all | solution.py:25
  27.8 1.1 copy-done.4
  28.9 0.8 copy-done.6
  29.8 2.6 %shard_map.136 = bf16[64,24,128]{2,1,0:T(8,128)(2,1)} custom-call(s32[128]{0:T(128)S(1)} %copy-done.8, s32[128,128]{1,0:T(8,128)S(1)} %copy-done.6, bf16[64,16,128]{2,1,0:T(8,128)(2,1)S(1)} %all_to_all.35.q_ref, bf16[24,128,128]{2,1,0:T(8,128)(2,1)S(1)} %copy-done.3, bf16[24,128,128]{2,1,0:T(8,128)(2,1)S(1)} %copy-done.4), custom_call_target="tpu_custom_call" | custom-call | tf_op jit(solution)/shard_map/pallas_call | solution.py:279
  32.3 5.1 %all-to-all-start.1 = ((bf16[64,24,128]{2,1,0:T(8,128)(2,1)}), bf16[64,24,128]{2,1,0:T(8,128)(2,1)S(1)}, u32[]{:S(2)}, u32[]{:S(2)}) async-start(bf16[64,24,128]{2,1,0:T(8,128)(2,1)} %shard_map.136), calls=%async_computation.1 | async-start | bytes 786432 | tf_op jit(solution)/shard_map/all_to_all | solution.py:25
  37.5 0.0 copy-start.10
  37.5 0.8 dynamic-slice_bitcast_fusion
  38.3 14.2 %all-to-all-done.1.part_ref = bf16[64,24,128]{2,1,0:T(8,128)(2,1)S(1)} async-done(((bf16[64,24,128]{2,1,0:T(8,128)(2,1)}), bf16[64,24,128]{2,1,0:T(8,128)(2,1)S(1)}, u32[]{:S(2)}, u32[]{:S(2)}) %all-to-all-start.1) | async-done | bytes 393248 | tf_op jit(solution)/shard_map/all_to_all | solution.py:25
  52.5 1.7 shard_map.137
  54.2 5.6 %all-to-all-start.2 = ((bf16[64,16,128]{2,1,0:T(8,128)(2,1)}), bf16[64,16,128]{2,1,0:T(8,128)(2,1)S(1)}, u32[]{:S(2)}, u32[]{:S(2)}) async-start(bf16[64,16,128]{2,1,0:T(8,128)(2,1)} %shard_map.137), calls=%async_computation.2 | async-start | bytes 524288 | tf_op jit(solution)/shard_map/all_to_all | solution.py:25
  59.8 0.0 copy-start.5
  59.8 1.0 pad_maximum_fusion
  60.8 2.4 %collective-permute-start = (bf16[2,128,1792]{2,1,0:T(8,128)(2,1)}, bf16[2,128,1792]{2,1,0:T(8,128)(2,1)S(1)}, u32[]{:S(2)}, u32[]{:S(2)}) collective-permute-start(bf16[2,128,1792]{2,1,0:T(8,128)(2,1)} %pad_maximum_fusion), channel_id=1, source_target_pairs={{0,8},{8,0},{1,9},{9,1},{2,10},{10,2},{3,11},{11,3},{4,12},{12,4},... | collective-permute-start | bytes 2752520 | tf_op jit(solution)/shard_map/ppermute | solution.py:274
  63.2 9.2 %all-to-all-done.2.att_ref = bf16[64,16,128]{2,1,0:T(8,128)(2,1)S(1)} async-done(((bf16[64,16,128]{2,1,0:T(8,128)(2,1)}), bf16[64,16,128]{2,1,0:T(8,128)(2,1)S(1)}, u32[]{:S(2)}, u32[]{:S(2)}) %all-to-all-start.2) | async-done | bytes 262176 | tf_op jit(solution)/shard_map/all_to_all | solution.py:25
  72.4 0.3 shard_map.138
  72.6 19.6 %all_to_all.36.part_ref = bf16[8,128,128]{2,1,0:T(8,128)(2,1)S(1)} all-to-all(bf16[8,128,128]{2,1,0:T(8,128)(2,1)S(1)} %shard_map.138), channel_id=1, replica_groups=mesh['y'=8,'zl'=4,'core'=2,'zh'=2,'x'=4] {'zh','x'}, dimensions={0} | all-to-all | bytes 524288 | tf_op jit(solution)/shard_map/all_to_all | solution.py:25
  92.3 0.7 copy-done.11
  92.9 0.1 shard_map.139
  93.1 3.9 %all-gather = bf16[4,128,128]{2,1,0:T(8,128)(2,1)S(1)} all-gather(bf16[2,128,128]{2,1,0:T(8,128)(2,1)S(1)} %get-tuple-element.9), channel_id=2, replica_groups=mesh['y'=8,'zl'=4,'core'=2,'zh'=2,'x'=4] {'core'}, dimensions={0}, use_global_device_ids=true | all-gather | bytes 196608 | tf_op jit(solution)/shard_map/all_gather | solution.py:299
  97.0 0.6 shard_map.140
  97.6 31.9 %all_to_all.37.part_ref = bf16[32,120,128]{2,1,0:T(8,128)(2,1)S(1)} all-to-all(bf16[32,120,128]{2,1,0:T(8,128)(2,1)S(1)} %bitcast.15), channel_id=1, replica_groups=mesh['y'=8,'zl'=4,'core'=2,'zh'=2,'x'=4] {'y','zl'}, dimensions={0} | all-to-all | bytes 1966080 | tf_op jit(solution)/shard_map/all_to_all | solution.py:25
  129.6 0.3 shard_map.141
  129.8 23.1 %all_to_all.38 = bf16[32,64,128]{2,1,0:T(8,128)(2,1)S(1)} all-to-all(bf16[32,64,128]{2,1,0:T(8,128)(2,1)S(1)} %shard_map.141), channel_id=1, replica_groups=mesh['y'=8,'zl'=4,'core'=2,'zh'=2,'x'=4] {'y','zl'}, dimensions={0} | all-to-all | bytes 1048576 | tf_op jit(solution)/shard_map/all_to_all | solution.py:25
  152.9 4.2 %collective-permute-start.1 = (bf16[32,64,128]{2,1,0:T(8,128)(2,1)S(1)}, bf16[32,64,128]{2,1,0:T(8,128)(2,1)S(1)}, u32[]{:S(2)}, u32[]{:S(2)}) collective-permute-start(bf16[32,64,128]{2,1,0:T(8,128)(2,1)S(1)} %all_to_all.38), channel_id=1, source_target_pairs={{0,8},{8,0},{1,9},{9,1},{2,10},{10,2},{3,11},{11,3},{4,12},{12,4},... | collective-permute-start | bytes 1572872 | tf_op jit(solution)/shard_map/ppermute | solution.py:314
  157.2 1.5 collective-permute-done.1
  158.7 0.7 copy-done.12
  159.3 1.2 shard_map.142
  160.6 3.3 %all-to-all-start.6 = ((bf16[8,16,128]{2,1,0:T(8,128)(2,1)}), bf16[8,16,128]{2,1,0:T(8,128)(2,1)S(1)}, u32[]{:S(2)}, u32[]{:S(2)}) async-start(bf16[8,16,128]{2,1,0:T(8,128)(2,1)} %bitcast.10), calls=%async_computation.6 | async-start | bytes 65536 | tf_op jit(solution)/shard_map/all_to_all | solution.py:25
  163.9 8.9 %all-to-all-done.6 = bf16[8,16,128]{2,1,0:T(8,128)(2,1)S(1)} async-done(((bf16[8,16,128]{2,1,0:T(8,128)(2,1)}), bf16[8,16,128]{2,1,0:T(8,128)(2,1)S(1)}, u32[]{:S(2)}, u32[]{:S(2)}) %all-to-all-start.6) | async-done | bytes 32800 | tf_op jit(solution)/shard_map/all_to_all | solution.py:25
  172.9 0.6 fusion
  (24 shorter events, 0.1 us)
Async XLA Ops:
  0.0 27.8 %copy-start.3 = (bf16[24,128,128]{2,1,0:T(8,128)(2,1)S(1)}, bf16[24,128,128]{2,1,0:T(8,128)(2,1)}, u32[]{:S(2)}) copy-start(bf16[24,128,128]{2,1,0:T(8,128)(2,1)} %k_ref.1) | copy-start | bytes 2359300
  0.8 27.0 %copy-start.8 = (s32[128]{0:T(128)S(1)}, s32[128]{0:T(128)}, u32[]{:S(2)}) copy-start(s32[128]{0:T(128)} %len_ref.1) | copy-start | bytes 1540
  27.8 1.1 copy-start.4
  28.9 0.8 copy-start.6
  29.8 7.7 %copy-start = (bf16[128,3584]{1,0:T(8,128)(2,1)S(1)}, bf16[128,3584]{1,0:T(8,128)(2,1)}, u32[]{:S(2)}) copy-start(bf16[128,3584]{1,0:T(8,128)(2,1)} %gate_ref.1) | copy-start | bytes 2752516
  29.8 7.7 %copy-start.1 = (bf16[128,3584]{1,0:T(8,128)(2,1)S(1)}, bf16[128,3584]{1,0:T(8,128)(2,1)}, u32[]{:S(2)}) copy-start(bf16[128,3584]{1,0:T(8,128)(2,1)} %up_ref.1) | copy-start | bytes 2752516
  32.3 20.2 %all-to-all-start.1 = ((bf16[64,24,128]{2,1,0:T(8,128)(2,1)}), bf16[64,24,128]{2,1,0:T(8,128)(2,1)S(1)}, u32[]{:S(2)}, u32[]{:S(2)}) async-start(bf16[64,24,128]{2,1,0:T(8,128)(2,1)} %shard_map.136), calls=%async_computation.1 | async-start | bytes 786432 | tf_op jit(solution)/shard_map/all_to_all | solution.py:25
  37.5 15.0 %copy-start.9 = (bf16[2,128]{1,0:T(2,128)(2,1)S(1)}, bf16[2,128]{1,0:T(2,128)(2,1)}, u32[]{:S(2)}) copy-start(bf16[2,128]{1,0:T(2,128)(2,1)} %fk_ref.1) | copy-start | bytes 1540
  37.5 15.0 %copy-start.10 = (bf16[2,128]{1,0:T(2,128)(2,1)S(1)}, bf16[2,128]{1,0:T(2,128)(2,1)}, u32[]{:S(2)}) copy-start(bf16[2,128]{1,0:T(2,128)(2,1)} %fv_ref.1) | copy-start | bytes 1540
  54.2 5.6 %copy-start.13 = (bf16[1,128,1792]{2,1,0:T(8,128)(2,1)S(1)}, bf16[1,128,1792]{2,1,0:T(8,128)(2,1)}, u32[]{:S(2)}) copy-start(bf16[1,128,1792]{2,1,0:T(8,128)(2,1)} %get-tuple-element.13) | copy-start | bytes 1376260
  54.2 18.2 %all-to-all-start.2 = ((bf16[64,16,128]{2,1,0:T(8,128)(2,1)}), bf16[64,16,128]{2,1,0:T(8,128)(2,1)S(1)}, u32[]{:S(2)}, u32[]{:S(2)}) async-start(bf16[64,16,128]{2,1,0:T(8,128)(2,1)} %shard_map.137), calls=%async_computation.2 | async-start | bytes 524288 | tf_op jit(solution)/shard_map/all_to_all | solution.py:25
  59.8 12.6 %copy-start.5 = (bf16[1024,128]{1,0:T(8,128)(2,1)S(1)}, bf16[1024,128]{1,0:T(8,128)(2,1)}, u32[]{:S(2)}) copy-start(bf16[1024,128]{1,0:T(8,128)(2,1)} %w_ref.2) | copy-start | bytes 786436
  60.8 36.2 %collective-permute-start = (bf16[2,128,1792]{2,1,0:T(8,128)(2,1)}, bf16[2,128,1792]{2,1,0:T(8,128)(2,1)S(1)}, u32[]{:S(2)}, u32[]{:S(2)}) collective-permute-start(bf16[2,128,1792]{2,1,0:T(8,128)(2,1)} %pad_maximum_fusion), channel_id=1, source_target_pairs={{0,8},{8,0},{1,9},{9,1},{2,10},{10,2},{3,11},{11,3},{4,12},{12,4},... | collective-permute-start | bytes 2752520 | tf_op jit(solution)/shard_map/ppermute | solution.py:274
  72.6 19.7 %copy-start.7 = (bf16[128,128]{1,0:T(8,128)(2,1)S(1)}, bf16[128,128]{1,0:T(8,128)(2,1)}, u32[]{:S(2)}) copy-start(bf16[128,128]{1,0:T(8,128)(2,1)} %resid_ref.1) | copy-start | bytes 98308
  92.3 0.7 copy-start.11
  129.6 29.1 %copy-start.2 = (bf16[3584,128]{1,0:T(8,128)(2,1)S(1)}, bf16[3584,128]{1,0:T(8,128)(2,1)}, u32[]{:S(2)}) copy-start(bf16[3584,128]{1,0:T(8,128)(2,1)} %w_ref.3) | copy-start | bytes 2752516
  152.9 5.7 %collective-permute-start.1 = (bf16[32,64,128]{2,1,0:T(8,128)(2,1)S(1)}, bf16[32,64,128]{2,1,0:T(8,128)(2,1)S(1)}, u32[]{:S(2)}, u32[]{:S(2)}) collective-permute-start(bf16[32,64,128]{2,1,0:T(8,128)(2,1)S(1)} %all_to_all.38), channel_id=1, source_target_pairs={{0,8},{8,0},{1,9},{9,1},{2,10},{10,2},{3,11},{11,3},{4,12},{12,4},... | collective-permute-start | bytes 1572872 | tf_op jit(solution)/shard_map/ppermute | solution.py:314
  158.7 0.7 copy-start.12
  160.6 12.3 %all-to-all-start.6 = ((bf16[8,16,128]{2,1,0:T(8,128)(2,1)}), bf16[8,16,128]{2,1,0:T(8,128)(2,1)S(1)}, u32[]{:S(2)}, u32[]{:S(2)}) async-start(bf16[8,16,128]{2,1,0:T(8,128)(2,1)} %bitcast.10), calls=%async_computation.6 | async-start | bytes 65536 | tf_op jit(solution)/shard_map/all_to_all | solution.py:25

commit v4 on v3

v4 whole, which is shorter than its diff:
```python
import jax
import jax.numpy as jnp
from jax import lax
from jax.experimental import pallas as pl
from jax.experimental.pallas import tpu as pltpu
from jax.sharding import Mesh
from jax.sharding import PartitionSpec as P

HD = 128
GROUP = 8
LANES = 128
EPS = 1e-05
NEG = -1e30
VMEM_LIMIT = 16 * 2**20
CTX = ("y", "zlh", "zll", "core")
RING = ("y", "zlh", "zll")
REST = ("y", "zlh")
TEAM = ("zll", "core")
GRP = ("zh", "x")
LAST = ("core", "zh", "x")
F32 = jnp.float32
BF16 = jnp.bfloat16
VMEM = pl.BlockSpec(memory_space=pltpu.VMEM)
SMEM = pl.BlockSpec(memory_space=pltpu.SMEM)


def exchange(x, axes):
    return lax.all_to_all(x, axes, 0, 0, tiled=True)


def lane_ids(shape):
    return lax.broadcasted_iota(jnp.int32, shape, len(shape) - 1)


def call(body, out_shape, in_specs, scratch=(), out_specs=None):
    return pl.pallas_call(
        body,
        out_shape=out_shape,
        in_specs=in_specs,
        out_specs=jax.tree.map(lambda _: VMEM, out_shape) if out_specs is None else out_specs,
        scratch_shapes=list(scratch),
        compiler_params=pltpu.CompilerParams(vmem_limit_bytes=VMEM_LIMIT),
    )


def prepare_body(len_ref, table_ref, gain_ref, order_ref, meta_ref, wide_gain_ref, pick_ref):
    slots = meta_ref.shape[0] // 2
    first = lax.axis_index(CTX) * slots
    table = table_ref[...] - first
    rows, cols = table.shape
    code = lax.broadcasted_iota(jnp.int32, (rows, cols), 0) * cols + lane_ids((rows, cols))
    for s in range(slots):
        found = jnp.min(jnp.where(table == s, code, rows * cols - 1))
        owner = found // cols
        meta_ref[s] = owner
        meta_ref[slots + s] = len_ref[owner] - (found % cols) * LANES
    wide_gain_ref[...] = jnp.broadcast_to(gain_ref[...].astype(F32), wide_gain_ref.shape)
    pick = lax.broadcasted_iota(jnp.int32, pick_ref.shape, 0) == order_ref[...]
    pick_ref[...] = pick.astype(F32).astype(BF16)


def cut_body(gate_ref, up_ref, *out_refs):
    me = lax.axis_index(TEAM)
    width = out_refs[0].shape[2]
    for flip, out_ref in enumerate(out_refs, 1):
        start = pl.multiple_of((me ^ flip) * width, LANES)
        out_ref[0] = gate_ref[:, pl.ds(start, width)]
        out_ref[1] = up_ref[:, pl.ds(start, width)]


def cut_down_body(w_ref, out_ref):
    other = 1 - lax.axis_index("core")
    height = out_ref.shape[1]
    for z in range(2):
        start = pl.multiple_of((2 * z + other) * height, LANES)
        out_ref[z] = w_ref[pl.ds(start, height), :]


def attend_body(meta_ref, q_ref, k_ref, v_ref, out_ref, top_ref, sum_ref, acc_ref):
    slots, page = k_ref.shape[0], k_ref.shape[1]
    top_ref[...] = jnp.full(top_ref.shape, NEG, F32)
    sum_ref[...] = jnp.zeros(sum_ref.shape, F32)
    acc_ref[...] = jnp.zeros(acc_ref.shape, F32)
    lane = lane_ids((GROUP, page))
    owners, scores = [], []
    for s in range(slots):
        owner, live = meta_ref[s], meta_ref[slots + s]
        home = owner // 2
        pair = q_ref[home % 2, home // 2].astype(F32)
        q = jnp.where(owner % 2 == 1, pair[GROUP:], pair[:GROUP]).astype(BF16)
        score = lax.dot_general(q, k_ref[s], (((1,), (1,)), ((), ())), preferred_element_type=F32)
        score = jnp.where(lane < live, score * HD ** (-0.5), NEG)
        best = jnp.max(score, axis=1, keepdims=True)
        top_ref[owner] = jnp.maximum(top_ref[owner], jnp.broadcast_to(best, (GROUP, LANES)))
        owners.append(owner)
        scores.append(score)
    for s in range(slots):
        owner = owners[s]
        shift = top_ref[owner].astype(BF16).astype(F32)
        weight = jnp.exp(scores[s] - shift)
        total = jnp.sum(weight, axis=1, keepdims=True)
        sum_ref[owner] = sum_ref[owner] + jnp.broadcast_to(total, (GROUP, LANES))
        acc_ref[owner] = acc_ref[owner] + jnp.dot(
            weight.astype(BF16), v_ref[s], preferred_element_type=F32
        )
    lane = lane_ids((GROUP, LANES))
    for d in range(out_ref.shape[0]):
        stats = jnp.zeros((GROUP, LANES), F32)
        for par in range(2):
            total = sum_ref[2 * d + par]
            high = total.astype(BF16).astype(F32)
            base = par * 64
            stats = jnp.where(lane == base, top_ref[2 * d + par], stats)
            stats = jnp.where(lane == base + 1, high, stats)
            stats = jnp.where(lane == base + 2, total - high, stats)
        block = jnp.concatenate([acc_ref[2 * d], acc_ref[2 * d + 1], stats], axis=0)
        out_ref[d] = block.astype(BF16)


def combine_body(part_ref, q_ref, fk_ref, fv_ref, out_ref):
    count = part_ref.shape[0]
    fk, fv = fk_ref[...].astype(F32), fv_ref[...].astype(F32)
    q = q_ref[...].astype(F32)
    done = []
    for par in range(2):
        base = par * 64
        mine = slice(par * GROUP, (par + 1) * GROUP)
        own = jnp.sum(q[mine] * fk[par : par + 1], axis=1, keepdims=True) * HD ** (-0.5)
        best = own
        for d in range(count):
            stats = part_ref[d].astype(F32)[2 * GROUP :]
            best = jnp.maximum(best, stats[:, base : base + 1])
        own_weight = jnp.exp(own - best)
        total = own_weight
        acc = own_weight.astype(BF16).astype(F32) * fv[par : par + 1]
        for d in range(count):
            block = part_ref[d].astype(F32)
            stats = block[2 * GROUP :]
            factor = jnp.exp(stats[:, base : base + 1] - best)
            total = total + factor * (stats[:, base + 1 : base + 2] + stats[:, base + 2 : base + 3])
            acc = acc + factor * block[mine]
        done.append(acc / total)
    rows = jnp.concatenate(done, axis=0).astype(BF16)
    for d in range(out_ref.shape[0]):
        out_ref[d] = rows


def project_body(att_ref, w_ref, out_ref, rows_ref):
    cores, count, per, _ = att_ref.shape
    for d in range(count):
        for c in range(cores):
            start = (d * cores + c) * per
            rows_ref[start : start + per, :] = att_ref[c, d].astype(F32)
    reqs = rows_ref.shape[0] // GROUP
    total = jnp.zeros((reqs, w_ref.shape[1]), F32)
    for h in range(GROUP):
        head = rows_ref[pl.ds(h, reqs, stride=GROUP), :].astype(BF16)
        total = total + jnp.dot(head, w_ref[h * HD : (h + 1) * HD, :], preferred_element_type=F32)
    total = total.astype(BF16)
    for g in range(out_ref.shape[0]):
        out_ref[g] = total


def turned(column):
    return jnp.transpose(jnp.broadcast_to(column, (LANES, LANES)))


def hidden_body(part_ref, resid_ref, gain_ref, hidden_ref, pay_ref):
    projected = part_ref[0].astype(F32)
    for g in range(1, part_ref.shape[0]):
        projected = projected + part_ref[g].astype(F32)
    hidden = (resid_ref[...].astype(F32) + projected).astype(BF16)
    hidden_ref[...] = hidden
    wide = hidden.astype(F32)
    reqs = wide.shape[0]
    pay_ref[:reqs] = (wide * gain_ref[0:1, :]).astype(BF16)
    square = jnp.sum(wide * wide, axis=1, keepdims=True)
    square = jnp.concatenate([square, jnp.zeros((LANES - reqs, 1), F32)], axis=0) if reqs < LANES else square
    square = turned(square)[:8]
    high = square.astype(BF16).astype(F32)
    row = lax.broadcasted_iota(jnp.int32, (8, LANES), 0)
    pay_ref[reqs:] = jnp.where(row == 0, high, jnp.where(row == 1, square - high, 0.0)).astype(BF16)


def widen_body(pay_ref, gate_ref, up_ref, met1_ref, met2_ref, met3_ref, out_ref):
    me = lax.axis_index(TEAM)
    team, reqs = pay_ref.shape[0], pay_ref.shape[1] - 8
    mets = (met1_ref, met2_ref, met3_ref)
    width = met1_ref.shape[2]
    start = pl.multiple_of(me * width, LANES)
    tiles = []
    for which, ref in enumerate((gate_ref, up_ref)):
        x = jnp.dot(pay_ref[me, :reqs], ref[:, pl.ds(start, width)], preferred_element_type=F32)
        for flip, met_ref in enumerate(mets, 1):
            x = x + jnp.dot(pay_ref[me ^ flip, :reqs], met_ref[which], preferred_element_type=F32)
        for b in range(width // LANES):
            tiles.append(x[:, b * LANES : (b + 1) * LANES].reshape(reqs // 8, 8, LANES))
    for i in range(len(tiles) // 2):
        out_ref[:, i * 16 : (i + 1) * 16, :] = jnp.concatenate(
            [tiles[2 * i], tiles[2 * i + 1]], axis=1
        ).astype(BF16)
    square = pay_ref[0, reqs:].astype(F32)
    for d in range(1, team):
        square = square + pay_ref[d, reqs:].astype(F32)
    square = turned(square[0:1] + square[1:2])[:reqs]
    high = square.astype(BF16).astype(F32)
    lane = lane_ids(square.shape)
    square = jnp.where(lane == 0, high, jnp.where(lane == 1, square - high, 0.0))
    out_ref[:, len(tiles) * 8 :, :] = square.reshape(reqs // 8, 8, LANES).astype(BF16)


def activate_body(width, part_ref, out_ref):
    total = part_ref[0].astype(F32)
    for d in range(1, part_ref.shape[0]):
        total = total + part_ref[d].astype(F32)
    units = (total.shape[0] - 8) // 2
    square = total[2 * units :]
    square = square[:, 0:1] + square[:, 1:2]
    inv_rms = lax.rsqrt(jnp.broadcast_to(square, (8, LANES)) / width + EPS)[None]
    gate = total[:units].reshape(units // 8, 8, LANES) * inv_rms
    up = total[units : 2 * units].reshape(units // 8, 8, LANES) * inv_rms
    active = (gate / (1.0 + jnp.exp(-gate)) * up).reshape(units, LANES).astype(BF16)
    for d in range(out_ref.shape[0]):
        out_ref[d] = active


def down_body(act_ref, w_ref, met_ref, pick_ref, hidden_ref, out_ref, kept_ref):
    core = lax.axis_index("core")
    dests = act_ref.shape[0]
    reqs = dests * 8
    height = met_ref.shape[1]
    mine = jnp.zeros((reqs, LANES), F32)
    other = jnp.zeros((reqs, LANES), F32)
    for z in range(2):
        act = act_ref[:, z].astype(F32)
        blocks = [
            act[:, b * 8 : b * 8 + 8].reshape(reqs, LANES).astype(BF16) for b in range(height // LANES)
        ]
        act = jnp.concatenate(blocks, axis=1)
        start = pl.multiple_of((2 * z + core) * height, LANES)
        mine = mine + jnp.dot(act, w_ref[pl.ds(start, height), :], preferred_element_type=F32)
        other = other + jnp.dot(act, met_ref[z], preferred_element_type=F32)
    pick = pick_ref[...]
    dims = (((0,), (0,)), ((), ()))
    out_ref[core] = lax.dot_general(
        pick, mine.astype(BF16), dims, preferred_element_type=F32
    ).astype(BF16)
    out_ref[1 - core] = lax.dot_general(
        pick, other.astype(BF16), dims, preferred_element_type=F32
    ).astype(BF16)
    kept = lax.dot_general(pick, hidden_ref[...], dims, preferred_element_type=F32)
    kept_ref[...] = kept.astype(BF16)


def shards(
    queries,
    fresh_keys,
    fresh_values,
    key_cache,
    value_cache,
    lengths,
    block_table,
    resid,
    out_weight,
    norm_gain,
    gate_weight,
    up_weight,
    down_weight,
    row_order,
):
    ctx, ring, rest, grp = (lax.axis_size(axes) for axes in (CTX, RING, REST, GRP))
    team = lax.axis_size(TEAM)
    reqs, width = resid.shape
    slots = key_cache.shape[0]
    shape = jax.ShapeDtypeStruct

    quarter = gate_weight.shape[1] // team
    given = call(cut_body, (shape((2, width, quarter), BF16),) * 3, [VMEM] * 2)(gate_weight, up_weight)
    met = [
        lax.ppermute(block, TEAM, [(i, i ^ flip) for i in range(team)])
        for flip, block in enumerate(given, 1)
    ]
    given_down = call(cut_down_body, shape((2, quarter, width), BF16), [VMEM])(down_weight)
    met_down = lax.ppermute(given_down, "core", [(0, 1), (1, 0)])
    meta, wide_gain, pick = call(
        prepare_body,
        (shape((2 * slots,), jnp.int32), shape((8, width), F32), shape((reqs, reqs), BF16)),
        [SMEM] + [VMEM] * 3,
        out_specs=(SMEM, VMEM, VMEM),
    )(lengths, block_table, norm_gain.reshape(1, width), row_order.reshape(1, reqs))

    my_queries = queries.reshape(2 * GROUP, HD)
    all_queries = exchange(jnp.broadcast_to(my_queries[None], (ring, 2 * GROUP, HD)), RING)
    all_queries = lax.all_gather(all_queries, "core", axis=0, tiled=False)
    scratch = [pltpu.VMEM((reqs, GROUP, LANES), F32)] * 3
    parts = call(attend_body, shape((ctx, 3 * GROUP, HD), BF16), [SMEM] + [VMEM] * 3, scratch)(
        meta, all_queries, key_cache, value_cache
    )
    parts = exchange(parts, CTX)
    local = call(combine_body, shape((ring, 2 * GROUP, HD), BF16), [VMEM] * 4)(
        parts, my_queries, fresh_keys, fresh_values
    )
    attended = lax.all_gather(exchange(local, RING), "core", axis=0, tiled=False)
    attended, *met = lax.optimization_barrier((attended, *met))
    projected = call(
        project_body,
        shape((grp, reqs, width), BF16),
        [VMEM] * 2,
        [pltpu.VMEM((reqs * GROUP, HD), F32)],
    )(attended, out_weight)
    projected = exchange(projected, GRP)
    hidden, pay = call(
        hidden_body,
        (shape((reqs, width), BF16), shape((reqs + 8, width), BF16)),
        [VMEM] * 3,
    )(projected, resid, wide_gain)
    pay = lax.all_gather(pay, TEAM, axis=0, tiled=False)
    units = quarter // LANES * 8
    wide = call(widen_body, shape((rest, 2 * units + 8, LANES), BF16), [VMEM] * 6)(
        pay, gate_weight, up_weight, *met
    )
    wide = exchange(wide, REST)
    model_width = width * ctx

    def activate(part_ref, out_ref):
        activate_body(model_width, part_ref, out_ref)

    active = call(activate, shape((ring, units, LANES), BF16), [VMEM])(wide)
    active = exchange(active, RING)
    rows, kept = call(
        down_body,
        (shape((2, reqs, width), BF16), shape((reqs, width), BF16)),
        [VMEM] * 5,
    )(active.reshape(rest, 2, units, LANES), down_weight, met_down, pick, hidden)
    share = reqs // grp
    rows = exchange(rows.reshape(2 * grp, share, width), LAST)
    kept = lax.dynamic_index_in_dim(kept.reshape(grp, share, width), lax.axis_index(GRP), 0, False)
    return (kept.astype(F32) + jnp.sum(rows.astype(F32), axis=0)).astype(BF16)


def solution(mesh, sizes=(8, 2, 2, 2, 2, 4)):
    inner = Mesh(mesh.devices.reshape(sizes), ("y", "zlh", "zll", "core", "zh", "x"))
    in_specs = (
        P(CTX, GRP),
        P(CTX, GRP),
        P(CTX, GRP),
        P(CTX, None, GRP),
        P(CTX, None, GRP),
        P(),
        P(),
        P(None, CTX),
        P(GRP, CTX),
        P(CTX),
        P(CTX, GRP),
        P(CTX, GRP),
        P(GRP, CTX),
        P(),
    )
    out_specs = P(GRP, CTX)
    return jax.shard_map(shards, mesh=inner, in_specs=in_specs, out_specs=out_specs, check_vma=False)
```

time: 174 us -> 168 us (0.966)
  blocking collectives: 106 us -> 76.4 us
  starting transfers between devices: 20.5 us -> 41.4 us
  Pallas kernels: 6.75 us -> 10.4 us
    all_to_all x4 -> x3, blocking collectives: 102 us -> 61.4 us  [exchange(): return lax.all_to_all(x, axes, 0, 0, tiled=True)]
    all_to_all x3 -> x4, starting transfers between devices: 14 us -> 30.3 us  [exchange(): return lax.all_to_all(x, axes, 0, 0, tiled=True)]
    all_gather x1 -> x3, blocking collectives: 3.91 us -> 15 us  [the longest x1 8.53 us: shards(): pay = lax.all_gather(pay, TEAM, axis=0, tiled=False)]
    ppermute x2 -> x4, starting transfers between devices: 6.56 us -> 11.1 us  [the longest x3 7.92 us: shards(): lax.ppermute(block, TEAM, [(i, i ^ flip) for i in range(team)])]
    pallas_call x6 -> x9, Pallas kernels: 6.5 us -> 10.2 us  [the longest x1 2.25 us: shards(): call(attend_body, shape((ctx, 3 * GROUP, HD), BF16), [SMEM] + [VMEM] * 3,...]
    all_to_all x3 -> x4, waiting for transfers between devices: 32.3 us -> 31.6 us  [exchange(): return lax.all_to_all(x, axes, 0, 0, tiled=True)]
    unnamed x28 -> x26, local copies, waits for them, and re-layouts: 3.33 us -> 3.97 us
  transfers between devices with their start and end apart: 5 -> 8, of which waited for: 4 -> 5; matrix products, arithmetic and copies ran while one was open for 1% -> 0% of each run, Pallas kernels for 0% -> 2%
where the time goes in v4:
time: 168 us; the launch traced here: 167 us
  blocking collectives  76.4 us (45%)
  starting transfers between devices  41.4 us (25%)
  waiting for transfers between devices  33 us (20%)
  Pallas kernels  10.4 us (6%)
  local copies, waits for them, and re-layouts  5.41 us (3%)
    all_to_all x3, blocking collectives, exchange(): return lax.all_to_all(x, axes, 0, 0, tiled=True)  61.4 us
    all_to_all x4, waiting for transfers between devices, exchange(): return lax.all_to_all(x, axes, 0, 0, tiled=True)  31.6 us
    all_to_all x4, starting transfers between devices, exchange(): return lax.all_to_all(x, axes, 0, 0, tiled=True)  30.3 us
    all_gather x1, blocking collectives, shards(): pay = lax.all_gather(pay, TEAM, axis=0, tiled=False)  8.53 us
    ppermute x3, starting transfers between devices, shards(): lax.ppermute(block, TEAM, [(i, i ^ flip) for i in range(team)])  7.92 us
    unnamed x26, local copies, waits for them, and re-layouts  3.97 us
    all_gather x1, blocking collectives, shards(): all_queries = lax.all_gather(all_queries, 'core', axis=0, tiled=False)  3.68 us
  transfers between devices with their start and end apart: 8, of which 5 were waited for; matrix products, arithmetic and copies ran while one was open for 0% of the time, Pallas kernels for 2%

profile of v4, /device:TPU:1, one launch (start us, length us, event | category | flops | bytes accessed | tf_op | source)
XLA Modules:
  0.0 167.4 jit_solution(5937196430875112077)
XLA Ops:
  0.0 0.8 broadcast_in_dim.7.q_ref
  0.8 0.7 broadcast_in_dim.8
  1.4 13.5 %all-to-all-start = ((bf16[32,16,128]{2,1,0:T(8,128)(2,1)}), bf16[32,16,128]{2,1,0:T(8,128)(2,1)S(1)}, u32[]{:S(2)}, u32[]{:S(2)}) async-start(bf16[32,16,128]{2,1,0:T(8,128)(2,1)} %broadcast_in_dim.8), calls=%async_computation | async-start | bytes 262144 | tf_op jit(solution)/shard_map/all_to_all | solution.py:28
  14.9 0.8 copy-done.6
  15.8 0.7 copy-done.8
  16.4 0.7 copy-done.9
  17.7 1.6 shard_map.136
  19.4 5.5 %all-to-all-done = bf16[32,16,128]{2,1,0:T(8,128)(2,1)S(1)} async-done(((bf16[32,16,128]{2,1,0:T(8,128)(2,1)}), bf16[32,16,128]{2,1,0:T(8,128)(2,1)S(1)}, u32[]{:S(2)}, u32[]{:S(2)}) %all-to-all-start) | async-done | bytes 131104 | tf_op jit(solution)/shard_map/all_to_all | solution.py:28
  24.9 3.7 %all-gather = bf16[64,16,128]{2,1,0:T(8,128)(2,1)S(1)} all-gather(bf16[32,16,128]{2,1,0:T(8,128)(2,1)S(1)} %all-to-all-done), channel_id=2, replica_groups=mesh['y'=8,'zlh'=2,'zll'=2,'core'=2,'zh'=2,'x'=4] {'core'}, dimensions={0}, use_global_device_ids=true | all-gather | bytes 393216 | tf_op jit(solution)/shard_map/all_gather | solution.py:294
  28.5 1.1 copy-done.4
  29.7 2.3 %shard_map.137 = bf16[64,24,128]{2,1,0:T(8,128)(2,1)} custom-call(s32[48]{0:T(128)S(1)} %get-tuple-element.19.meta_ref, bf16[2,32,16,128]{3,2,1,0:T(8,128)(2,1)S(1)} %bitcast.13, bf16[24,128,128]{2,1,0:T(8,128)(2,1)S(1)} %copy-done.3, bf16[24,128,128]{2,1,0:T(8,128)(2,1)S(1)} %copy-done.4), custom_call_target="tpu_custom_call" | custom-call | tf_op jit(solution)/shard_map/pallas_call | solution.py:296
  31.9 4.4 %all-to-all-start.1 = ((bf16[64,24,128]{2,1,0:T(8,128)(2,1)}), bf16[64,24,128]{2,1,0:T(8,128)(2,1)S(1)}, u32[]{:S(2)}, u32[]{:S(2)}) async-start(bf16[64,24,128]{2,1,0:T(8,128)(2,1)} %shard_map.137), calls=%async_computation.1 | async-start | bytes 786432 | tf_op jit(solution)/shard_map/all_to_all | solution.py:28
  36.4 1.2 shard_map.139
  37.6 2.5 %collective-permute-start = (bf16[2,128,896]{2,1,0:T(8,128)(2,1)}, bf16[2,128,896]{2,1,0:T(8,128)(2,1)S(1)}, u32[]{:S(2)}, u32[]{:S(2)}) collective-permute-start(bf16[2,128,896]{2,1,0:T(8,128)(2,1)} %get-tuple-element.20), channel_id=1, source_target_pairs={{0,8},{8,0},{16,24},{24,16},{1,9},{9,1},{17,25},{25,17},{2,10},{10... | collective-permute-start | bytes 1376264 | tf_op jit(solution)/shard_map/ppermute | solution.py:280
  40.1 3.1 %collective-permute-start.1 = (bf16[2,128,896]{2,1,0:T(8,128)(2,1)}, bf16[2,128,896]{2,1,0:T(8,128)(2,1)S(1)}, u32[]{:S(2)}, u32[]{:S(2)}) collective-permute-start(bf16[2,128,896]{2,1,0:T(8,128)(2,1)} %get-tuple-element.21), channel_id=1, source_target_pairs={{0,16},{8,24},{16,0},{24,8},{1,17},{9,25},{17,1},{25,9},{2,18},{10... | collective-permute-start | bytes 1376264 | tf_op jit(solution)/shard_map/ppermute | solution.py:280
  43.2 2.4 %collective-permute-start.2 = (bf16[2,128,896]{2,1,0:T(8,128)(2,1)}, bf16[2,128,896]{2,1,0:T(8,128)(2,1)}, u32[]{:S(2)}, u32[]{:S(2)}) collective-permute-start(bf16[2,128,896]{2,1,0:T(8,128)(2,1)} %get-tuple-element.22), channel_id=1, source_target_pairs={{0,24},{8,16},{16,8},{24,0},{1,25},{9,17},{17,9},{25,1},{2,26},{10... | collective-permute-start | bytes 1376264 | tf_op jit(solution)/shard_map/ppermute | solution.py:280
  45.6 6.0 %all-to-all-done.1.part_ref = bf16[64,24,128]{2,1,0:T(8,128)(2,1)S(1)} async-done(((bf16[64,24,128]{2,1,0:T(8,128)(2,1)}), bf16[64,24,128]{2,1,0:T(8,128)(2,1)S(1)}, u32[]{:S(2)}, u32[]{:S(2)}) %all-to-all-start.1) | async-done | bytes 393248 | tf_op jit(solution)/shard_map/all_to_all | solution.py:28
  51.6 1.1 shard_map.138
  52.6 18.0 %all_to_all.35 = bf16[32,16,128]{2,1,0:T(8,128)(2,1)S(1)} all-to-all(bf16[32,16,128]{2,1,0:T(8,128)(2,1)S(1)} %shard_map.138), channel_id=1, replica_groups=mesh['y'=8,'zlh'=2,'zll'=2,'core'=2,'zh'=2,'x'=4] {'y','zlh','zll'}, dimensions={0} | all-to-all | bytes 262144 | tf_op jit(solution)/shard_map/all_to_all | solution.py:28
  70.6 2.8 %all-gather.1 = bf16[64,16,128]{2,1,0:T(8,128)(2,1)S(1)} all-gather(bf16[32,16,128]{2,1,0:T(8,128)(2,1)S(1)} %all_to_all.35), channel_id=3, replica_groups=mesh['y'=8,'zlh'=2,'zll'=2,'core'=2,'zh'=2,'x'=4] {'core'}, dimensions={0}, use_global_device_ids=true | all-gather | bytes 393216 | tf_op jit(solution)/shard_map/all_gather | solution.py:303
  73.7 19.6 %all_to_all.36.part_ref = bf16[8,128,128]{2,1,0:T(8,128)(2,1)S(1)} all-to-all(bf16[8,128,128]{2,1,0:T(8,128)(2,1)S(1)} %shard_map.140), channel_id=1, replica_groups=mesh['y'=8,'zlh'=2,'zll'=2,'core'=2,'zh'=2,'x'=4] {'zh','x'}, dimensions={0} | all-to-all | bytes 524288 | tf_op jit(solution)/shard_map/all_to_all | solution.py:28
  93.5 8.5 %all-gather.2 = bf16[544,128]{1,0:T(8,128)(2,1)S(1)} all-gather(bf16[136,128]{1,0:T(8,128)(2,1)S(1)} %get-tuple-element.25), channel_id=4, replica_groups=mesh['y'=8,'zlh'=2,'zll'=2,'core'=2,'zh'=2,'x'=4] {'zll','core'}, dimensions={0}, use_global_device_ids=true | all-gather | bytes 174080 | tf_op jit(solution)/shard_map/all_gather | solution.py:317
  102.0 1.6 shard_map.142
  103.7 23.8 %all_to_all.37.part_ref = bf16[16,120,128]{2,1,0:T(8,128)(2,1)S(1)} all-to-all(bf16[16,120,128]{2,1,0:T(8,128)(2,1)S(1)} %shard_map.142), channel_id=1, replica_groups=mesh['y'=8,'zlh'=2,'zll'=2,'core'=2,'zh'=2,'x'=4] {'y','zlh'}, dimensions={0} | all-to-all | bytes 983040 | tf_op jit(solution)/shard_map/all_to_all | solution.py:28
  127.4 1.0 shard_map.143
  128.4 6.0 %all-to-all-start.5 = ((bf16[32,56,128]{2,1,0:T(8,128)(2,1)}), bf16[32,56,128]{2,1,0:T(8,128)(2,1)S(1)}, u32[]{:S(2)}, u32[]{:S(2)}) async-start(bf16[32,56,128]{2,1,0:T(8,128)(2,1)} %shard_map.143), calls=%async_computation.5 | async-start | bytes 917504 | tf_op jit(solution)/shard_map/all_to_all | solution.py:28
  134.4 3.2 %collective-permute-start.3 = (bf16[2,896,128]{2,1,0:T(8,128)(2,1)S(1)}, bf16[2,896,128]{2,1,0:T(8,128)(2,1)S(1)}, u32[]{:S(2)}, u32[]{:S(2)}) collective-permute-start(bf16[2,896,128]{2,1,0:T(8,128)(2,1)S(1)} %shard_map.144), channel_id=1, source_target_pairs={{0,8},{8,0},{1,9},{9,1},{2,10},{10,2},{3,11},{11,3},{4,12},{12,4},... | collective-permute-start | bytes 1376264 | tf_op jit(solution)/shard_map/ppermute | solution.py:284
  137.7 1.4 collective-permute-done.3.met_ref
  139.1 10.4 %all-to-all-done.5 = bf16[32,56,128]{2,1,0:T(8,128)(2,1)S(1)} async-done(((bf16[32,56,128]{2,1,0:T(8,128)(2,1)}), bf16[32,56,128]{2,1,0:T(8,128)(2,1)S(1)}, u32[]{:S(2)}, u32[]{:S(2)}) %all-to-all-start.5) | async-done | bytes 458784 | tf_op jit(solution)/shard_map/all_to_all | solution.py:28
  149.5 1.2 shard_map.145
  150.6 6.4 %all-to-all-start.6 = ((bf16[16,16,128]{2,1,0:T(8,128)(2,1)}), bf16[16,16,128]{2,1,0:T(8,128)(2,1)S(1)}, u32[]{:S(2)}, u32[]{:S(2)}) async-start(bf16[16,16,128]{2,1,0:T(8,128)(2,1)} %bitcast.8), calls=%async_computation.6 | async-start | bytes 131072 | tf_op jit(solution)/shard_map/all_to_all | solution.py:28
  157.0 9.8 %all-to-all-done.6 = bf16[16,16,128]{2,1,0:T(8,128)(2,1)S(1)} async-done(((bf16[16,16,128]{2,1,0:T(8,128)(2,1)}), bf16[16,16,128]{2,1,0:T(8,128)(2,1)S(1)}, u32[]{:S(2)}, u32[]{:S(2)}) %all-to-all-start.6) | async-done | bytes 65568 | tf_op jit(solution)/shard_map/all_to_all | solution.py:28
  (30 shorter events, 1.8 us)
Async XLA Ops:
  0.0 28.5 %copy-start.3 = (bf16[24,128,128]{2,1,0:T(8,128)(2,1)S(1)}, bf16[24,128,128]{2,1,0:T(8,128)(2,1)}, u32[]{:S(2)}) copy-start(bf16[24,128,128]{2,1,0:T(8,128)(2,1)} %k_ref.1) | copy-start | bytes 2359300
  1.4 23.4 %all-to-all-start = ((bf16[32,16,128]{2,1,0:T(8,128)(2,1)}), bf16[32,16,128]{2,1,0:T(8,128)(2,1)S(1)}, u32[]{:S(2)}, u32[]{:S(2)}) async-start(bf16[32,16,128]{2,1,0:T(8,128)(2,1)} %broadcast_in_dim.8), calls=%async_computation | async-start | bytes 262144 | tf_op jit(solution)/shard_map/all_to_all | solution.py:28
  14.9 0.8 copy-start.6
  15.8 0.7 copy-start.8
  16.4 0.7 copy-start.9
  17.1 0.7 copy-start.10
  28.5 1.1 copy-start.4
  29.7 6.7 %copy-start.1 = (bf16[128,3584]{1,0:T(8,128)(2,1)S(1)}, bf16[128,3584]{1,0:T(8,128)(2,1)}, u32[]{:S(2)}) copy-start(bf16[128,3584]{1,0:T(8,128)(2,1)} %gate_ref.3) | copy-start | bytes 2752516
  29.7 6.7 %copy-start.2 = (bf16[128,3584]{1,0:T(8,128)(2,1)S(1)}, bf16[128,3584]{1,0:T(8,128)(2,1)}, u32[]{:S(2)}) copy-start(bf16[128,3584]{1,0:T(8,128)(2,1)} %up_ref.3) | copy-start | bytes 2752516
  31.9 19.6 %all-to-all-start.1 = ((bf16[64,24,128]{2,1,0:T(8,128)(2,1)}), bf16[64,24,128]{2,1,0:T(8,128)(2,1)S(1)}, u32[]{:S(2)}, u32[]{:S(2)}) async-start(bf16[64,24,128]{2,1,0:T(8,128)(2,1)} %shard_map.137), calls=%async_computation.1 | async-start | bytes 786432 | tf_op jit(solution)/shard_map/all_to_all | solution.py:28
  37.6 35.8 %collective-permute-start = (bf16[2,128,896]{2,1,0:T(8,128)(2,1)}, bf16[2,128,896]{2,1,0:T(8,128)(2,1)S(1)}, u32[]{:S(2)}, u32[]{:S(2)}) collective-permute-start(bf16[2,128,896]{2,1,0:T(8,128)(2,1)} %get-tuple-element.20), channel_id=1, source_target_pairs={{0,8},{8,0},{16,24},{24,16},{1,9},{9,1},{17,25},{25,17},{2,10},{10... | collective-permute-start | bytes 1376264 | tf_op jit(solution)/shard_map/ppermute | solution.py:280
  40.1 11.5 %copy-start.11 = (bf16[2,128]{1,0:T(2,128)(2,1)S(1)}, bf16[2,128]{1,0:T(2,128)(2,1)}, u32[]{:S(2)}) copy-start(bf16[2,128]{1,0:T(2,128)(2,1)} %fk_ref.1) | copy-start | bytes 1540
  40.1 11.5 %copy-start.12 = (bf16[2,128]{1,0:T(2,128)(2,1)S(1)}, bf16[2,128]{1,0:T(2,128)(2,1)}, u32[]{:S(2)}) copy-start(bf16[2,128]{1,0:T(2,128)(2,1)} %fv_ref.1) | copy-start | bytes 1540
  40.1 33.3 %collective-permute-start.1 = (bf16[2,128,896]{2,1,0:T(8,128)(2,1)}, bf16[2,128,896]{2,1,0:T(8,128)(2,1)S(1)}, u32[]{:S(2)}, u32[]{:S(2)}) collective-permute-start(bf16[2,128,896]{2,1,0:T(8,128)(2,1)} %get-tuple-element.21), channel_id=1, source_target_pairs={{0,16},{8,24},{16,0},{24,8},{1,17},{9,25},{17,1},{25,9},{2,18},{10... | collective-permute-start | bytes 1376264 | tf_op jit(solution)/shard_map/ppermute | solution.py:280
  43.2 30.2 %collective-permute-start.2 = (bf16[2,128,896]{2,1,0:T(8,128)(2,1)}, bf16[2,128,896]{2,1,0:T(8,128)(2,1)}, u32[]{:S(2)}, u32[]{:S(2)}) collective-permute-start(bf16[2,128,896]{2,1,0:T(8,128)(2,1)} %get-tuple-element.22), channel_id=1, source_target_pairs={{0,24},{8,16},{16,8},{24,0},{1,25},{9,17},{17,9},{25,1},{2,26},{10... | collective-permute-start | bytes 1376264 | tf_op jit(solution)/shard_map/ppermute | solution.py:280
  70.6 2.8 %copy-start.5 = (bf16[1024,128]{1,0:T(8,128)(2,1)S(1)}, bf16[1024,128]{1,0:T(8,128)(2,1)}, u32[]{:S(2)}) copy-start(bf16[1024,128]{1,0:T(8,128)(2,1)} %w_ref.3) | copy-start | bytes 786436
  73.6 19.7 %copy-start.7 = (bf16[128,128]{1,0:T(8,128)(2,1)S(1)}, bf16[128,128]{1,0:T(8,128)(2,1)}, u32[]{:S(2)}) copy-start(bf16[128,128]{1,0:T(8,128)(2,1)} %resid_ref.1) | copy-start | bytes 98308
  127.4 7.0 %copy-start = (bf16[3584,128]{1,0:T(8,128)(2,1)S(1)}, bf16[3584,128]{1,0:T(8,128)(2,1)}, u32[]{:S(2)}) copy-start(bf16[3584,128]{1,0:T(8,128)(2,1)} %w_ref.5) | copy-start | bytes 2752516
  128.4 21.1 %all-to-all-start.5 = ((bf16[32,56,128]{2,1,0:T(8,128)(2,1)}), bf16[32,56,128]{2,1,0:T(8,128)(2,1)S(1)}, u32[]{:S(2)}, u32[]{:S(2)}) async-start(bf16[32,56,128]{2,1,0:T(8,128)(2,1)} %shard_map.143), calls=%async_computation.5 | async-start | bytes 917504 | tf_op jit(solution)/shard_map/all_to_all | solution.py:28
  134.4 4.6 %collective-permute-start.3 = (bf16[2,896,128]{2,1,0:T(8,128)(2,1)S(1)}, bf16[2,896,128]{2,1,0:T(8,128)(2,1)S(1)}, u32[]{:S(2)}, u32[]{:S(2)}) collective-permute-start(bf16[2,896,128]{2,1,0:T(8,128)(2,1)S(1)} %shard_map.144), channel_id=1, source_target_pairs={{0,8},{8,0},{1,9},{9,1},{2,10},{10,2},{3,11},{11,3},{4,12},{12,4},... | collective-permute-start | bytes 1376264 | tf_op jit(solution)/shard_map/ppermute | solution.py:284
  150.6 16.2 %all-to-all-start.6 = ((bf16[16,16,128]{2,1,0:T(8,128)(2,1)}), bf16[16,16,128]{2,1,0:T(8,128)(2,1)S(1)}, u32[]{:S(2)}, u32[]{:S(2)}) async-start(bf16[16,16,128]{2,1,0:T(8,128)(2,1)} %bitcast.8), calls=%async_computation.6 | async-start | bytes 131072 | tf_op jit(solution)/shard_map/all_to_all | solution.py:28

commit v5 on v4

v5 whole, which is shorter than its diff:
```python
import functools

import jax
import jax.numpy as jnp
from jax import lax
from jax.experimental import pallas as pl
from jax.experimental.pallas import tpu as pltpu
from jax.sharding import Mesh
from jax.sharding import PartitionSpec as P

HD = 128
GROUP = 8
LANES = 128
EPS = 1e-05
NEG = -1e30
VMEM_LIMIT = 16 * 2**20
CTX = ("yh", "yl", "zl", "core")
RING = ("yh", "yl", "zl")
REST = ("yh", "zl")
TEAM = ("yl", "core")
GRP = ("zh", "x")
LAST = TEAM + GRP
F32 = jnp.float32
BF16 = jnp.bfloat16
VMEM = pl.BlockSpec(memory_space=pltpu.VMEM)
SMEM = pl.BlockSpec(memory_space=pltpu.SMEM)


def exchange(x, axes):
    return lax.all_to_all(x, axes, 0, 0, tiled=True)


def lane_ids(shape):
    return lax.broadcasted_iota(jnp.int32, shape, len(shape) - 1)


def call(body, out_shape, in_specs, scratch=(), out_specs=None):
    return pl.pallas_call(
        body,
        out_shape=out_shape,
        in_specs=in_specs,
        out_specs=jax.tree.map(lambda _: VMEM, out_shape) if out_specs is None else out_specs,
        scratch_shapes=list(scratch),
        compiler_params=pltpu.CompilerParams(vmem_limit_bytes=VMEM_LIMIT),
    )


def request_of(place, ring):
    core, at = place >> ring.bit_length(), place & (2 * ring - 1)
    return (at >> 1) * 4 + core * 2 + (at & 1)


def prepare_body(ring, len_ref, table_ref, order_ref, meta_ref, pick_ref):
    slots = meta_ref.shape[0] // 2
    first = lax.axis_index(CTX) * slots
    table = table_ref[...] - first
    rows, cols = table.shape
    code = lax.broadcasted_iota(jnp.int32, (rows, cols), 0) * cols + lane_ids((rows, cols))
    for s in range(slots):
        found = jnp.min(jnp.where(table == s, code, rows * cols - 1))
        owner = found // cols
        meta_ref[s] = owner
        meta_ref[slots + s] = len_ref[owner] - (found % cols) * LANES
    place = lax.broadcasted_iota(jnp.int32, pick_ref.shape, 0)
    pick = request_of(place, ring) == order_ref[...]
    pick_ref[...] = pick.astype(F32).astype(BF16)


def cut_body(ring, gate_ref, up_ref, down_ref, resid_ref, gain_ref, *out_refs):
    me = lax.axis_index(TEAM)
    mine, out_refs = out_refs[0], out_refs[1:]
    reqs = resid_ref.shape[0]
    place = lax.broadcasted_iota(jnp.int32, (reqs, reqs), 0)
    turn = (request_of(place, ring) == lane_ids((reqs, reqs))).astype(F32).astype(BF16)
    resid = jnp.dot(turn, resid_ref[...], preferred_element_type=F32).astype(BF16)
    gain = jnp.broadcast_to(gain_ref[...].astype(F32), (LANES, LANES)).astype(BF16)
    mine[0, :reqs] = resid
    mine[1] = gain
    blocks = (out_refs[0].shape[0] - 2) // 3
    for flip, out_ref in enumerate(out_refs, 1):
        start = (me ^ flip) * blocks * LANES
        for b in range(blocks):
            cols = pl.ds(pl.multiple_of(start + b * LANES, LANES), LANES)
            out_ref[b] = gate_ref[:, cols]
            out_ref[blocks + b] = up_ref[:, cols]
            out_ref[2 * blocks + b] = down_ref[cols, :]
        out_ref[3 * blocks, :reqs] = resid
        out_ref[3 * blocks + 1] = gain


def attend_body(meta_ref, q_ref, k_ref, v_ref, out_ref, top_ref, sum_ref, acc_ref):
    slots, page = k_ref.shape[0], k_ref.shape[1]
    top_ref[...] = jnp.full(top_ref.shape, NEG, F32)
    sum_ref[...] = jnp.zeros(sum_ref.shape, F32)
    acc_ref[...] = jnp.zeros(acc_ref.shape, F32)
    lane = lane_ids((GROUP, page))
    owners, scores = [], []
    for s in range(slots):
        owner, live = meta_ref[s], meta_ref[slots + s]
        home = owner // 2
        pair = q_ref[home % 2, home // 2].astype(F32)
        q = jnp.where(owner % 2 == 1, pair[GROUP:], pair[:GROUP]).astype(BF16)
        score = lax.dot_general(q, k_ref[s], (((1,), (1,)), ((), ())), preferred_element_type=F32)
        score = jnp.where(lane < live, score * HD ** (-0.5), NEG)
        best = jnp.max(score, axis=1, keepdims=True)
        top_ref[owner] = jnp.maximum(top_ref[owner], jnp.broadcast_to(best, (GROUP, LANES)))
        owners.append(owner)
        scores.append(score)
    for s in range(slots):
        owner = owners[s]
        shift = top_ref[owner].astype(BF16).astype(F32)
        weight = jnp.exp(scores[s] - shift)
        total = jnp.sum(weight, axis=1, keepdims=True)
        sum_ref[owner] = sum_ref[owner] + jnp.broadcast_to(total, (GROUP, LANES))
        acc_ref[owner] = acc_ref[owner] + jnp.dot(
            weight.astype(BF16), v_ref[s], preferred_element_type=F32
        )
    lane = lane_ids((GROUP, LANES))
    for d in range(out_ref.shape[0]):
        stats = jnp.zeros((GROUP, LANES), F32)
        for par in range(2):
            total = sum_ref[2 * d + par]
            high = total.astype(BF16).astype(F32)
            base = par * 64
            stats = jnp.where(lane == base, top_ref[2 * d + par], stats)
            stats = jnp.where(lane == base + 1, high, stats)
            stats = jnp.where(lane == base + 2, total - high, stats)
        block = jnp.concatenate([acc_ref[2 * d], acc_ref[2 * d + 1], stats], axis=0)
        out_ref[d] = block.astype(BF16)


def combine_body(part_ref, q_ref, fk_ref, fv_ref, out_ref):
    count = part_ref.shape[0]
    fk, fv = fk_ref[...].astype(F32), fv_ref[...].astype(F32)
    q = q_ref[...].astype(F32)
    done = []
    for par in range(2):
        base = par * 64
        mine = slice(par * GROUP, (par + 1) * GROUP)
        own = jnp.sum(q[mine] * fk[par : par + 1], axis=1, keepdims=True) * HD ** (-0.5)
        best = own
        for d in range(count):
            stats = part_ref[d].astype(F32)[2 * GROUP :]
            best = jnp.maximum(best, stats[:, base : base + 1])
        own_weight = jnp.exp(own - best)
        total = own_weight
        acc = own_weight.astype(BF16).astype(F32) * fv[par : par + 1]
        for d in range(count):
            block = part_ref[d].astype(F32)
            stats = block[2 * GROUP :]
            factor = jnp.exp(stats[:, base : base + 1] - best)
            total = total + factor * (stats[:, base + 1 : base + 2] + stats[:, base + 2 : base + 3])
            acc = acc + factor * block[mine]
        done.append(acc / total)
    rows = jnp.concatenate(done, axis=0).astype(BF16)
    for d in range(out_ref.shape[0]):
        out_ref[d] = rows


def project_body(att_ref, w_ref, met_ref, out_ref, rows_ref):
    core = lax.axis_index("core")
    count, per, _ = att_ref.shape
    rows_ref[...] = att_ref[...].astype(F32).reshape(count * per, HD)
    reqs = count * per // GROUP
    heads = [rows_ref[pl.ds(h, reqs, stride=GROUP), :].astype(BF16) for h in range(GROUP)]
    heads = jnp.concatenate(heads, axis=1)
    for at, ref in ((core, w_ref), (1 - core, met_ref)):
        total = jnp.dot(heads, ref[...], preferred_element_type=F32).astype(BF16)
        for g in range(out_ref.shape[0]):
            out_ref[g, at] = total


def gather_body(part_ref, out_ref):
    total = part_ref[0].astype(F32)
    for g in range(1, part_ref.shape[0]):
        total = total + part_ref[g].astype(F32)
    out_ref[...] = total.astype(BF16)


def widen_body(
    pay_ref, mine_ref, gate_ref, up_ref, met1_ref, met2_ref, met3_ref, out_ref, hidden_ref
):
    me = lax.axis_index(TEAM)
    team = 2 * pay_ref.shape[0]
    reqs = 2 * pay_ref.shape[3]
    mets = (met1_ref, met2_ref, met3_ref)
    blocks = (met1_ref.shape[0] - 2) // 3
    square = jnp.zeros((reqs, 1), F32)
    gained = []
    for flip in range(team):
        ref, at = (mine_ref, 0) if flip == 0 else (mets[flip - 1], 3 * blocks)
        owner = me ^ flip
        chip, core = owner // 2, owner % 2
        projected = jnp.concatenate([pay_ref[chip, c, core].astype(F32) for c in range(2)], axis=0)
        hidden = (ref[at, :reqs].astype(F32) + projected).astype(BF16)
        if flip == 0:
            hidden_ref[...] = hidden
        wide = hidden.astype(F32)
        square = square + jnp.sum(wide * wide, axis=1, keepdims=True)
        gained.append((wide * ref[at + 1, :reqs].astype(F32)).astype(BF16))
    gained = jnp.concatenate(gained, axis=1)
    tiles = []
    for b in range(2 * blocks):
        ref, at = (gate_ref, b) if b < blocks else (up_ref, b - blocks)
        cols = pl.ds(pl.multiple_of((me * blocks + at) * LANES, LANES), LANES)
        w = jnp.concatenate([ref[:, cols]] + [met_ref[b] for met_ref in mets], axis=0)
        x = jnp.dot(gained, w, preferred_element_type=F32)
        tiles.append(x.reshape(reqs // 8, 8, LANES))
    for i in range(blocks):
        out_ref[:, i * 16 : (i + 1) * 16, :] = jnp.concatenate(
            [tiles[2 * i], tiles[2 * i + 1]], axis=1
        ).astype(BF16)
    square = jnp.broadcast_to(square, (reqs, LANES))
    high = square.astype(BF16).astype(F32)
    lane = lane_ids(square.shape)
    square = jnp.where(lane == 0, high, jnp.where(lane == 1, square - high, 0.0))
    out_ref[:, blocks * 16 :, :] = square.reshape(reqs // 8, 8, LANES).astype(BF16)


def activate_body(width, part_ref, out_ref):
    total = part_ref[0].astype(F32)
    for d in range(1, part_ref.shape[0]):
        total = total + part_ref[d].astype(F32)
    units = (total.shape[0] - 8) // 2
    square = total[2 * units :]
    square = square[:, 0:1] + square[:, 1:2]
    inv_rms = lax.rsqrt(jnp.broadcast_to(square, (8, LANES)) / width + EPS)[None]
    gate = total[:units].reshape(units // 8, 8, LANES) * inv_rms
    up = total[units : 2 * units].reshape(units // 8, 8, LANES) * inv_rms
    active = (gate / (1.0 + jnp.exp(-gate)) * up).reshape(units, LANES).astype(BF16)
    for d in range(out_ref.shape[0]):
        out_ref[d] = active


def down_body(
    act_ref, w_ref, met1_ref, met2_ref, met3_ref, pick_ref, hidden_ref, out_ref, kept_ref
):
    me = lax.axis_index(TEAM)
    reqs = act_ref.shape[0] * 8
    blocks = act_ref.shape[1] // 8
    act = act_ref[...].astype(F32)
    act = jnp.concatenate(
        [act[:, b * 8 : b * 8 + 8].reshape(reqs, LANES).astype(BF16) for b in range(blocks)], axis=1
    )
    height = blocks * LANES
    pick = pick_ref[...]
    dims = (((0,), (0,)), ((), ()))
    for flip, ref in enumerate((w_ref, met1_ref, met2_ref, met3_ref)):
        if flip == 0:
            w = ref[pl.ds(pl.multiple_of(me * height, LANES), height), :]
        else:
            w = ref[2 * blocks : 3 * blocks].reshape(height, LANES)
        total = jnp.dot(act, w, preferred_element_type=F32).astype(BF16)
        total = lax.dot_general(pick, total, dims, preferred_element_type=F32)
        out_ref[me ^ flip] = total.astype(BF16)
    kept = lax.dot_general(pick, hidden_ref[...], dims, preferred_element_type=F32)
    kept_ref[...] = kept.astype(BF16)


def shards(
    queries,
    fresh_keys,
    fresh_values,
    key_cache,
    value_cache,
    lengths,
    block_table,
    resid,
    out_weight,
    norm_gain,
    gate_weight,
    up_weight,
    down_weight,
    row_order,
):
    ctx, ring, rest, grp = (lax.axis_size(axes) for axes in (CTX, RING, REST, GRP))
    team = lax.axis_size(TEAM)
    reqs, width = resid.shape
    slots = key_cache.shape[0]
    share = reqs // grp
    shape = jax.ShapeDtypeStruct
    blocks = gate_weight.shape[1] // (team * LANES)

    def passed(blocks_out):
        return [
            lax.ppermute(block, TEAM, [(i, i ^ flip) for i in range(team)])
            for flip, block in enumerate(blocks_out, 1)
        ]

    bundle = shape((3 * blocks + 2, LANES, LANES), BF16)
    mine, *given = call(
        functools.partial(cut_body, ring),
        (shape((2, LANES, LANES), BF16),) + (bundle,) * 3,
        [VMEM] * 5,
    )(gate_weight, up_weight, down_weight, resid, norm_gain.reshape(1, width))
    met = passed(given)
    met_out = lax.ppermute(out_weight, "core", [(0, 1), (1, 0)])
    meta, pick = call(
        functools.partial(prepare_body, ring),
        (shape((2 * slots,), jnp.int32), shape((reqs, reqs), BF16)),
        [SMEM] + [VMEM] * 2,
        out_specs=(SMEM, VMEM),
    )(lengths, block_table, row_order.reshape(1, reqs))

    my_queries = queries.reshape(2 * GROUP, HD)
    all_queries = exchange(jnp.broadcast_to(my_queries[None], (ring, 2 * GROUP, HD)), RING)
    all_queries = lax.all_gather(all_queries, "core", axis=0, tiled=False)
    scratch = [pltpu.VMEM((reqs, GROUP, LANES), F32)] * 3
    parts = call(attend_body, shape((ctx, 3 * GROUP, HD), BF16), [SMEM] + [VMEM] * 3, scratch)(
        meta, all_queries, key_cache, value_cache
    )
    parts = exchange(parts, CTX)
    parts, mine = lax.optimization_barrier((parts, mine))
    local = call(combine_body, shape((ring, 2 * GROUP, HD), BF16), [VMEM] * 4)(
        parts, my_queries, fresh_keys, fresh_values
    )
    attended = exchange(local, RING)
    projected = call(
        project_body,
        shape((grp, 2, reqs // 2, width), BF16),
        [VMEM] * 3,
        [pltpu.VMEM((ring * 2 * GROUP, HD), F32)],
    )(attended, out_weight, met_out)
    projected = exchange(projected.reshape(grp, reqs, width), GRP)
    pay = call(gather_body, shape((reqs, width), BF16), [VMEM])(projected)
    pay = lax.all_gather(pay, TEAM, axis=0, tiled=False)
    units = blocks * 8
    wide, hidden = call(
        widen_body,
        (shape((rest, 2 * units + 8, LANES), BF16), shape((reqs, width), BF16)),
        [VMEM] * 7,
    )(pay.reshape(team // 2, 2, 2, reqs // 2, width), mine, gate_weight, up_weight, *met)
    wide = exchange(wide, REST)
    active = call(
        functools.partial(activate_body, width * ctx), shape((rest, units, LANES), BF16), [VMEM]
    )(wide)
    active = exchange(active, REST)
    rows, kept = call(
        down_body,
        (shape((team, reqs, width), BF16), shape((reqs, width), BF16)),
        [VMEM] * 7,
    )(active, down_weight, *met, pick, hidden)
    rows = exchange(rows.reshape(team * grp, share, width), LAST)
    kept = lax.dynamic_index_in_dim(kept.reshape(grp, share, width), lax.axis_index(GRP), 0, False)
    return (kept.astype(F32) + jnp.sum(rows.astype(F32), axis=0)).astype(BF16)


def solution(mesh, sizes=(4, 2, 4, 2, 2, 4)):
    inner = Mesh(mesh.devices.reshape(sizes), ("yh", "yl", "zl", "core", "zh", "x"))
    in_specs = (
        P(CTX, GRP),
        P(CTX, GRP),
        P(CTX, GRP),
        P(CTX, None, GRP),
        P(CTX, None, GRP),
        P(),
        P(),
        P(None, CTX),
        P(GRP, CTX),
        P(CTX),
        P(CTX, GRP),
        P(CTX, GRP),
        P(GRP, CTX),
        P(),
    )
    out_specs = P(GRP, CTX)
    return jax.shard_map(shards, mesh=inner, in_specs=in_specs, out_specs=out_specs, check_vma=False)
```

time: 168 us -> 172 us (1.024)
  waiting for transfers between devices: 33 us -> 27.4 us
  starting transfers between devices: 41.4 us -> 46 us
  local copies, waits for them, and re-layouts: 5.41 us -> 8.67 us
  Pallas kernels: 10.4 us -> 12.4 us
    all_to_all x4, starting transfers between devices: 30.3 us -> 35.4 us  [exchange(): return lax.all_to_all(x, axes, 0, 0, tiled=True)]
    all_to_all x4, waiting for transfers between devices: 31.6 us -> 27.4 us  [exchange(): return lax.all_to_all(x, axes, 0, 0, tiled=True)]
    unnamed x26 -> x38, local copies, waits for them, and re-layouts: 3.97 us -> 7.23 us
    all_gather x1 -> x0, blocking collectives: 2.76 us -> none  [shards(): lax.all_gather(exchange(local, RING), 'core', axis=0, tiled=False)]
    all_gather x1, blocking collectives: 8.53 us -> 10.7 us  [shards(): pay = lax.all_gather(pay, TEAM, axis=0, tiled=False)]
    pallas_call x8 -> x7, Pallas kernels: 7.11 us -> 8.46 us  [the longest x1 2.92 us: shards(): call(down_body, (shape((team, reqs, width), BF16), shape((reqs, width), B...]
  transfers between devices with their start and end apart: 8 -> 8, of which waited for: 5 -> 4; matrix products, arithmetic and copies ran while one was open for 0% -> 0% of each run, Pallas kernels for 2% -> 3%
where the time goes in v5:
time: 172 us; the launch traced here: 171 us
  blocking collectives  76.2 us (44%)
  starting transfers between devices  46 us (27%)
  waiting for transfers between devices  27.4 us (16%)
  Pallas kernels  12.4 us (7%)
  local copies, waits for them, and re-layouts  8.67 us (5%)
    all_to_all x3, blocking collectives, exchange(): return lax.all_to_all(x, axes, 0, 0, tiled=True)  61.7 us
    all_to_all x4, starting transfers between devices, exchange(): return lax.all_to_all(x, axes, 0, 0, tiled=True)  35.4 us
    all_to_all x4, waiting for transfers between devices, exchange(): return lax.all_to_all(x, axes, 0, 0, tiled=True)  27.4 us
    all_gather x1, blocking collectives, shards(): pay = lax.all_gather(pay, TEAM, axis=0, tiled=False)  10.7 us
    ppermute x3, starting transfers between devices, passed(): lax.ppermute(block, TEAM, [(i, i ^ flip) for i in range(team)])  8.16 us
    unnamed x38, local copies, waits for them, and re-layouts  7.23 us
    all_gather x1, blocking collectives, shards(): all_queries = lax.all_gather(all_queries, 'core', axis=0, tiled=False)  3.68 us
  transfers between devices with their start and end apart: 8, of which 4 were waited for; matrix products, arithmetic and copies ran while one was open for 0% of the time, Pallas kernels for 3%

profile of v5, /device:TPU:1, one launch (start us, length us, event | category | flops | bytes accessed | tf_op | source)
XLA Modules:
  0.0 171.5 jit_solution(3887015917933044404)
XLA Ops:
  0.0 0.8 broadcast_in_dim.7.q_ref
  0.8 0.7 broadcast_in_dim.8
  1.4 13.5 %all-to-all-start = ((bf16[32,16,128]{2,1,0:T(8,128)(2,1)}), bf16[32,16,128]{2,1,0:T(8,128)(2,1)S(1)}, u32[]{:S(2)}, u32[]{:S(2)}) async-start(bf16[32,16,128]{2,1,0:T(8,128)(2,1)} %broadcast_in_dim.8), calls=%async_computation | async-start | bytes 262144 | tf_op jit(solution)/shard_map/all_to_all | solution.py:30
  14.9 0.8 copy-done.7
  15.8 0.7 copy-done.11
  16.4 0.7 copy-done.12
  17.1 1.6 shard_map.136
  19.3 5.5 %all-to-all-done = bf16[32,16,128]{2,1,0:T(8,128)(2,1)S(1)} async-done(((bf16[32,16,128]{2,1,0:T(8,128)(2,1)}), bf16[32,16,128]{2,1,0:T(8,128)(2,1)S(1)}, u32[]{:S(2)}, u32[]{:S(2)}) %all-to-all-start) | async-done | bytes 131104 | tf_op jit(solution)/shard_map/all_to_all | solution.py:30
  24.9 3.7 %all-gather = bf16[64,16,128]{2,1,0:T(8,128)(2,1)S(1)} all-gather(bf16[32,16,128]{2,1,0:T(8,128)(2,1)S(1)} %all-to-all-done), channel_id=2, replica_groups=mesh['yh'=4,'yl'=2,'zl'=4,'core'=2,'zh'=2,'x'=4] {'core'}, dimensions={0}, use_global_device_ids=true | all-gather | bytes 393216 | tf_op jit(solution)/shard_map/all_gather | solution.py:307
  28.5 1.1 copy-done.4
  29.7 2.3 %shard_map.137 = bf16[64,24,128]{2,1,0:T(8,128)(2,1)} custom-call(s32[48]{0:T(128)S(1)} %get-tuple-element.17.meta_ref, bf16[2,32,16,128]{3,2,1,0:T(8,128)(2,1)S(1)} %bitcast.10, bf16[24,128,128]{2,1,0:T(8,128)(2,1)S(1)} %copy-done.3, bf16[24,128,128]{2,1,0:T(8,128)(2,1)S(1)} %copy-done.4), custom_call_target="tpu_custom_call" | custom-call | tf_op jit(solution)/shard_map/pallas_call | solution.py:309
  32.0 4.6 %all-to-all-start.1 = ((bf16[64,24,128]{2,1,0:T(8,128)(2,1)}), bf16[64,24,128]{2,1,0:T(8,128)(2,1)S(1)}, u32[]{:S(2)}, u32[]{:S(2)}) async-start(bf16[64,24,128]{2,1,0:T(8,128)(2,1)} %shard_map.137), calls=%async_computation.1 | async-start | bytes 786432 | tf_op jit(solution)/shard_map/all_to_all | solution.py:30
  36.5 2.5 %collective-permute-start = (bf16[1024,128]{1,0:T(8,128)(2,1)}, bf16[1024,128]{1,0:T(8,128)(2,1)}, u32[]{:S(2)}, u32[]{:S(2)}) collective-permute-start(bf16[1024,128]{1,0:T(8,128)(2,1)} %w_ref.2), channel_id=1, source_target_pairs={{0,8},{8,0},{1,9},{9,1},{2,10},{10,2},{3,11},{11,3},{4,12},{12,4},... | collective-permute-start | bytes 786440 | tf_op jit(solution)/shard_map/ppermute | solution.py:297
  40.0 0.9 copy-done.16
  40.9 0.9 copy-done.17
  41.8 0.9 copy-done.18
  42.7 9.0 %all-to-all-done.1.part_ref = bf16[64,24,128]{2,1,0:T(8,128)(2,1)S(1)} async-done(((bf16[64,24,128]{2,1,0:T(8,128)(2,1)}), bf16[64,24,128]{2,1,0:T(8,128)(2,1)S(1)}, u32[]{:S(2)}, u32[]{:S(2)}) %all-to-all-start.1) | async-done | bytes 393248 | tf_op jit(solution)/shard_map/all_to_all | solution.py:30
  51.7 1.6 shard_map.139
  53.3 4.6 %all-to-all-start.2 = ((bf16[32,16,128]{2,1,0:T(8,128)(2,1)}), bf16[32,16,128]{2,1,0:T(8,128)(2,1)}, u32[]{:S(2)}, u32[]{:S(2)}) async-start(bf16[32,16,128]{2,1,0:T(8,128)(2,1)} %shard_map.139), calls=%async_computation.2 | async-start | bytes 262144 | tf_op jit(solution)/shard_map/all_to_all | solution.py:30
  57.9 2.7 %collective-permute-start.1 = (bf16[23,128,128]{2,1,0:T(8,128)(2,1)}, bf16[23,128,128]{2,1,0:T(8,128)(2,1)S(1)}, u32[]{:S(2)}, u32[]{:S(2)}) collective-permute-start(bf16[23,128,128]{2,1,0:T(8,128)(2,1)} %copy-done.18), channel_id=1, source_target_pairs={{0,8},{8,0},{64,72},{72,64},{1,9},{9,1},{65,73},{73,65},{2,10},{10... | collective-permute-start | bytes 2261000 | tf_op jit(solution)/shard_map/ppermute | solution.py:286
  60.7 3.3 %collective-permute-start.2 = (bf16[23,128,128]{2,1,0:T(8,128)(2,1)}, bf16[23,128,128]{2,1,0:T(8,128)(2,1)}, u32[]{:S(2)}, u32[]{:S(2)}) collective-permute-start(bf16[23,128,128]{2,1,0:T(8,128)(2,1)} %copy-done.17), channel_id=1, source_target_pairs={{0,64},{8,72},{64,0},{72,8},{1,65},{9,73},{65,1},{73,9},{2,66},{10... | collective-permute-start | bytes 2261000 | tf_op jit(solution)/shard_map/ppermute | solution.py:286
  64.0 2.1 %collective-permute-start.3 = (bf16[23,128,128]{2,1,0:T(8,128)(2,1)}, bf16[23,128,128]{2,1,0:T(8,128)(2,1)}, u32[]{:S(2)}, u32[]{:S(2)}) collective-permute-start(bf16[23,128,128]{2,1,0:T(8,128)(2,1)} %copy-done.16), channel_id=1, source_target_pairs={{0,72},{8,64},{64,8},{72,0},{1,73},{9,65},{65,9},{73,1},{2,74},{10... | collective-permute-start | bytes 2261000 | tf_op jit(solution)/shard_map/ppermute | solution.py:286
  66.1 1.7 all-to-all-done.2.att_ref
  67.9 1.3 shard_map.140
  69.2 19.5 %all_to_all.35.part_ref = bf16[8,128,128]{2,1,0:T(8,128)(2,1)S(1)} all-to-all(bf16[8,128,128]{2,1,0:T(8,128)(2,1)S(1)} %bitcast.11), channel_id=1, replica_groups=mesh['yh'=4,'yl'=2,'zl'=4,'core'=2,'zh'=2,'x'=4] {'zh','x'}, dimensions={0} | all-to-all | bytes 524288 | tf_op jit(solution)/shard_map/all_to_all | solution.py:30
  88.8 10.7 %all-gather.1 = bf16[512,128]{1,0:T(8,128)(2,1)S(1)} all-gather(bf16[128,128]{1,0:T(8,128)(2,1)S(1)} %shard_map.141), channel_id=3, replica_groups=mesh['yh'=4,'yl'=2,'zl'=4,'core'=2,'zh'=2,'x'=4] {'yl','core'}, dimensions={0}, use_global_device_ids=true | all-gather | bytes 163840 | tf_op jit(solution)/shard_map/all_gather | solution.py:326
  99.6 2.0 %shard_map.142 = (bf16[16,120,128]{2,1,0:T(8,128)(2,1)S(1)}, bf16[128,128]{1,0:T(8,128)(2,1)S(1)}) custom-call(bf16[2,2,2,64,128]{4,3,2,1,0:T(8,128)(2,1)S(1)} %bitcast.12, bf16[2,128,128]{2,1,0:T(8,128)(2,1)S(1)} %copy-done.6, bf16[128,3584]{1,0:T(8,128)(2,1)S(1)} %copy-done, bf16[128,3584]{1,0:T(8,128)(2,1)S(1)} %copy-done.1, ...), custom_call_target="tpu_custom_call" | custom-call | tf_op jit(solution)/shard_map/pallas_call | solution.py:328
  101.6 25.9 %all_to_all.36.part_ref = bf16[16,120,128]{2,1,0:T(8,128)(2,1)S(1)} all-to-all(bf16[16,120,128]{2,1,0:T(8,128)(2,1)S(1)} %get-tuple-element.24), channel_id=1, replica_groups=mesh['yh'=4,'yl'=2,'zl'=4,'core'=2,'zh'=2,'x'=4] {'yh','zl'}, dimensions={0} | all-to-all | bytes 983040 | tf_op jit(solution)/shard_map/all_to_all | solution.py:30
  127.7 16.3 %all_to_all.37.act_ref = bf16[16,56,128]{2,1,0:T(8,128)(2,1)S(1)} all-to-all(bf16[16,56,128]{2,1,0:T(8,128)(2,1)S(1)} %shard_map.143), channel_id=1, replica_groups=mesh['yh'=4,'yl'=2,'zl'=4,'core'=2,'zh'=2,'x'=4] {'yh','zl'}, dimensions={0} | all-to-all | bytes 458752 | tf_op jit(solution)/shard_map/all_to_all | solution.py:30
  144.0 2.9 %shard_map.144 = (bf16[4,128,128]{2,1,0:T(8,128)(2,1)}, bf16[128,128]{1,0:T(8,128)(2,1)S(1)}) custom-call(bf16[16,56,128]{2,1,0:T(8,128)(2,1)S(1)} %all_to_all.37.act_ref, bf16[3584,128]{1,0:T(8,128)(2,1)S(1)} %copy-done.2, bf16[23,128,128]{2,1,0:T(8,128)(2,1)S(1)} %collective-permute-done.1.met1_ref, bf16[23,128,128]{2,1,0:T(8,128)(2,1)} %collective-permute-done.2.met2_ref, ...), custom_call_target="tpu_custom_call" | custom-call | tf_op jit(solution)/shard_map/pallas_call | solution.py:338
  146.9 12.8 %all-to-all-start.6 = ((bf16[32,16,128]{2,1,0:T(8,128)(2,1)}), bf16[32,16,128]{2,1,0:T(8,128)(2,1)S(1)}, u32[]{:S(2)}, u32[]{:S(2)}) async-start(bf16[32,16,128]{2,1,0:T(8,128)(2,1)} %bitcast.7), calls=%async_computation.6 | async-start | bytes 262144 | tf_op jit(solution)/shard_map/all_to_all | solution.py:30
  159.7 11.2 %all-to-all-done.6 = bf16[32,16,128]{2,1,0:T(8,128)(2,1)S(1)} async-done(((bf16[32,16,128]{2,1,0:T(8,128)(2,1)}), bf16[32,16,128]{2,1,0:T(8,128)(2,1)S(1)}, u32[]{:S(2)}, u32[]{:S(2)}) %all-to-all-start.6) | async-done | bytes 131104 | tf_op jit(solution)/shard_map/all_to_all | solution.py:30
  (40 shorter events, 2.5 us)
Async XLA Ops:
  0.0 28.5 %copy-start.3 = (bf16[24,128,128]{2,1,0:T(8,128)(2,1)S(1)}, bf16[24,128,128]{2,1,0:T(8,128)(2,1)}, u32[]{:S(2)}) copy-start(bf16[24,128,128]{2,1,0:T(8,128)(2,1)} %k_ref.1) | copy-start | bytes 2359300
  1.4 23.4 %all-to-all-start = ((bf16[32,16,128]{2,1,0:T(8,128)(2,1)}), bf16[32,16,128]{2,1,0:T(8,128)(2,1)S(1)}, u32[]{:S(2)}, u32[]{:S(2)}) async-start(bf16[32,16,128]{2,1,0:T(8,128)(2,1)} %broadcast_in_dim.8), calls=%async_computation | async-start | bytes 262144 | tf_op jit(solution)/shard_map/all_to_all | solution.py:30
  14.9 0.8 copy-start.7
  15.8 0.7 copy-start.11
  16.4 0.7 copy-start.12
  18.7 0.6 copy-start.9
  28.5 1.1 copy-start.4
  29.7 9.4 %copy-start = (bf16[128,3584]{1,0:T(8,128)(2,1)S(1)}, bf16[128,3584]{1,0:T(8,128)(2,1)}, u32[]{:S(2)}) copy-start(bf16[128,3584]{1,0:T(8,128)(2,1)} %gate_ref.3) | copy-start | bytes 2752516
  29.7 9.4 %copy-start.1 = (bf16[128,3584]{1,0:T(8,128)(2,1)S(1)}, bf16[128,3584]{1,0:T(8,128)(2,1)}, u32[]{:S(2)}) copy-start(bf16[128,3584]{1,0:T(8,128)(2,1)} %up_ref.3) | copy-start | bytes 2752516
  29.7 9.4 %copy-start.2 = (bf16[3584,128]{1,0:T(8,128)(2,1)S(1)}, bf16[3584,128]{1,0:T(8,128)(2,1)}, u32[]{:S(2)}) copy-start(bf16[3584,128]{1,0:T(8,128)(2,1)} %w_ref.3) | copy-start | bytes 2752516
  32.0 7.1 %copy-start.8 = (bf16[128,128]{1,0:T(8,128)(2,1)S(1)}, bf16[128,128]{1,0:T(8,128)(2,1)}, u32[]{:S(2)}) copy-start(bf16[128,128]{1,0:T(8,128)(2,1)} %resid_ref.1) | copy-start | bytes 98308
  32.0 19.7 %all-to-all-start.1 = ((bf16[64,24,128]{2,1,0:T(8,128)(2,1)}), bf16[64,24,128]{2,1,0:T(8,128)(2,1)S(1)}, u32[]{:S(2)}, u32[]{:S(2)}) async-start(bf16[64,24,128]{2,1,0:T(8,128)(2,1)} %shard_map.137), calls=%async_computation.1 | async-start | bytes 786432 | tf_op jit(solution)/shard_map/all_to_all | solution.py:30
  36.5 2.5 %copy-start.13 = (bf16[128]{0:T(256)(128)(2,1)S(1)}, bf16[128]{0:T(256)(128)(2,1)}, u32[]{:S(2)}) copy-start(bf16[128]{0:T(256)(128)(2,1)} %param.23) | copy-start | bytes 772
  36.5 29.6 %collective-permute-start = (bf16[1024,128]{1,0:T(8,128)(2,1)}, bf16[1024,128]{1,0:T(8,128)(2,1)}, u32[]{:S(2)}, u32[]{:S(2)}) collective-permute-start(bf16[1024,128]{1,0:T(8,128)(2,1)} %w_ref.2), channel_id=1, source_target_pairs={{0,8},{8,0},{1,9},{9,1},{2,10},{10,2},{3,11},{11,3},{4,12},{12,4},... | collective-permute-start | bytes 786440 | tf_op jit(solution)/shard_map/ppermute | solution.py:297
  39.4 0.6 copy-start.5
  40.0 0.9 copy-start.16
  40.9 0.9 copy-start.17
  41.8 0.9 copy-start.18
  42.7 9.0 %copy-start.14 = (bf16[2,128]{1,0:T(2,128)(2,1)S(1)}, bf16[2,128]{1,0:T(2,128)(2,1)}, u32[]{:S(2)}) copy-start(bf16[2,128]{1,0:T(2,128)(2,1)} %fk_ref.1) | copy-start | bytes 1540
  42.7 9.0 %copy-start.15 = (bf16[2,128]{1,0:T(2,128)(2,1)S(1)}, bf16[2,128]{1,0:T(2,128)(2,1)}, u32[]{:S(2)}) copy-start(bf16[2,128]{1,0:T(2,128)(2,1)} %fv_ref.1) | copy-start | bytes 1540
  53.3 14.5 %all-to-all-start.2 = ((bf16[32,16,128]{2,1,0:T(8,128)(2,1)}), bf16[32,16,128]{2,1,0:T(8,128)(2,1)}, u32[]{:S(2)}, u32[]{:S(2)}) async-start(bf16[32,16,128]{2,1,0:T(8,128)(2,1)} %shard_map.139), calls=%async_computation.2 | async-start | bytes 262144 | tf_op jit(solution)/shard_map/all_to_all | solution.py:30
  57.9 41.6 %collective-permute-start.1 = (bf16[23,128,128]{2,1,0:T(8,128)(2,1)}, bf16[23,128,128]{2,1,0:T(8,128)(2,1)S(1)}, u32[]{:S(2)}, u32[]{:S(2)}) collective-permute-start(bf16[23,128,128]{2,1,0:T(8,128)(2,1)} %copy-done.18), channel_id=1, source_target_pairs={{0,8},{8,0},{64,72},{72,64},{1,9},{9,1},{65,73},{73,65},{2,10},{10... | collective-permute-start | bytes 2261000 | tf_op jit(solution)/shard_map/ppermute | solution.py:286
  60.7 38.9 %collective-permute-start.2 = (bf16[23,128,128]{2,1,0:T(8,128)(2,1)}, bf16[23,128,128]{2,1,0:T(8,128)(2,1)}, u32[]{:S(2)}, u32[]{:S(2)}) collective-permute-start(bf16[23,128,128]{2,1,0:T(8,128)(2,1)} %copy-done.17), channel_id=1, source_target_pairs={{0,64},{8,72},{64,0},{72,8},{1,65},{9,73},{65,1},{73,9},{2,66},{10... | collective-permute-start | bytes 2261000 | tf_op jit(solution)/shard_map/ppermute | solution.py:286
  64.0 35.5 %collective-permute-start.3 = (bf16[23,128,128]{2,1,0:T(8,128)(2,1)}, bf16[23,128,128]{2,1,0:T(8,128)(2,1)}, u32[]{:S(2)}, u32[]{:S(2)}) collective-permute-start(bf16[23,128,128]{2,1,0:T(8,128)(2,1)} %copy-done.16), channel_id=1, source_target_pairs={{0,72},{8,64},{64,8},{72,0},{1,73},{9,65},{65,9},{73,1},{2,74},{10... | collective-permute-start | bytes 2261000 | tf_op jit(solution)/shard_map/ppermute | solution.py:286
  88.8 10.8 %copy-start.6 = (bf16[2,128,128]{2,1,0:T(8,128)(2,1)S(1)}, bf16[2,128,128]{2,1,0:T(8,128)(2,1)}, u32[]{:S(2)}) copy-start(bf16[2,128,128]{2,1,0:T(8,128)(2,1)} %copy-done.5) | copy-start | bytes 196612
  127.7 16.3 %copy-start.10 = (bf16[128,128]{1,0:T(8,128)(2,1)S(1)}, bf16[128,128]{1,0:T(8,128)(2,1)}, u32[]{:S(2)}) copy-start(bf16[128,128]{1,0:T(8,128)(2,1)} %copy-done.9) | copy-start | bytes 98308
  146.9 23.9 %all-to-all-start.6 = ((bf16[32,16,128]{2,1,0:T(8,128)(2,1)}), bf16[32,16,128]{2,1,0:T(8,128)(2,1)S(1)}, u32[]{:S(2)}, u32[]{:S(2)}) async-start(bf16[32,16,128]{2,1,0:T(8,128)(2,1)} %bitcast.7), calls=%async_computation.6 | async-start | bytes 262144 | tf_op jit(solution)/shard_map/all_to_all | solution.py:30

commit v6 on v5

--- a/solution.py
+++ b/solution.py
@@ -19,11 +19,12 @@
 REST = ("yh", "zl")
 TEAM = ("yl", "core")
 GRP = ("zh", "x")
-LAST = TEAM + GRP
+LAST = ("core",) + GRP
 F32 = jnp.float32
 BF16 = jnp.bfloat16
 VMEM = pl.BlockSpec(memory_space=pltpu.VMEM)
 SMEM = pl.BlockSpec(memory_space=pltpu.SMEM)
+HBM = pl.BlockSpec(memory_space=pltpu.HBM)
 
 
 def exchange(x, axes):
@@ -35,7 +36,7 @@
 
 
 def call(body, out_shape, in_specs, scratch=(), out_specs=None):
-    return pl.pallas_call(
+    kernel = pl.pallas_call(
         body,
         out_shape=out_shape,
         in_specs=in_specs,
@@ -44,13 +45,41 @@
         compiler_params=pltpu.CompilerParams(vmem_limit_bytes=VMEM_LIMIT),
     )
 
+    def run(*operands):
+        placed = [
+            pltpu.with_memory_space_constraint(x, pltpu.HBM) if spec is HBM else x
+            for x, spec in zip(operands, in_specs, strict=True)
+        ]
+        return kernel(*placed)
+
+    return run
+
 
 def request_of(place, ring):
     core, at = place >> ring.bit_length(), place & (2 * ring - 1)
     return (at >> 1) * 4 + core * 2 + (at & 1)
 
 
-def prepare_body(ring, len_ref, table_ref, order_ref, meta_ref, pick_ref):
+def pack_body(q_ref, out_ref, mine_ref):
+    wide = q_ref[...].astype(F32)
+    rows = [
+        wide[r : r + 1, h * HD : (h + 1) * HD] for r in range(wide.shape[0]) for h in range(GROUP)
+    ]
+    rows = jnp.concatenate(rows, axis=0).astype(BF16)
+    mine_ref[...] = rows
+    for d in range(out_ref.shape[0]):
+        out_ref[d] = rows
+
+
+def prepare_body(
+    ring, len_hbm, table_hbm, order_hbm, meta_ref, pick_ref, len_ref, table_ref, order_ref, sems
+):
+    pairs = ((table_hbm, table_ref), (len_hbm, len_ref), (order_hbm, order_ref))
+    copies = [pltpu.make_async_copy(a, b, sems.at[i]) for i, (a, b) in enumerate(pairs)]
+    for copy in copies:
+        copy.start()
+    for copy in copies:
+        copy.wait()
     slots = meta_ref.shape[0] // 2
     first = lax.axis_index(CTX) * slots
     table = table_ref[...] - first
@@ -66,9 +95,8 @@
     pick_ref[...] = pick.astype(F32).astype(BF16)
 
 
-def cut_body(ring, gate_ref, up_ref, down_ref, resid_ref, gain_ref, *out_refs):
+def cut_body(ring, gate_ref, up_ref, down_ref, w_ref, resid_ref, gain_ref, mine, core_ref, *out_refs):
     me = lax.axis_index(TEAM)
-    mine, out_refs = out_refs[0], out_refs[1:]
     reqs = resid_ref.shape[0]
     place = lax.broadcasted_iota(jnp.int32, (reqs, reqs), 0)
     turn = (request_of(place, ring) == lane_ids((reqs, reqs))).astype(F32).astype(BF16)
@@ -76,20 +104,28 @@
     gain = jnp.broadcast_to(gain_ref[...].astype(F32), (LANES, LANES)).astype(BF16)
     mine[0, :reqs] = resid
     mine[1] = gain
-    blocks = (out_refs[0].shape[0] - 2) // 3
+    blocks = (out_refs[0].shape[0] - 2) // 2
+    heads = w_ref.shape[0] // LANES
+    core_ref[:heads] = w_ref[...].reshape(heads, LANES, LANES)
+    other = 1 - lax.axis_index("core")
+    for z in range(2):
+        start = pl.multiple_of((2 * z + other) * blocks * LANES, LANES)
+        rows = down_ref[pl.ds(start, blocks * LANES), :]
+        core_ref[heads + z * blocks : heads + (z + 1) * blocks] = rows.reshape(blocks, LANES, LANES)
     for flip, out_ref in enumerate(out_refs, 1):
         start = (me ^ flip) * blocks * LANES
         for b in range(blocks):
             cols = pl.ds(pl.multiple_of(start + b * LANES, LANES), LANES)
             out_ref[b] = gate_ref[:, cols]
             out_ref[blocks + b] = up_ref[:, cols]
-            out_ref[2 * blocks + b] = down_ref[cols, :]
-        out_ref[3 * blocks, :reqs] = resid
-        out_ref[3 * blocks + 1] = gain
-
-
-def attend_body(meta_ref, q_ref, k_ref, v_ref, out_ref, top_ref, sum_ref, acc_ref):
+        out_ref[2 * blocks, :reqs] = resid
+        out_ref[2 * blocks + 1] = gain
+
+
+def attend_body(meta_ref, q_ref, k_ref, v_hbm, out_ref, top_ref, sum_ref, acc_ref, v_ref, sem):
     slots, page = k_ref.shape[0], k_ref.shape[1]
+    fetch = pltpu.make_async_copy(v_hbm, v_ref, sem)
+    fetch.start()
     top_ref[...] = jnp.full(top_ref.shape, NEG, F32)
     sum_ref[...] = jnp.zeros(sum_ref.shape, F32)
     acc_ref[...] = jnp.zeros(acc_ref.shape, F32)
@@ -106,6 +142,7 @@
         top_ref[owner] = jnp.maximum(top_ref[owner], jnp.broadcast_to(best, (GROUP, LANES)))
         owners.append(owner)
         scores.append(score)
+    fetch.wait()
     for s in range(slots):
         owner = owners[s]
         shift = top_ref[owner].astype(BF16).astype(F32)
@@ -165,7 +202,8 @@
     heads = [rows_ref[pl.ds(h, reqs, stride=GROUP), :].astype(BF16) for h in range(GROUP)]
     heads = jnp.concatenate(heads, axis=1)
     for at, ref in ((core, w_ref), (1 - core, met_ref)):
-        total = jnp.dot(heads, ref[...], preferred_element_type=F32).astype(BF16)
+        w = ref[...] if ref is w_ref else ref[:GROUP].reshape(GROUP * HD, LANES)
+        total = jnp.dot(heads, w, preferred_element_type=F32).astype(BF16)
         for g in range(out_ref.shape[0]):
             out_ref[g, at] = total
 
@@ -184,11 +222,11 @@
     team = 2 * pay_ref.shape[0]
     reqs = 2 * pay_ref.shape[3]
     mets = (met1_ref, met2_ref, met3_ref)
-    blocks = (met1_ref.shape[0] - 2) // 3
+    blocks = (met1_ref.shape[0] - 2) // 2
     square = jnp.zeros((reqs, 1), F32)
     gained = []
     for flip in range(team):
-        ref, at = (mine_ref, 0) if flip == 0 else (mets[flip - 1], 3 * blocks)
+        ref, at = (mine_ref, 0) if flip == 0 else (mets[flip - 1], 2 * blocks)
         owner = me ^ flip
         chip, core = owner // 2, owner % 2
         projected = jnp.concatenate([pay_ref[chip, c, core].astype(F32) for c in range(2)], axis=0)
@@ -232,29 +270,34 @@
         out_ref[d] = active
 
 
-def down_body(
-    act_ref, w_ref, met1_ref, met2_ref, met3_ref, pick_ref, hidden_ref, out_ref, kept_ref
-):
-    me = lax.axis_index(TEAM)
-    reqs = act_ref.shape[0] * 8
-    blocks = act_ref.shape[1] // 8
-    act = act_ref[...].astype(F32)
-    act = jnp.concatenate(
-        [act[:, b * 8 : b * 8 + 8].reshape(reqs, LANES).astype(BF16) for b in range(blocks)], axis=1
-    )
+def down_body(act_ref, w_ref, met_ref, pick_ref, hidden_ref, out_ref, kept_ref):
+    core = lax.axis_index("core")
+    reqs = act_ref.shape[0] * act_ref.shape[2] * 8
+    blocks = act_ref.shape[3] // 8
     height = blocks * LANES
+    acts, own = [], []
+    for z in range(2):
+        act = act_ref[:, z].astype(F32).reshape(reqs // 8, blocks * 8, LANES)
+        for b in range(blocks):
+            acts.append(act[:, b * 8 : b * 8 + 8].reshape(reqs, LANES).astype(BF16))
+        own.append(w_ref[pl.ds(pl.multiple_of((2 * z + core) * height, LANES), height), :])
+    acts = jnp.concatenate(acts, axis=1)
+    met = met_ref[GROUP:].reshape(2 * height, LANES)
     pick = pick_ref[...]
     dims = (((0,), (0,)), ((), ()))
-    for flip, ref in enumerate((w_ref, met1_ref, met2_ref, met3_ref)):
-        if flip == 0:
-            w = ref[pl.ds(pl.multiple_of(me * height, LANES), height), :]
-        else:
-            w = ref[2 * blocks : 3 * blocks].reshape(height, LANES)
-        total = jnp.dot(act, w, preferred_element_type=F32).astype(BF16)
+    for at, w in ((core, jnp.concatenate(own, axis=0)), (1 - core, met)):
+        total = jnp.dot(acts, w, preferred_element_type=F32).astype(BF16)
         total = lax.dot_general(pick, total, dims, preferred_element_type=F32)
-        out_ref[me ^ flip] = total.astype(BF16)
+        out_ref[at] = total.astype(BF16)
     kept = lax.dot_general(pick, hidden_ref[...], dims, preferred_element_type=F32)
     kept_ref[...] = kept.astype(BF16)
+
+
+def finish_body(part_ref, kept_ref, out_ref):
+    total = kept_ref[lax.axis_index(GRP)].astype(F32)
+    for d in range(part_ref.shape[0]):
+        total = total + part_ref[d].astype(F32)
+    out_ref[...] = total.astype(BF16)
 
 
 def shards(
@@ -287,26 +330,39 @@
             for flip, block in enumerate(blocks_out, 1)
         ]
 
-    bundle = shape((3 * blocks + 2, LANES, LANES), BF16)
-    mine, *given = call(
+    bundle = shape((2 * blocks + 2, LANES, LANES), BF16)
+    core_bundle = shape((GROUP + 2 * blocks, LANES, LANES), BF16)
+    mine, given_core, *given = call(
         functools.partial(cut_body, ring),
-        (shape((2, LANES, LANES), BF16),) + (bundle,) * 3,
-        [VMEM] * 5,
-    )(gate_weight, up_weight, down_weight, resid, norm_gain.reshape(1, width))
-    met = passed(given)
-    met_out = lax.ppermute(out_weight, "core", [(0, 1), (1, 0)])
+        (shape((2, LANES, LANES), BF16), core_bundle) + (bundle,) * 3,
+        [VMEM] * 6,
+    )(gate_weight, up_weight, down_weight, out_weight, resid, norm_gain.reshape(1, width))
+    met = [
+        lax.ppermute(block, TEAM, [(i, i ^ flip) for i in range(team)])
+        for flip, block in enumerate(given, 1)
+    ]
+    met_core = lax.ppermute(given_core, "core", [(0, 1), (1, 0)])
     meta, pick = call(
         functools.partial(prepare_body, ring),
         (shape((2 * slots,), jnp.int32), shape((reqs, reqs), BF16)),
-        [SMEM] + [VMEM] * 2,
+        [HBM] * 3,
+        [
+            pltpu.SMEM(lengths.shape, jnp.int32),
+            pltpu.VMEM(block_table.shape, jnp.int32),
+            pltpu.VMEM((1, reqs), jnp.int32),
+            pltpu.SemaphoreType.DMA((3,)),
+        ],
         out_specs=(SMEM, VMEM),
     )(lengths, block_table, row_order.reshape(1, reqs))
 
-    my_queries = queries.reshape(2 * GROUP, HD)
-    all_queries = exchange(jnp.broadcast_to(my_queries[None], (ring, 2 * GROUP, HD)), RING)
+    packed, my_queries = call(
+        pack_body, (shape((ring, 2 * GROUP, HD), BF16), shape((2 * GROUP, HD), BF16)), [VMEM]
+    )(queries)
+    all_queries = exchange(packed, RING)
     all_queries = lax.all_gather(all_queries, "core", axis=0, tiled=False)
     scratch = [pltpu.VMEM((reqs, GROUP, LANES), F32)] * 3
-    parts = call(attend_body, shape((ctx, 3 * GROUP, HD), BF16), [SMEM] + [VMEM] * 3, scratch)(
+    scratch += [pltpu.VMEM(value_cache.shape, BF16), pltpu.SemaphoreType.DMA(())]
+    parts = call(attend_body, shape((ctx, 3 * GROUP, HD), BF16), [SMEM, VMEM, VMEM, HBM], scratch)(
         meta, all_queries, key_cache, value_cache
     )
     parts = exchange(parts, CTX)
@@ -315,12 +371,13 @@
         parts, my_queries, fresh_keys, fresh_values
     )
     attended = exchange(local, RING)
+    attended, met_core, *met = lax.optimization_barrier((attended, met_core, *met))
     projected = call(
         project_body,
         shape((grp, 2, reqs // 2, width), BF16),
         [VMEM] * 3,
         [pltpu.VMEM((ring * 2 * GROUP, HD), F32)],
-    )(attended, out_weight, met_out)
+    )(attended, out_weight, met_core)
     projected = exchange(projected.reshape(grp, reqs, width), GRP)
     pay = call(gather_body, shape((reqs, width), BF16), [VMEM])(projected)
     pay = lax.all_gather(pay, TEAM, axis=0, tiled=False)
@@ -332,17 +389,19 @@
     )(pay.reshape(team // 2, 2, 2, reqs // 2, width), mine, gate_weight, up_weight, *met)
     wide = exchange(wide, REST)
     active = call(
-        functools.partial(activate_body, width * ctx), shape((rest, units, LANES), BF16), [VMEM]
+        functools.partial(activate_body, width * ctx), shape((ring, units, LANES), BF16), [VMEM]
     )(wide)
-    active = exchange(active, REST)
+    active = exchange(active, RING)
+    line = lax.axis_size("zl")
     rows, kept = call(
         down_body,
-        (shape((team, reqs, width), BF16), shape((reqs, width), BF16)),
-        [VMEM] * 7,
-    )(active, down_weight, *met, pick, hidden)
-    rows = exchange(rows.reshape(team * grp, share, width), LAST)
-    kept = lax.dynamic_index_in_dim(kept.reshape(grp, share, width), lax.axis_index(GRP), 0, False)
-    return (kept.astype(F32) + jnp.sum(rows.astype(F32), axis=0)).astype(BF16)
+        (shape((2, reqs, width), BF16), shape((reqs, width), BF16)),
+        [VMEM] * 5,
+    )(active.reshape(ring // (2 * line), 2, line, units, LANES), down_weight, met_core, pick, hidden)
+    rows = exchange(rows.reshape(2 * grp, share, width), LAST)
+    return call(finish_body, shape((share, width), BF16), [VMEM] * 2)(
+        rows, kept.reshape(grp, share, width)
+    )
 
 
 def solution(mesh, sizes=(4, 2, 4, 2, 2, 4)):

time: 172 us -> 172 us (level)
  blocking collectives: 76.2 us -> 89.4 us
  starting transfers between devices: 46 us -> 36.4 us
  local copies, waits for them, and re-layouts: 8.67 us -> 4.72 us
  Pallas kernels: 12.4 us -> 14.2 us
    all_to_all x3 -> x4, blocking collectives: 61.7 us -> 76.8 us  [exchange(): return lax.all_to_all(x, axes, 0, 0, tiled=True)]
    all_to_all x4 -> x3, waiting for transfers between devices: 27.4 us -> 17.2 us  [exchange(): return lax.all_to_all(x, axes, 0, 0, tiled=True)]
    all_to_all x4 -> x3, starting transfers between devices: 35.4 us -> 26 us  [exchange(): return lax.all_to_all(x, axes, 0, 0, tiled=True)]
    ppermute x4, waiting for transfers between devices: 0.01 us -> 9.32 us  [the longest x3 9.32 us: shards(): lax.ppermute(block, TEAM, [(i, i ^ flip) for i in range(team)])]
    unnamed x38 -> x28, local copies, waits for them, and re-layouts: 7.23 us -> 4.72 us
    all_gather x1, blocking collectives: 10.7 us -> 8.76 us  [shards(): pay = lax.all_gather(pay, TEAM, axis=0, tiled=False)]
    pallas_call x9 -> x11, Pallas kernels: 12.4 us -> 14.2 us  [run(): return kernel(*placed)]
  transfers between devices with their start and end apart: 8 -> 7, of which waited for: 4 -> 4; matrix products, arithmetic and copies ran while one was open for 0% -> 0% of each run, Pallas kernels for 3% -> 3%
where the time goes in v6:
time: 172 us
  blocking collectives  89.4 us (52%)
  starting transfers between devices  36.4 us (21%)
  waiting for transfers between devices  26.5 us (15%)
  Pallas kernels  14.2 us (8%)
  local copies, waits for them, and re-layouts  4.72 us (3%)
    all_to_all x4, blocking collectives, exchange(): return lax.all_to_all(x, axes, 0, 0, tiled=True)  76.8 us
    all_to_all x3, starting transfers between devices, exchange(): return lax.all_to_all(x, axes, 0, 0, tiled=True)  26 us
    all_to_all x3, waiting for transfers between devices, exchange(): return lax.all_to_all(x, axes, 0, 0, tiled=True)  17.2 us
    pallas_call x11, Pallas kernels, run(): return kernel(*placed)  14.2 us
    ppermute x3, waiting for transfers between devices, shards(): lax.ppermute(block, TEAM, [(i, i ^ flip) for i in range(team)])  9.32 us
    all_gather x1, blocking collectives, shards(): pay = lax.all_gather(pay, TEAM, axis=0, tiled=False)  8.76 us
    ppermute x3, starting transfers between devices, shards(): lax.ppermute(block, TEAM, [(i, i ^ flip) for i in range(team)])  7.87 us
    unnamed x28, local copies, waits for them, and re-layouts  4.72 us
  transfers between devices with their start and end apart: 7, of which 4 were waited for; matrix products, arithmetic and copies ran while one was open for 0% of the time, Pallas kernels for 3%

profile of v6, /device:TPU:1, one launch (start us, length us, event | category | flops | bytes accessed | tf_op | source)
XLA Modules:
  0.0 171.5 jit_solution(15012015421252877330)
XLA Ops:
  0.0 0.7 copy-done.10
  0.7 0.7 shard_map.137
  1.4 13.5 %all-to-all-start = ((bf16[32,16,128]{2,1,0:T(8,128)(2,1)}), bf16[32,16,128]{2,1,0:T(8,128)(2,1)S(1)}, u32[]{:S(2)}, u32[]{:S(2)}) async-start(bf16[32,16,128]{2,1,0:T(8,128)(2,1)} %get-tuple-element.26), calls=%async_computation | async-start | bytes 262144 | tf_op jit(solution)/shard_map/all_to_all | solution.py:31
  14.8 2.0 %shard_map.136 = (s32[48]{0:T(128)S(1)}, bf16[128,128]{1,0:T(8,128)(2,1)S(1)}) custom-call(s32[128]{0:T(128)} %len_hbm.1, s32[128,128]{1,0:T(8,128)} %table_hbm.1, s32[1,128]{1,0:T(1,128)} %bitcast.15), custom_call_target="tpu_custom_call" | custom-call | tf_op jit(solution)/shard_map/pallas_call | solution.py:53
  16.9 7.9 %all-to-all-done = bf16[32,16,128]{2,1,0:T(8,128)(2,1)S(1)} async-done(((bf16[32,16,128]{2,1,0:T(8,128)(2,1)}), bf16[32,16,128]{2,1,0:T(8,128)(2,1)S(1)}, u32[]{:S(2)}, u32[]{:S(2)}) %all-to-all-start) | async-done | bytes 131104 | tf_op jit(solution)/shard_map/all_to_all | solution.py:31
  24.8 3.8 %all-gather = bf16[64,16,128]{2,1,0:T(8,128)(2,1)S(1)} all-gather(bf16[32,16,128]{2,1,0:T(8,128)(2,1)S(1)} %all-to-all-done), channel_id=2, replica_groups=mesh['yh'=4,'yl'=2,'zl'=4,'core'=2,'zh'=2,'x'=4] {'core'}, dimensions={0}, use_global_device_ids=true | all-gather | bytes 393216 | tf_op jit(solution)/shard_map/all_gather | solution.py:362
  28.6 1.1 copy-done.5
  29.7 3.3 %shard_map.138 = bf16[64,24,128]{2,1,0:T(8,128)(2,1)} custom-call(s32[48]{0:T(128)S(1)} %get-tuple-element.25.meta_ref, bf16[2,32,16,128]{3,2,1,0:T(8,128)(2,1)S(1)} %bitcast.9, bf16[24,128,128]{2,1,0:T(8,128)(2,1)S(1)} %copy-done.5, bf16[24,128,128]{2,1,0:T(8,128)(2,1)} %v_hbm.1), custom_call_target="tpu_custom_call" | custom-call | tf_op jit(solution)/shard_map/pallas_call | solution.py:53
  33.0 5.3 %all-to-all-start.1 = ((bf16[64,24,128]{2,1,0:T(8,128)(2,1)}), bf16[64,24,128]{2,1,0:T(8,128)(2,1)}, u32[]{:S(2)}, u32[]{:S(2)}) async-start(bf16[64,24,128]{2,1,0:T(8,128)(2,1)} %shard_map.138), calls=%async_computation.1 | async-start | bytes 786432 | tf_op jit(solution)/shard_map/all_to_all | solution.py:31
  38.4 0.6 copy-done.11
  39.0 1.5 shard_map.139
  40.5 2.5 %collective-permute-start = (bf16[22,128,128]{2,1,0:T(8,128)(2,1)}, bf16[22,128,128]{2,1,0:T(8,128)(2,1)S(1)}, u32[]{:S(2)}, u32[]{:S(2)}) collective-permute-start(bf16[22,128,128]{2,1,0:T(8,128)(2,1)} %get-tuple-element.30), channel_id=1, source_target_pairs={{0,8},{8,0},{1,9},{9,1},{2,10},{10,2},{3,11},{11,3},{4,12},{12,4},... | collective-permute-start | bytes 2162696 | tf_op jit(solution)/shard_map/ppermute | solution.py:344
  43.1 1.9 %collective-permute-start.1 = (bf16[16,128,128]{2,1,0:T(8,128)(2,1)}, bf16[16,128,128]{2,1,0:T(8,128)(2,1)}, u32[]{:S(2)}, u32[]{:S(2)}) collective-permute-start(bf16[16,128,128]{2,1,0:T(8,128)(2,1)} %get-tuple-element.31), channel_id=1, source_target_pairs={{0,8},{8,0},{64,72},{72,64},{1,9},{9,1},{65,73},{73,65},{2,10},{10... | collective-permute-start | bytes 1572872 | tf_op jit(solution)/shard_map/ppermute | solution.py:341
  45.0 3.2 %collective-permute-start.2 = (bf16[16,128,128]{2,1,0:T(8,128)(2,1)}, bf16[16,128,128]{2,1,0:T(8,128)(2,1)}, u32[]{:S(2)}, u32[]{:S(2)}) collective-permute-start(bf16[16,128,128]{2,1,0:T(8,128)(2,1)} %get-tuple-element.32), channel_id=1, source_target_pairs={{0,64},{8,72},{64,0},{72,8},{1,65},{9,73},{65,1},{73,9},{2,66},{10... | collective-permute-start | bytes 1572872 | tf_op jit(solution)/shard_map/ppermute | solution.py:341
  48.2 2.7 %collective-permute-start.3 = (bf16[16,128,128]{2,1,0:T(8,128)(2,1)}, bf16[16,128,128]{2,1,0:T(8,128)(2,1)}, u32[]{:S(2)}, u32[]{:S(2)}) collective-permute-start(bf16[16,128,128]{2,1,0:T(8,128)(2,1)} %get-tuple-element.33), channel_id=1, source_target_pairs={{0,72},{8,64},{64,8},{72,0},{1,73},{9,65},{65,9},{73,1},{2,74},{10... | collective-permute-start | bytes 1572872 | tf_op jit(solution)/shard_map/ppermute | solution.py:341
  51.0 2.5 %all-to-all-done.1.part_ref = bf16[64,24,128]{2,1,0:T(8,128)(2,1)} async-done(((bf16[64,24,128]{2,1,0:T(8,128)(2,1)}), bf16[64,24,128]{2,1,0:T(8,128)(2,1)}, u32[]{:S(2)}, u32[]{:S(2)}) %all-to-all-start.1) | async-done | bytes 393248 | tf_op jit(solution)/shard_map/all_to_all | solution.py:31
  53.5 0.7 copy-done.12
  54.1 2.1 %shard_map.140 = bf16[32,16,128]{2,1,0:T(8,128)(2,1)S(1)} custom-call(bf16[64,24,128]{2,1,0:T(8,128)(2,1)} %all-to-all-done.1.part_ref, bf16[16,128]{1,0:T(8,128)(2,1)S(1)} %get-tuple-element.29.q_ref, bf16[2,128]{1,0:T(2,128)(2,1)S(1)} %copy-done.12, bf16[2,128]{1,0:T(2,128)(2,1)S(1)} %copy-done.13), custom_call_target="tpu_custom_call" | custom-call | tf_op jit(solution)/shard_map/pallas_call | solution.py:53
  56.2 0.6 copy-done.6
  56.9 7.3 %all-to-all-start.2 = ((bf16[32,16,128]{2,1,0:T(8,128)(2,1)}), bf16[32,16,128]{2,1,0:T(8,128)(2,1)}, u32[]{:S(2)}, u32[]{:S(2)}) async-start(bf16[32,16,128]{2,1,0:T(8,128)(2,1)} %copy-done.6), calls=%async_computation.2 | async-start | bytes 262144 | tf_op jit(solution)/shard_map/all_to_all | solution.py:31
  64.2 9.3 %collective-permute-done.3.met3_ref = bf16[16,128,128]{2,1,0:T(8,128)(2,1)} collective-permute-done((bf16[16,128,128]{2,1,0:T(8,128)(2,1)}, bf16[16,128,128]{2,1,0:T(8,128)(2,1)}, u32[]{:S(2)}, u32[]{:S(2)}) %collective-permute-start.3) | collective-permute-done | bytes 524320 | tf_op jit(solution)/shard_map/ppermute | solution.py:341
  73.5 6.8 %all-to-all-done.2.att_ref = bf16[32,16,128]{2,1,0:T(8,128)(2,1)} async-done(((bf16[32,16,128]{2,1,0:T(8,128)(2,1)}), bf16[32,16,128]{2,1,0:T(8,128)(2,1)}, u32[]{:S(2)}, u32[]{:S(2)}) %all-to-all-start.2) | async-done | bytes 131104 | tf_op jit(solution)/shard_map/all_to_all | solution.py:31
  80.2 0.9 copy-done.4
  81.2 1.1 shard_map.141
  82.3 19.5 %all_to_all.35.part_ref = bf16[8,128,128]{2,1,0:T(8,128)(2,1)S(1)} all-to-all(bf16[8,128,128]{2,1,0:T(8,128)(2,1)S(1)} %bitcast.10), channel_id=1, replica_groups=mesh['yh'=4,'yl'=2,'zl'=4,'core'=2,'zh'=2,'x'=4] {'zh','x'}, dimensions={0} | all-to-all | bytes 524288 | tf_op jit(solution)/shard_map/all_to_all | solution.py:31
  101.9 8.8 %all-gather.1 = bf16[512,128]{1,0:T(8,128)(2,1)S(1)} all-gather(bf16[128,128]{1,0:T(8,128)(2,1)S(1)} %shard_map.142), channel_id=3, replica_groups=mesh['yh'=4,'yl'=2,'zl'=4,'core'=2,'zh'=2,'x'=4] {'yl','core'}, dimensions={0}, use_global_device_ids=true | all-gather | bytes 163840 | tf_op jit(solution)/shard_map/all_gather | solution.py:383
  110.7 2.0 %shard_map.143 = (bf16[16,120,128]{2,1,0:T(8,128)(2,1)S(1)}, bf16[128,128]{1,0:T(8,128)(2,1)S(1)}) custom-call(bf16[2,2,2,64,128]{4,3,2,1,0:T(8,128)(2,1)S(1)} %bitcast.11, bf16[2,128,128]{2,1,0:T(8,128)(2,1)S(1)} %get-tuple-element.36.mine_ref, bf16[128,3584]{1,0:T(8,128)(2,1)S(1)} %copy-done, bf16[128,3584]{1,0:T(8,128)(2,1)S(1)} %copy-done.1, ...), custom_call_target="tpu_custom_call" | custom-call | tf_op jit(solution)/shard_map/pallas_call | solution.py:53
  112.7 20.5 %all_to_all.36.part_ref = bf16[16,120,128]{2,1,0:T(8,128)(2,1)S(1)} all-to-all(bf16[16,120,128]{2,1,0:T(8,128)(2,1)S(1)} %get-tuple-element.40), channel_id=1, replica_groups=mesh['yh'=4,'yl'=2,'zl'=4,'core'=2,'zh'=2,'x'=4] {'yh','zl'}, dimensions={0} | all-to-all | bytes 983040 | tf_op jit(solution)/shard_map/all_to_all | solution.py:31
  133.4 21.4 %all_to_all.37 = bf16[32,56,128]{2,1,0:T(8,128)(2,1)S(1)} all-to-all(bf16[32,56,128]{2,1,0:T(8,128)(2,1)S(1)} %shard_map.144), channel_id=1, replica_groups=mesh['yh'=4,'yl'=2,'zl'=4,'core'=2,'zh'=2,'x'=4] {'yh','yl','zl'}, dimensions={0} | all-to-all | bytes 917504 | tf_op jit(solution)/shard_map/all_to_all | solution.py:31
  154.8 0.7 shard_map.145
  155.5 15.4 %all_to_all.38.part_ref = bf16[16,16,128]{2,1,0:T(8,128)(2,1)S(1)} all-to-all(bf16[16,16,128]{2,1,0:T(8,128)(2,1)S(1)} %bitcast.12), channel_id=1, replica_groups=mesh['yh'=4,'yl'=2,'zl'=4,'core'=2,'zh'=2,'x'=4] {'core','zh','x'}, dimensions={0} | all-to-all | bytes 131072 | tf_op jit(solution)/shard_map/all_to_all | solution.py:31
  170.9 0.6 shard_map.146
  (27 shorter events, 0.3 us)
Async XLA Ops:
  0.0 0.7 copy-start.10
  1.4 23.4 %all-to-all-start = ((bf16[32,16,128]{2,1,0:T(8,128)(2,1)}), bf16[32,16,128]{2,1,0:T(8,128)(2,1)S(1)}, u32[]{:S(2)}, u32[]{:S(2)}) async-start(bf16[32,16,128]{2,1,0:T(8,128)(2,1)} %get-tuple-element.26), calls=%async_computation | async-start | bytes 262144 | tf_op jit(solution)/shard_map/all_to_all | solution.py:31
  16.8 11.8 %copy-start.8 = (bf16[128,128]{1,0:T(8,128)(2,1)}, bf16[128,128]{1,0:T(8,128)(2,1)S(1)}, u32[]{:S(2)}) copy-start(bf16[128,128]{1,0:T(8,128)(2,1)S(1)} %get-tuple-element.41.pick_ref) | copy-start | bytes 98308
  24.8 13.6 %copy-start.7 = (bf16[128,128]{1,0:T(8,128)(2,1)S(1)}, bf16[128,128]{1,0:T(8,128)(2,1)}, u32[]{:S(2)}) copy-start(bf16[128,128]{1,0:T(8,128)(2,1)} %resid_ref.1) | copy-start | bytes 98308
  28.6 1.1 copy-start.5
  29.7 8.6 %copy-start = (bf16[128,3584]{1,0:T(8,128)(2,1)S(1)}, bf16[128,3584]{1,0:T(8,128)(2,1)}, u32[]{:S(2)}) copy-start(bf16[128,3584]{1,0:T(8,128)(2,1)} %gate_ref.3) | copy-start | bytes 2752516
  29.7 8.7 %copy-start.1 = (bf16[128,3584]{1,0:T(8,128)(2,1)S(1)}, bf16[128,3584]{1,0:T(8,128)(2,1)}, u32[]{:S(2)}) copy-start(bf16[128,3584]{1,0:T(8,128)(2,1)} %up_ref.3) | copy-start | bytes 2752516
  29.7 8.7 %copy-start.2 = (bf16[3584,128]{1,0:T(8,128)(2,1)S(1)}, bf16[3584,128]{1,0:T(8,128)(2,1)}, u32[]{:S(2)}) copy-start(bf16[3584,128]{1,0:T(8,128)(2,1)} %w_ref.5) | copy-start | bytes 2752516
  33.0 5.4 %copy-start.3 = (bf16[1024,128]{1,0:T(8,128)(2,1)S(1)}, bf16[1024,128]{1,0:T(8,128)(2,1)}, u32[]{:S(2)}) copy-start(bf16[1024,128]{1,0:T(8,128)(2,1)} %w_ref.4) | copy-start | bytes 786436
  33.0 20.4 %all-to-all-start.1 = ((bf16[64,24,128]{2,1,0:T(8,128)(2,1)}), bf16[64,24,128]{2,1,0:T(8,128)(2,1)}, u32[]{:S(2)}, u32[]{:S(2)}) async-start(bf16[64,24,128]{2,1,0:T(8,128)(2,1)} %shard_map.138), calls=%async_computation.1 | async-start | bytes 786432 | tf_op jit(solution)/shard_map/all_to_all | solution.py:31
  38.4 0.7 copy-start.11
  40.5 33.0 %collective-permute-start = (bf16[22,128,128]{2,1,0:T(8,128)(2,1)}, bf16[22,128,128]{2,1,0:T(8,128)(2,1)S(1)}, u32[]{:S(2)}, u32[]{:S(2)}) collective-permute-start(bf16[22,128,128]{2,1,0:T(8,128)(2,1)} %get-tuple-element.30), channel_id=1, source_target_pairs={{0,8},{8,0},{1,9},{9,1},{2,10},{10,2},{3,11},{11,3},{4,12},{12,4},... | collective-permute-start | bytes 2162696 | tf_op jit(solution)/shard_map/ppermute | solution.py:344
  43.1 21.1 %collective-permute-start.1 = (bf16[16,128,128]{2,1,0:T(8,128)(2,1)}, bf16[16,128,128]{2,1,0:T(8,128)(2,1)}, u32[]{:S(2)}, u32[]{:S(2)}) collective-permute-start(bf16[16,128,128]{2,1,0:T(8,128)(2,1)} %get-tuple-element.31), channel_id=1, source_target_pairs={{0,8},{8,0},{64,72},{72,64},{1,9},{9,1},{65,73},{73,65},{2,10},{10... | collective-permute-start | bytes 1572872 | tf_op jit(solution)/shard_map/ppermute | solution.py:341
  45.0 19.2 %collective-permute-start.2 = (bf16[16,128,128]{2,1,0:T(8,128)(2,1)}, bf16[16,128,128]{2,1,0:T(8,128)(2,1)}, u32[]{:S(2)}, u32[]{:S(2)}) collective-permute-start(bf16[16,128,128]{2,1,0:T(8,128)(2,1)} %get-tuple-element.32), channel_id=1, source_target_pairs={{0,64},{8,72},{64,0},{72,8},{1,65},{9,73},{65,1},{73,9},{2,66},{10... | collective-permute-start | bytes 1572872 | tf_op jit(solution)/shard_map/ppermute | solution.py:341
  48.2 25.3 %collective-permute-start.3 = (bf16[16,128,128]{2,1,0:T(8,128)(2,1)}, bf16[16,128,128]{2,1,0:T(8,128)(2,1)}, u32[]{:S(2)}, u32[]{:S(2)}) collective-permute-start(bf16[16,128,128]{2,1,0:T(8,128)(2,1)} %get-tuple-element.33), channel_id=1, source_target_pairs={{0,72},{8,64},{64,8},{72,0},{1,73},{9,65},{65,9},{73,1},{2,74},{10... | collective-permute-start | bytes 1572872 | tf_op jit(solution)/shard_map/ppermute | solution.py:341
  53.5 0.7 copy-start.12
  53.5 0.7 copy-start.13
  56.2 0.7 copy-start.6
  56.9 23.4 %all-to-all-start.2 = ((bf16[32,16,128]{2,1,0:T(8,128)(2,1)}), bf16[32,16,128]{2,1,0:T(8,128)(2,1)}, u32[]{:S(2)}, u32[]{:S(2)}) async-start(bf16[32,16,128]{2,1,0:T(8,128)(2,1)} %copy-done.6), calls=%async_computation.2 | async-start | bytes 262144 | tf_op jit(solution)/shard_map/all_to_all | solution.py:31
  80.2 1.0 copy-start.4
  133.4 21.4 %copy-start.9 = (bf16[128,128]{1,0:T(8,128)(2,1)S(1)}, bf16[128,128]{1,0:T(8,128)(2,1)}, u32[]{:S(2)}) copy-start(bf16[128,128]{1,0:T(8,128)(2,1)} %copy-done.8) | copy-start | bytes 98308

commit v7 on v6

--- a/solution.py
+++ b/solution.py
@@ -12,6 +12,7 @@
 GROUP = 8
 LANES = 128
 EPS = 1e-05
+CHUNKS = 6
 NEG = -1e30
 VMEM_LIMIT = 16 * 2**20
 CTX = ("yh", "yl", "zl", "core")
@@ -71,10 +72,8 @@
         out_ref[d] = rows
 
 
-def prepare_body(
-    ring, len_hbm, table_hbm, order_hbm, meta_ref, pick_ref, len_ref, table_ref, order_ref, sems
-):
-    pairs = ((table_hbm, table_ref), (len_hbm, len_ref), (order_hbm, order_ref))
+def prepare_body(len_hbm, table_hbm, meta_ref, len_ref, table_ref, sems):
+    pairs = ((table_hbm, table_ref), (len_hbm, len_ref))
     copies = [pltpu.make_async_copy(a, b, sems.at[i]) for i, (a, b) in enumerate(pairs)]
     for copy in copies:
         copy.start()
@@ -90,9 +89,6 @@
         owner = found // cols
         meta_ref[s] = owner
         meta_ref[slots + s] = len_ref[owner] - (found % cols) * LANES
-    place = lax.broadcasted_iota(jnp.int32, pick_ref.shape, 0)
-    pick = request_of(place, ring) == order_ref[...]
-    pick_ref[...] = pick.astype(F32).astype(BF16)
 
 
 def cut_body(ring, gate_ref, up_ref, down_ref, w_ref, resid_ref, gain_ref, mine, core_ref, *out_refs):
@@ -122,16 +118,28 @@
         out_ref[2 * blocks + 1] = gain
 
 
-def attend_body(meta_ref, q_ref, k_ref, v_hbm, out_ref, top_ref, sum_ref, acc_ref, v_ref, sem):
+def attend_body(
+    meta_ref, q_ref, k_hbm, v_hbm, out_ref, top_ref, sum_ref, acc_ref, k_ref, v_ref, sems
+):
     slots, page = k_ref.shape[0], k_ref.shape[1]
-    fetch = pltpu.make_async_copy(v_hbm, v_ref, sem)
-    fetch.start()
+    part = slots // CHUNKS
+    fetches = [
+        [
+            pltpu.make_async_copy(a.at[pl.ds(i * part, part)], b.at[pl.ds(i * part, part)], sems.at[w, i])
+            for i in range(CHUNKS)
+        ]
+        for w, (a, b) in enumerate(((k_hbm, k_ref), (v_hbm, v_ref)))
+    ]
+    for fetch in fetches[0] + fetches[1]:
+        fetch.start()
     top_ref[...] = jnp.full(top_ref.shape, NEG, F32)
     sum_ref[...] = jnp.zeros(sum_ref.shape, F32)
     acc_ref[...] = jnp.zeros(acc_ref.shape, F32)
     lane = lane_ids((GROUP, page))
     owners, scores = [], []
     for s in range(slots):
+        if s % part == 0:
+            fetches[0][s // part].wait()
         owner, live = meta_ref[s], meta_ref[slots + s]
         home = owner // 2
         pair = q_ref[home % 2, home // 2].astype(F32)
@@ -142,8 +150,9 @@
         top_ref[owner] = jnp.maximum(top_ref[owner], jnp.broadcast_to(best, (GROUP, LANES)))
         owners.append(owner)
         scores.append(score)
-    fetch.wait()
     for s in range(slots):
+        if s % part == 0:
+            fetches[1][s // part].wait()
         owner = owners[s]
         shift = top_ref[owner].astype(BF16).astype(F32)
         weight = jnp.exp(scores[s] - shift)
@@ -166,42 +175,56 @@
         out_ref[d] = block.astype(BF16)
 
 
-def combine_body(part_ref, q_ref, fk_ref, fv_ref, out_ref):
+def combine_body(part_ref, q_ref, fk_hbm, fv_hbm, out_ref, fk_ref, fv_ref, sems):
+    fetches = [
+        pltpu.make_async_copy(fk_hbm, fk_ref, sems.at[0]),
+        pltpu.make_async_copy(fv_hbm, fv_ref, sems.at[1]),
+    ]
+    for fetch in fetches:
+        fetch.start()
     count = part_ref.shape[0]
+    best = jnp.full((GROUP, LANES), NEG, F32)
+    for d in range(count):
+        best = jnp.maximum(best, part_ref[d].astype(F32)[2 * GROUP :])
+    for fetch in fetches:
+        fetch.wait()
     fk, fv = fk_ref[...].astype(F32), fv_ref[...].astype(F32)
     q = q_ref[...].astype(F32)
-    done = []
+    tops, totals, accs = [], [], []
     for par in range(2):
-        base = par * 64
         mine = slice(par * GROUP, (par + 1) * GROUP)
         own = jnp.sum(q[mine] * fk[par : par + 1], axis=1, keepdims=True) * HD ** (-0.5)
-        best = own
-        for d in range(count):
-            stats = part_ref[d].astype(F32)[2 * GROUP :]
-            best = jnp.maximum(best, stats[:, base : base + 1])
-        own_weight = jnp.exp(own - best)
-        total = own_weight
-        acc = own_weight.astype(BF16).astype(F32) * fv[par : par + 1]
-        for d in range(count):
-            block = part_ref[d].astype(F32)
-            stats = block[2 * GROUP :]
-            factor = jnp.exp(stats[:, base : base + 1] - best)
-            total = total + factor * (stats[:, base + 1 : base + 2] + stats[:, base + 2 : base + 3])
-            acc = acc + factor * block[mine]
-        done.append(acc / total)
-    rows = jnp.concatenate(done, axis=0).astype(BF16)
+        top = jnp.maximum(best[:, par * 64 : par * 64 + 1], own)
+        own_weight = jnp.exp(own - top)
+        tops.append(top)
+        totals.append(own_weight)
+        accs.append(own_weight.astype(BF16).astype(F32) * fv[par : par + 1])
+    for d in range(count):
+        block = part_ref[d].astype(F32)
+        stats = block[2 * GROUP :]
+        for par in range(2):
+            base = par * 64
+            factor = jnp.exp(stats[:, base : base + 1] - tops[par])
+            total = stats[:, base + 1 : base + 2] + stats[:, base + 2 : base + 3]
+            totals[par] = totals[par] + factor * total
+            accs[par] = accs[par] + factor * block[par * GROUP : (par + 1) * GROUP]
+    rows = jnp.concatenate([accs[par] / totals[par] for par in range(2)], axis=0).astype(BF16)
     for d in range(out_ref.shape[0]):
         out_ref[d] = rows
 
 
-def project_body(att_ref, w_ref, met_ref, out_ref, rows_ref):
+def project_body(att_ref, w_hbm, met_ref, out_ref, rows_ref, w_ref, sem):
+    fetch = pltpu.make_async_copy(w_hbm, w_ref, sem)
+    fetch.start()
     core = lax.axis_index("core")
     count, per, _ = att_ref.shape
     rows_ref[...] = att_ref[...].astype(F32).reshape(count * per, HD)
     reqs = count * per // GROUP
     heads = [rows_ref[pl.ds(h, reqs, stride=GROUP), :].astype(BF16) for h in range(GROUP)]
     heads = jnp.concatenate(heads, axis=1)
-    for at, ref in ((core, w_ref), (1 - core, met_ref)):
+    for at, ref in ((1 - core, met_ref), (core, w_ref)):
+        if ref is w_ref:
+            fetch.wait()
         w = ref[...] if ref is w_ref else ref[:GROUP].reshape(GROUP * HD, LANES)
         total = jnp.dot(heads, w, preferred_element_type=F32).astype(BF16)
         for g in range(out_ref.shape[0]):
@@ -270,7 +293,11 @@
         out_ref[d] = active
 
 
-def down_body(act_ref, w_ref, met_ref, pick_ref, hidden_ref, out_ref, kept_ref):
+def down_body(
+    ring, act_ref, w_ref, met_ref, hidden_ref, order_hbm, out_ref, kept_ref, order_ref, sem
+):
+    fetch = pltpu.make_async_copy(order_hbm, order_ref, sem)
+    fetch.start()
     core = lax.axis_index("core")
     reqs = act_ref.shape[0] * act_ref.shape[2] * 8
     blocks = act_ref.shape[3] // 8
@@ -283,10 +310,15 @@
         own.append(w_ref[pl.ds(pl.multiple_of((2 * z + core) * height, LANES), height), :])
     acts = jnp.concatenate(acts, axis=1)
     met = met_ref[GROUP:].reshape(2 * height, LANES)
-    pick = pick_ref[...]
+    totals = [
+        jnp.dot(acts, w, preferred_element_type=F32).astype(BF16)
+        for w in (jnp.concatenate(own, axis=0), met)
+    ]
+    fetch.wait()
+    place = lax.broadcasted_iota(jnp.int32, (reqs, reqs), 0)
+    pick = (request_of(place, ring) == order_ref[...]).astype(F32).astype(BF16)
     dims = (((0,), (0,)), ((), ()))
-    for at, w in ((core, jnp.concatenate(own, axis=0)), (1 - core, met)):
-        total = jnp.dot(acts, w, preferred_element_type=F32).astype(BF16)
+    for at, total in ((core, totals[0]), (1 - core, totals[1])):
         total = lax.dot_general(pick, total, dims, preferred_element_type=F32)
         out_ref[at] = total.astype(BF16)
     kept = lax.dot_general(pick, hidden_ref[...], dims, preferred_element_type=F32)
@@ -342,18 +374,17 @@
         for flip, block in enumerate(given, 1)
     ]
     met_core = lax.ppermute(given_core, "core", [(0, 1), (1, 0)])
-    meta, pick = call(
-        functools.partial(prepare_body, ring),
-        (shape((2 * slots,), jnp.int32), shape((reqs, reqs), BF16)),
-        [HBM] * 3,
+    meta = call(
+        prepare_body,
+        shape((2 * slots,), jnp.int32),
+        [HBM] * 2,
         [
             pltpu.SMEM(lengths.shape, jnp.int32),
             pltpu.VMEM(block_table.shape, jnp.int32),
-            pltpu.VMEM((1, reqs), jnp.int32),
-            pltpu.SemaphoreType.DMA((3,)),
+            pltpu.SemaphoreType.DMA((2,)),
         ],
-        out_specs=(SMEM, VMEM),
-    )(lengths, block_table, row_order.reshape(1, reqs))
+        out_specs=SMEM,
+    )(lengths, block_table)
 
     packed, my_queries = call(
         pack_body, (shape((ring, 2 * GROUP, HD), BF16), shape((2 * GROUP, HD), BF16)), [VMEM]
@@ -361,22 +392,29 @@
     all_queries = exchange(packed, RING)
     all_queries = lax.all_gather(all_queries, "core", axis=0, tiled=False)
     scratch = [pltpu.VMEM((reqs, GROUP, LANES), F32)] * 3
-    scratch += [pltpu.VMEM(value_cache.shape, BF16), pltpu.SemaphoreType.DMA(())]
-    parts = call(attend_body, shape((ctx, 3 * GROUP, HD), BF16), [SMEM, VMEM, VMEM, HBM], scratch)(
+    scratch += [pltpu.VMEM(value_cache.shape, BF16)] * 2 + [pltpu.SemaphoreType.DMA((2, CHUNKS))]
+    parts = call(attend_body, shape((ctx, 3 * GROUP, HD), BF16), [SMEM, VMEM, HBM, HBM], scratch)(
         meta, all_queries, key_cache, value_cache
     )
     parts = exchange(parts, CTX)
     parts, mine = lax.optimization_barrier((parts, mine))
-    local = call(combine_body, shape((ring, 2 * GROUP, HD), BF16), [VMEM] * 4)(
+    scratch = [pltpu.VMEM(fresh_keys.shape, BF16)] * 2 + [pltpu.SemaphoreType.DMA((2,))]
+    local = call(
+        combine_body, shape((ring, 2 * GROUP, HD), BF16), [VMEM, VMEM, HBM, HBM], scratch
+    )(
         parts, my_queries, fresh_keys, fresh_values
     )
+    local, met_core = lax.optimization_barrier((local, met_core))
     attended = exchange(local, RING)
-    attended, met_core, *met = lax.optimization_barrier((attended, met_core, *met))
     projected = call(
         project_body,
         shape((grp, 2, reqs // 2, width), BF16),
-        [VMEM] * 3,
-        [pltpu.VMEM((ring * 2 * GROUP, HD), F32)],
+        [VMEM, HBM, VMEM],
+        [
+            pltpu.VMEM((ring * 2 * GROUP, HD), F32),
+            pltpu.VMEM(out_weight.shape, BF16),
+            pltpu.SemaphoreType.DMA(()),
+        ],
     )(attended, out_weight, met_core)
     projected = exchange(projected.reshape(grp, reqs, width), GRP)
     pay = call(gather_body, shape((reqs, width), BF16), [VMEM])(projected)
@@ -394,10 +432,17 @@
     active = exchange(active, RING)
     line = lax.axis_size("zl")
     rows, kept = call(
-        down_body,
+        functools.partial(down_body, ring),
         (shape((2, reqs, width), BF16), shape((reqs, width), BF16)),
-        [VMEM] * 5,
-    )(active.reshape(ring // (2 * line), 2, line, units, LANES), down_weight, met_core, pick, hidden)
+        [VMEM] * 4 + [HBM],
+        [pltpu.VMEM((1, reqs), jnp.int32), pltpu.SemaphoreType.DMA(())],
+    )(
+        active.reshape(ring // (2 * line), 2, line, units, LANES),
+        down_weight,
+        met_core,
+        hidden,
+        row_order.reshape(1, reqs),
+    )
     rows = exchange(rows.reshape(2 * grp, share, width), LAST)
     return call(finish_body, shape((share, width), BF16), [VMEM] * 2)(
         rows, kept.reshape(grp, share, width)

time: 172 us -> 168 us (0.977)
  waiting for transfers between devices: 26.5 us -> 18 us
  blocking collectives: 89.4 us -> 93.1 us
  Pallas kernels: 14.2 us -> 17.7 us
  starting transfers between devices: 36.4 us -> 34.1 us
    ppermute x3, waiting for transfers between devices: 9.32 us -> 0.01 us  [shards(): lax.ppermute(block, TEAM, [(i, i ^ flip) for i in range(team)])]
    all_to_all x4, blocking collectives: 76.8 us -> 80.5 us  [exchange(): return lax.all_to_all(x, axes, 0, 0, tiled=True)]
    pallas_call x11, Pallas kernels: 14.2 us -> 17.7 us  [run(): return kernel(*placed)]
    all_to_all x3, starting transfers between devices: 26 us -> 23.4 us  [exchange(): return lax.all_to_all(x, axes, 0, 0, tiled=True)]
    unnamed x28 -> x22, local copies, waits for them, and re-layouts: 4.72 us -> 4.36 us
  transfers between devices with their start and end apart: 7 -> 7, of which waited for: 4 -> 3; matrix products, arithmetic and copies ran while one was open for 0% -> 0% of each run, Pallas kernels for 3% -> 5%
where the time goes in v7:
time: 168 us; the launch traced here: 167 us
  blocking collectives  93.1 us (55%)
  starting transfers between devices  34.1 us (20%)
  waiting for transfers between devices  18 us (11%)
  Pallas kernels  17.7 us (11%)
  local copies, waits for them, and re-layouts  4.36 us (3%)
    all_to_all x4, blocking collectives, exchange(): return lax.all_to_all(x, axes, 0, 0, tiled=True)  80.5 us
    all_to_all x3, starting transfers between devices, exchange(): return lax.all_to_all(x, axes, 0, 0, tiled=True)  23.4 us
    all_to_all x3, waiting for transfers between devices, exchange(): return lax.all_to_all(x, axes, 0, 0, tiled=True)  18 us
    pallas_call x11, Pallas kernels, run(): return kernel(*placed)  17.7 us
    all_gather x1, blocking collectives, shards(): pay = lax.all_gather(pay, TEAM, axis=0, tiled=False)  8.78 us
    ppermute x3, starting transfers between devices, shards(): lax.ppermute(block, TEAM, [(i, i ^ flip) for i in range(team)])  8.16 us
    unnamed x22, local copies, waits for them, and re-layouts  4.36 us
    all_gather x1, blocking collectives, shards(): all_queries = lax.all_gather(all_queries, 'core', axis=0, tiled=False)  3.81 us
  transfers between devices with their start and end apart: 7, of which 3 were waited for; matrix products, arithmetic and copies ran while one was open for 0% of the time, Pallas kernels for 5%

profile of v7, /device:TPU:1, one launch (start us, length us, event | category | flops | bytes accessed | tf_op | source)
XLA Modules:
  0.0 167.5 jit_solution(14903045623036215855)
XLA Ops:
  0.0 0.7 copy-done.6
  0.7 0.7 shard_map.137
  1.3 13.5 %all-to-all-start = ((bf16[32,16,128]{2,1,0:T(8,128)(2,1)}), bf16[32,16,128]{2,1,0:T(8,128)(2,1)S(1)}, u32[]{:S(2)}, u32[]{:S(2)}) async-start(bf16[32,16,128]{2,1,0:T(8,128)(2,1)} %get-tuple-element.20), calls=%async_computation | async-start | bytes 262144 | tf_op jit(solution)/shard_map/all_to_all | solution.py:32
  14.8 2.0 %shard_map.136.meta_ref = s32[48]{0:T(128)S(1)} custom-call(s32[128]{0:T(128)} %len_hbm.1, s32[128,128]{1,0:T(8,128)} %table_hbm.1), custom_call_target="tpu_custom_call" | custom-call | tf_op jit(solution)/shard_map/pallas_call | solution.py:54
  16.8 8.0 %all-to-all-done = bf16[32,16,128]{2,1,0:T(8,128)(2,1)S(1)} async-done(((bf16[32,16,128]{2,1,0:T(8,128)(2,1)}), bf16[32,16,128]{2,1,0:T(8,128)(2,1)S(1)}, u32[]{:S(2)}, u32[]{:S(2)}) %all-to-all-start) | async-done | bytes 131104 | tf_op jit(solution)/shard_map/all_to_all | solution.py:32
  24.8 3.8 %all-gather = bf16[64,16,128]{2,1,0:T(8,128)(2,1)S(1)} all-gather(bf16[32,16,128]{2,1,0:T(8,128)(2,1)S(1)} %all-to-all-done), channel_id=2, replica_groups=mesh['yh'=4,'yl'=2,'zl'=4,'core'=2,'zh'=2,'x'=4] {'core'}, dimensions={0}, use_global_device_ids=true | all-gather | bytes 393216 | tf_op jit(solution)/shard_map/all_gather | solution.py:393
  28.6 5.2 %shard_map.138 = bf16[64,24,128]{2,1,0:T(8,128)(2,1)} custom-call(s32[48]{0:T(128)S(1)} %shard_map.136.meta_ref, bf16[2,32,16,128]{3,2,1,0:T(8,128)(2,1)S(1)} %bitcast.9, bf16[24,128,128]{2,1,0:T(8,128)(2,1)} %k_hbm.1, bf16[24,128,128]{2,1,0:T(8,128)(2,1)} %v_hbm.1), custom_call_target="tpu_custom_call" | custom-call | tf_op jit(solution)/shard_map/pallas_call | solution.py:54
  33.8 5.3 %all-to-all-start.1 = ((bf16[64,24,128]{2,1,0:T(8,128)(2,1)}), bf16[64,24,128]{2,1,0:T(8,128)(2,1)}, u32[]{:S(2)}, u32[]{:S(2)}) async-start(bf16[64,24,128]{2,1,0:T(8,128)(2,1)} %shard_map.138), calls=%async_computation.1 | async-start | bytes 786432 | tf_op jit(solution)/shard_map/all_to_all | solution.py:32
  39.2 0.6 copy-done.7
  39.7 1.2 shard_map.139
  40.9 0.8 copy-done.8
  41.7 0.8 copy-done.9
  42.5 0.8 copy-done.10
  43.3 2.5 %collective-permute-start = (bf16[22,128,128]{2,1,0:T(8,128)(2,1)}, bf16[22,128,128]{2,1,0:T(8,128)(2,1)S(1)}, u32[]{:S(2)}, u32[]{:S(2)}) collective-permute-start(bf16[22,128,128]{2,1,0:T(8,128)(2,1)} %get-tuple-element.24), channel_id=1, source_target_pairs={{0,8},{8,0},{1,9},{9,1},{2,10},{10,2},{3,11},{11,3},{4,12},{12,4},... | collective-permute-start | bytes 2162696 | tf_op jit(solution)/shard_map/ppermute | solution.py:376
  45.9 8.3 %all-to-all-done.1.part_ref = bf16[64,24,128]{2,1,0:T(8,128)(2,1)} async-done(((bf16[64,24,128]{2,1,0:T(8,128)(2,1)}), bf16[64,24,128]{2,1,0:T(8,128)(2,1)}, u32[]{:S(2)}, u32[]{:S(2)}) %all-to-all-start.1) | async-done | bytes 393248 | tf_op jit(solution)/shard_map/all_to_all | solution.py:32
  54.2 2.6 %shard_map.140 = bf16[32,16,128]{2,1,0:T(8,128)(2,1)S(1)} custom-call(bf16[64,24,128]{2,1,0:T(8,128)(2,1)} %all-to-all-done.1.part_ref, bf16[16,128]{1,0:T(8,128)(2,1)S(1)} %get-tuple-element.23.q_ref, bf16[2,128]{1,0:T(2,128)(2,1)} %fk_hbm.1, bf16[2,128]{1,0:T(2,128)(2,1)} %fv_hbm.1), custom_call_target="tpu_custom_call" | custom-call | tf_op jit(solution)/shard_map/pallas_call | solution.py:54
  56.8 0.6 copy-done.4
  57.5 4.6 %all-to-all-start.2 = ((bf16[32,16,128]{2,1,0:T(8,128)(2,1)}), bf16[32,16,128]{2,1,0:T(8,128)(2,1)}, u32[]{:S(2)}, u32[]{:S(2)}) async-start(bf16[32,16,128]{2,1,0:T(8,128)(2,1)} %copy-done.4), calls=%async_computation.2 | async-start | bytes 262144 | tf_op jit(solution)/shard_map/all_to_all | solution.py:32
  62.1 2.7 %collective-permute-start.1 = (bf16[16,128,128]{2,1,0:T(8,128)(2,1)}, bf16[16,128,128]{2,1,0:T(8,128)(2,1)}, u32[]{:S(2)}, u32[]{:S(2)}) collective-permute-start(bf16[16,128,128]{2,1,0:T(8,128)(2,1)} %copy-done.10), channel_id=1, source_target_pairs={{0,8},{8,0},{64,72},{72,64},{1,9},{9,1},{65,73},{73,65},{2,10},{10... | collective-permute-start | bytes 1572872 | tf_op jit(solution)/shard_map/ppermute | solution.py:373
  64.8 3.3 %collective-permute-start.2 = (bf16[16,128,128]{2,1,0:T(8,128)(2,1)}, bf16[16,128,128]{2,1,0:T(8,128)(2,1)}, u32[]{:S(2)}, u32[]{:S(2)}) collective-permute-start(bf16[16,128,128]{2,1,0:T(8,128)(2,1)} %copy-done.9), channel_id=1, source_target_pairs={{0,64},{8,72},{64,0},{72,8},{1,65},{9,73},{65,1},{73,9},{2,66},{10... | collective-permute-start | bytes 1572872 | tf_op jit(solution)/shard_map/ppermute | solution.py:373
  68.2 2.1 %collective-permute-start.3 = (bf16[16,128,128]{2,1,0:T(8,128)(2,1)}, bf16[16,128,128]{2,1,0:T(8,128)(2,1)}, u32[]{:S(2)}, u32[]{:S(2)}) collective-permute-start(bf16[16,128,128]{2,1,0:T(8,128)(2,1)} %copy-done.8), channel_id=1, source_target_pairs={{0,72},{8,64},{64,8},{72,0},{1,73},{9,65},{65,9},{73,1},{2,74},{10... | collective-permute-start | bytes 1572872 | tf_op jit(solution)/shard_map/ppermute | solution.py:373
  70.3 1.7 %all-to-all-done.2.att_ref = bf16[32,16,128]{2,1,0:T(8,128)(2,1)} async-done(((bf16[32,16,128]{2,1,0:T(8,128)(2,1)}), bf16[32,16,128]{2,1,0:T(8,128)(2,1)}, u32[]{:S(2)}, u32[]{:S(2)}) %all-to-all-start.2) | async-done | bytes 131104 | tf_op jit(solution)/shard_map/all_to_all | solution.py:32
  72.0 2.1 %shard_map.141 = bf16[8,2,64,128]{3,2,1,0:T(8,128)(2,1)S(1)} custom-call(bf16[32,16,128]{2,1,0:T(8,128)(2,1)} %all-to-all-done.2.att_ref, bf16[1024,128]{1,0:T(8,128)(2,1)} %w_hbm.1, bf16[22,128,128]{2,1,0:T(8,128)(2,1)S(1)} %collective-permute-done.met_ref), custom_call_target="tpu_custom_call" | custom-call | tf_op jit(solution)/shard_map/pallas_call | solution.py:54
  74.1 19.5 %all_to_all.35.part_ref = bf16[8,128,128]{2,1,0:T(8,128)(2,1)S(1)} all-to-all(bf16[8,128,128]{2,1,0:T(8,128)(2,1)S(1)} %bitcast.10), channel_id=1, replica_groups=mesh['yh'=4,'yl'=2,'zl'=4,'core'=2,'zh'=2,'x'=4] {'zh','x'}, dimensions={0} | all-to-all | bytes 524288 | tf_op jit(solution)/shard_map/all_to_all | solution.py:32
  93.7 8.8 %all-gather.1 = bf16[512,128]{1,0:T(8,128)(2,1)S(1)} all-gather(bf16[128,128]{1,0:T(8,128)(2,1)S(1)} %shard_map.142), channel_id=3, replica_groups=mesh['yh'=4,'yl'=2,'zl'=4,'core'=2,'zh'=2,'x'=4] {'yl','core'}, dimensions={0}, use_global_device_ids=true | all-gather | bytes 163840 | tf_op jit(solution)/shard_map/all_gather | solution.py:421
  102.5 2.0 %shard_map.143 = (bf16[16,120,128]{2,1,0:T(8,128)(2,1)S(1)}, bf16[128,128]{1,0:T(8,128)(2,1)S(1)}) custom-call(bf16[2,2,2,64,128]{4,3,2,1,0:T(8,128)(2,1)S(1)} %bitcast.11, bf16[2,128,128]{2,1,0:T(8,128)(2,1)S(1)} %get-tuple-element.27.mine_ref, bf16[128,3584]{1,0:T(8,128)(2,1)S(1)} %copy-done, bf16[128,3584]{1,0:T(8,128)(2,1)S(1)} %copy-done.1, ...), custom_call_target="tpu_custom_call" | custom-call | tf_op jit(solution)/shard_map/pallas_call | solution.py:54
  104.5 24.5 %all_to_all.36.part_ref = bf16[16,120,128]{2,1,0:T(8,128)(2,1)S(1)} all-to-all(bf16[16,120,128]{2,1,0:T(8,128)(2,1)S(1)} %get-tuple-element.31), channel_id=1, replica_groups=mesh['yh'=4,'yl'=2,'zl'=4,'core'=2,'zh'=2,'x'=4] {'yh','zl'}, dimensions={0} | all-to-all | bytes 983040 | tf_op jit(solution)/shard_map/all_to_all | solution.py:32
  129.0 0.2 shard_map.144
  129.2 20.7 %all_to_all.37 = bf16[32,56,128]{2,1,0:T(8,128)(2,1)S(1)} all-to-all(bf16[32,56,128]{2,1,0:T(8,128)(2,1)S(1)} %shard_map.144), channel_id=1, replica_groups=mesh['yh'=4,'yl'=2,'zl'=4,'core'=2,'zh'=2,'x'=4] {'yh','yl','zl'}, dimensions={0} | all-to-all | bytes 917504 | tf_op jit(solution)/shard_map/all_to_all | solution.py:32
  149.9 1.2 shard_map.145
  151.1 15.8 %all_to_all.38.part_ref = bf16[16,16,128]{2,1,0:T(8,128)(2,1)S(1)} all-to-all(bf16[16,16,128]{2,1,0:T(8,128)(2,1)S(1)} %bitcast.12), channel_id=1, replica_groups=mesh['yh'=4,'yl'=2,'zl'=4,'core'=2,'zh'=2,'x'=4] {'core','zh','x'}, dimensions={0} | all-to-all | bytes 131072 | tf_op jit(solution)/shard_map/all_to_all | solution.py:32
  166.8 0.6 shard_map.146
  (21 shorter events, 0.1 us)
Async XLA Ops:
  0.0 0.7 copy-start.6
  1.3 23.4 %all-to-all-start = ((bf16[32,16,128]{2,1,0:T(8,128)(2,1)}), bf16[32,16,128]{2,1,0:T(8,128)(2,1)S(1)}, u32[]{:S(2)}, u32[]{:S(2)}) async-start(bf16[32,16,128]{2,1,0:T(8,128)(2,1)} %get-tuple-element.20), calls=%async_computation | async-start | bytes 262144 | tf_op jit(solution)/shard_map/all_to_all | solution.py:32
  24.8 14.3 %copy-start.5 = (bf16[128,128]{1,0:T(8,128)(2,1)S(1)}, bf16[128,128]{1,0:T(8,128)(2,1)}, u32[]{:S(2)}) copy-start(bf16[128,128]{1,0:T(8,128)(2,1)} %resid_ref.1) | copy-start | bytes 98308
  28.6 10.5 %copy-start = (bf16[128,3584]{1,0:T(8,128)(2,1)S(1)}, bf16[128,3584]{1,0:T(8,128)(2,1)}, u32[]{:S(2)}) copy-start(bf16[128,3584]{1,0:T(8,128)(2,1)} %gate_ref.3) | copy-start | bytes 2752516
  28.6 10.6 %copy-start.1 = (bf16[128,3584]{1,0:T(8,128)(2,1)S(1)}, bf16[128,3584]{1,0:T(8,128)(2,1)}, u32[]{:S(2)}) copy-start(bf16[128,3584]{1,0:T(8,128)(2,1)} %up_ref.3) | copy-start | bytes 2752516
  28.6 10.6 %copy-start.2 = (bf16[3584,128]{1,0:T(8,128)(2,1)S(1)}, bf16[3584,128]{1,0:T(8,128)(2,1)}, u32[]{:S(2)}) copy-start(bf16[3584,128]{1,0:T(8,128)(2,1)} %w_ref.3) | copy-start | bytes 2752516
  33.7 5.4 %copy-start.3 = (bf16[1024,128]{1,0:T(8,128)(2,1)S(1)}, bf16[1024,128]{1,0:T(8,128)(2,1)}, u32[]{:S(2)}) copy-start(bf16[1024,128]{1,0:T(8,128)(2,1)} %w_hbm.1) | copy-start | bytes 786436
  33.8 20.4 %all-to-all-start.1 = ((bf16[64,24,128]{2,1,0:T(8,128)(2,1)}), bf16[64,24,128]{2,1,0:T(8,128)(2,1)}, u32[]{:S(2)}, u32[]{:S(2)}) async-start(bf16[64,24,128]{2,1,0:T(8,128)(2,1)} %shard_map.138), calls=%async_computation.1 | async-start | bytes 786432 | tf_op jit(solution)/shard_map/all_to_all | solution.py:32
  39.1 0.7 copy-start.7
  40.9 0.8 copy-start.8
  41.7 0.8 copy-start.9
  42.5 0.8 copy-start.10
  43.3 14.2 %collective-permute-start = (bf16[22,128,128]{2,1,0:T(8,128)(2,1)}, bf16[22,128,128]{2,1,0:T(8,128)(2,1)S(1)}, u32[]{:S(2)}, u32[]{:S(2)}) collective-permute-start(bf16[22,128,128]{2,1,0:T(8,128)(2,1)} %get-tuple-element.24), channel_id=1, source_target_pairs={{0,8},{8,0},{1,9},{9,1},{2,10},{10,2},{3,11},{11,3},{4,12},{12,4},... | collective-permute-start | bytes 2162696 | tf_op jit(solution)/shard_map/ppermute | solution.py:376
  56.8 0.7 copy-start.4
  57.5 14.5 %all-to-all-start.2 = ((bf16[32,16,128]{2,1,0:T(8,128)(2,1)}), bf16[32,16,128]{2,1,0:T(8,128)(2,1)}, u32[]{:S(2)}, u32[]{:S(2)}) async-start(bf16[32,16,128]{2,1,0:T(8,128)(2,1)} %copy-done.4), calls=%async_computation.2 | async-start | bytes 262144 | tf_op jit(solution)/shard_map/all_to_all | solution.py:32
  62.1 40.4 %collective-permute-start.1 = (bf16[16,128,128]{2,1,0:T(8,128)(2,1)}, bf16[16,128,128]{2,1,0:T(8,128)(2,1)}, u32[]{:S(2)}, u32[]{:S(2)}) collective-permute-start(bf16[16,128,128]{2,1,0:T(8,128)(2,1)} %copy-done.10), channel_id=1, source_target_pairs={{0,8},{8,0},{64,72},{72,64},{1,9},{9,1},{65,73},{73,65},{2,10},{10... | collective-permute-start | bytes 1572872 | tf_op jit(solution)/shard_map/ppermute | solution.py:373
  64.8 37.7 %collective-permute-start.2 = (bf16[16,128,128]{2,1,0:T(8,128)(2,1)}, bf16[16,128,128]{2,1,0:T(8,128)(2,1)}, u32[]{:S(2)}, u32[]{:S(2)}) collective-permute-start(bf16[16,128,128]{2,1,0:T(8,128)(2,1)} %copy-done.9), channel_id=1, source_target_pairs={{0,64},{8,72},{64,0},{72,8},{1,65},{9,73},{65,1},{73,9},{2,66},{10... | collective-permute-start | bytes 1572872 | tf_op jit(solution)/shard_map/ppermute | solution.py:373
  68.2 34.3 %collective-permute-start.3 = (bf16[16,128,128]{2,1,0:T(8,128)(2,1)}, bf16[16,128,128]{2,1,0:T(8,128)(2,1)}, u32[]{:S(2)}, u32[]{:S(2)}) collective-permute-start(bf16[16,128,128]{2,1,0:T(8,128)(2,1)} %copy-done.8), channel_id=1, source_target_pairs={{0,72},{8,64},{64,8},{72,0},{1,73},{9,65},{65,9},{73,1},{2,74},{10... | collective-permute-start | bytes 1572872 | tf_op jit(solution)/shard_map/ppermute | solution.py:373

commit v8 on v7

--- a/solution.py
+++ b/solution.py
@@ -12,7 +12,6 @@
 GROUP = 8
 LANES = 128
 EPS = 1e-05
-CHUNKS = 6
 NEG = -1e30
 VMEM_LIMIT = 16 * 2**20
 CTX = ("yh", "yl", "zl", "core")
@@ -91,7 +90,7 @@
         meta_ref[slots + s] = len_ref[owner] - (found % cols) * LANES
 
 
-def cut_body(ring, gate_ref, up_ref, down_ref, w_ref, resid_ref, gain_ref, mine, core_ref, *out_refs):
+def cut_body(ring, gate_ref, up_ref, down_ref, resid_ref, gain_ref, mine, core_ref, *out_refs):
     me = lax.axis_index(TEAM)
     reqs = resid_ref.shape[0]
     place = lax.broadcasted_iota(jnp.int32, (reqs, reqs), 0)
@@ -101,13 +100,11 @@
     mine[0, :reqs] = resid
     mine[1] = gain
     blocks = (out_refs[0].shape[0] - 2) // 2
-    heads = w_ref.shape[0] // LANES
-    core_ref[:heads] = w_ref[...].reshape(heads, LANES, LANES)
     other = 1 - lax.axis_index("core")
     for z in range(2):
         start = pl.multiple_of((2 * z + other) * blocks * LANES, LANES)
         rows = down_ref[pl.ds(start, blocks * LANES), :]
-        core_ref[heads + z * blocks : heads + (z + 1) * blocks] = rows.reshape(blocks, LANES, LANES)
+        core_ref[z * blocks : (z + 1) * blocks] = rows.reshape(blocks, LANES, LANES)
     for flip, out_ref in enumerate(out_refs, 1):
         start = (me ^ flip) * blocks * LANES
         for b in range(blocks):
@@ -118,28 +115,14 @@
         out_ref[2 * blocks + 1] = gain
 
 
-def attend_body(
-    meta_ref, q_ref, k_hbm, v_hbm, out_ref, top_ref, sum_ref, acc_ref, k_ref, v_ref, sems
-):
+def attend_body(meta_ref, q_ref, k_ref, v_ref, out_ref, top_ref, sum_ref, acc_ref):
     slots, page = k_ref.shape[0], k_ref.shape[1]
-    part = slots // CHUNKS
-    fetches = [
-        [
-            pltpu.make_async_copy(a.at[pl.ds(i * part, part)], b.at[pl.ds(i * part, part)], sems.at[w, i])
-            for i in range(CHUNKS)
-        ]
-        for w, (a, b) in enumerate(((k_hbm, k_ref), (v_hbm, v_ref)))
-    ]
-    for fetch in fetches[0] + fetches[1]:
-        fetch.start()
     top_ref[...] = jnp.full(top_ref.shape, NEG, F32)
     sum_ref[...] = jnp.zeros(sum_ref.shape, F32)
     acc_ref[...] = jnp.zeros(acc_ref.shape, F32)
     lane = lane_ids((GROUP, page))
     owners, scores = [], []
     for s in range(slots):
-        if s % part == 0:
-            fetches[0][s // part].wait()
         owner, live = meta_ref[s], meta_ref[slots + s]
         home = owner // 2
         pair = q_ref[home % 2, home // 2].astype(F32)
@@ -151,8 +134,6 @@
         owners.append(owner)
         scores.append(score)
     for s in range(slots):
-        if s % part == 0:
-            fetches[1][s // part].wait()
         owner = owners[s]
         shift = top_ref[owner].astype(BF16).astype(F32)
         weight = jnp.exp(scores[s] - shift)
@@ -175,19 +156,11 @@
         out_ref[d] = block.astype(BF16)
 
 
-def combine_body(part_ref, q_ref, fk_hbm, fv_hbm, out_ref, fk_ref, fv_ref, sems):
-    fetches = [
-        pltpu.make_async_copy(fk_hbm, fk_ref, sems.at[0]),
-        pltpu.make_async_copy(fv_hbm, fv_ref, sems.at[1]),
-    ]
-    for fetch in fetches:
-        fetch.start()
+def combine_body(part_ref, q_ref, fk_ref, fv_ref, out_ref):
     count = part_ref.shape[0]
     best = jnp.full((GROUP, LANES), NEG, F32)
     for d in range(count):
         best = jnp.maximum(best, part_ref[d].astype(F32)[2 * GROUP :])
-    for fetch in fetches:
-        fetch.wait()
     fk, fv = fk_ref[...].astype(F32), fv_ref[...].astype(F32)
     q = q_ref[...].astype(F32)
     tops, totals, accs = [], [], []
@@ -213,20 +186,15 @@
         out_ref[d] = rows
 
 
-def project_body(att_ref, w_hbm, met_ref, out_ref, rows_ref, w_ref, sem):
-    fetch = pltpu.make_async_copy(w_hbm, w_ref, sem)
-    fetch.start()
+def project_body(att_ref, w_ref, met_ref, out_ref, rows_ref):
     core = lax.axis_index("core")
     count, per, _ = att_ref.shape
     rows_ref[...] = att_ref[...].astype(F32).reshape(count * per, HD)
     reqs = count * per // GROUP
     heads = [rows_ref[pl.ds(h, reqs, stride=GROUP), :].astype(BF16) for h in range(GROUP)]
     heads = jnp.concatenate(heads, axis=1)
-    for at, ref in ((1 - core, met_ref), (core, w_ref)):
-        if ref is w_ref:
-            fetch.wait()
-        w = ref[...] if ref is w_ref else ref[:GROUP].reshape(GROUP * HD, LANES)
-        total = jnp.dot(heads, w, preferred_element_type=F32).astype(BF16)
+    for at, ref in ((core, w_ref), (1 - core, met_ref)):
+        total = jnp.dot(heads, ref[...], preferred_element_type=F32).astype(BF16)
         for g in range(out_ref.shape[0]):
             out_ref[g, at] = total
 
@@ -309,7 +277,7 @@
             acts.append(act[:, b * 8 : b * 8 + 8].reshape(reqs, LANES).astype(BF16))
         own.append(w_ref[pl.ds(pl.multiple_of((2 * z + core) * height, LANES), height), :])
     acts = jnp.concatenate(acts, axis=1)
-    met = met_ref[GROUP:].reshape(2 * height, LANES)
+    met = met_ref[...].reshape(2 * height, LANES)
     totals = [
         jnp.dot(acts, w, preferred_element_type=F32).astype(BF16)
         for w in (jnp.concatenate(own, axis=0), met)
@@ -363,17 +331,18 @@
         ]
 
     bundle = shape((2 * blocks + 2, LANES, LANES), BF16)
-    core_bundle = shape((GROUP + 2 * blocks, LANES, LANES), BF16)
+    core_bundle = shape((2 * blocks, LANES, LANES), BF16)
     mine, given_core, *given = call(
         functools.partial(cut_body, ring),
         (shape((2, LANES, LANES), BF16), core_bundle) + (bundle,) * 3,
-        [VMEM] * 6,
-    )(gate_weight, up_weight, down_weight, out_weight, resid, norm_gain.reshape(1, width))
+        [VMEM] * 5,
+    )(gate_weight, up_weight, down_weight, resid, norm_gain.reshape(1, width))
     met = [
         lax.ppermute(block, TEAM, [(i, i ^ flip) for i in range(team)])
         for flip, block in enumerate(given, 1)
     ]
     met_core = lax.ppermute(given_core, "core", [(0, 1), (1, 0)])
+    met_out = lax.ppermute(out_weight, "core", [(0, 1), (1, 0)])
     meta = call(
         prepare_body,
         shape((2 * slots,), jnp.int32),
@@ -392,16 +361,12 @@
     all_queries = exchange(packed, RING)
     all_queries = lax.all_gather(all_queries, "core", axis=0, tiled=False)
     scratch = [pltpu.VMEM((reqs, GROUP, LANES), F32)] * 3
-    scratch += [pltpu.VMEM(value_cache.shape, BF16)] * 2 + [pltpu.SemaphoreType.DMA((2, CHUNKS))]
-    parts = call(attend_body, shape((ctx, 3 * GROUP, HD), BF16), [SMEM, VMEM, HBM, HBM], scratch)(
+    parts = call(attend_body, shape((ctx, 3 * GROUP, HD), BF16), [SMEM] + [VMEM] * 3, scratch)(
         meta, all_queries, key_cache, value_cache
     )
     parts = exchange(parts, CTX)
     parts, mine = lax.optimization_barrier((parts, mine))
-    scratch = [pltpu.VMEM(fresh_keys.shape, BF16)] * 2 + [pltpu.SemaphoreType.DMA((2,))]
-    local = call(
-        combine_body, shape((ring, 2 * GROUP, HD), BF16), [VMEM, VMEM, HBM, HBM], scratch
-    )(
+    local = call(combine_body, shape((ring, 2 * GROUP, HD), BF16), [VMEM] * 4)(
         parts, my_queries, fresh_keys, fresh_values
     )
     local, met_core = lax.optimization_barrier((local, met_core))
@@ -409,13 +374,9 @@
     projected = call(
         project_body,
         shape((grp, 2, reqs // 2, width), BF16),
-        [VMEM, HBM, VMEM],
-        [
-            pltpu.VMEM((ring * 2 * GROUP, HD), F32),
-            pltpu.VMEM(out_weight.shape, BF16),
-            pltpu.SemaphoreType.DMA(()),
-        ],
-    )(attended, out_weight, met_core)
+        [VMEM] * 3,
+        [pltpu.VMEM((ring * 2 * GROUP, HD), F32)],
+    )(attended, out_weight, met_out)
     projected = exchange(projected.reshape(grp, reqs, width), GRP)
     pay = call(gather_body, shape((reqs, width), BF16), [VMEM])(projected)
     pay = lax.all_gather(pay, TEAM, axis=0, tiled=False)

time: 168 us -> 167 us (level)
  Pallas kernels: 17.7 us -> 13.8 us
  local copies, waits for them, and re-layouts: 4.36 us -> 6.67 us
  waiting for transfers between devices: 18 us -> 16.3 us
    pallas_call x11, Pallas kernels: 17.7 us -> 13.8 us  [run(): return kernel(*placed)]
    unnamed x22 -> x26, local copies, waits for them, and re-layouts: 4.36 us -> 6.67 us
    ppermute x0 -> x1, starting transfers between devices: none -> 1.92 us  [shards(): met_out = lax.ppermute(out_weight, 'core', [(0, 1), (1, 0)])]
    all_to_all x3, waiting for transfers between devices: 18 us -> 16.3 us  [exchange(): return lax.all_to_all(x, axes, 0, 0, tiled=True)]
  transfers between devices with their start and end apart: 7 -> 8, of which waited for: 3 -> 3; matrix products, arithmetic and copies ran while one was open for 0% -> 0% of each run, Pallas kernels for 5% -> 4%
where the time goes in v8:
time: 167 us; the launch traced here: 166 us
  blocking collectives  93.8 us (56%)
  starting transfers between devices  35 us (21%)
  waiting for transfers between devices  16.3 us (10%)
  Pallas kernels  13.8 us (8%)
  local copies, waits for them, and re-layouts  6.67 us (4%)
    all_to_all x4, blocking collectives, exchange(): return lax.all_to_all(x, axes, 0, 0, tiled=True)  81.3 us
    all_to_all x3, starting transfers between devices, exchange(): return lax.all_to_all(x, axes, 0, 0, tiled=True)  22.5 us
    all_to_all x3, waiting for transfers between devices, exchange(): return lax.all_to_all(x, axes, 0, 0, tiled=True)  16.3 us
    pallas_call x11, Pallas kernels, run(): return kernel(*placed)  13.8 us
    all_gather x1, blocking collectives, shards(): pay = lax.all_gather(pay, TEAM, axis=0, tiled=False)  8.78 us
    ppermute x3, starting transfers between devices, shards(): lax.ppermute(block, TEAM, [(i, i ^ flip) for i in range(team)])  8.16 us
    unnamed x26, local copies, waits for them, and re-layouts  6.67 us
    all_gather x1, blocking collectives, shards(): all_queries = lax.all_gather(all_queries, 'core', axis=0, tiled=False)  3.68 us
  transfers between devices with their start and end apart: 8, of which 3 were waited for; matrix products, arithmetic and copies ran while one was open for 0% of the time, Pallas kernels for 4%

profile of v8, /device:TPU:1, one launch (start us, length us, event | category | flops | bytes accessed | tf_op | source)
XLA Modules:
  0.0 165.8 jit_solution(11480619606548542027)
XLA Ops:
  0.0 0.7 copy-done.6
  0.7 0.7 shard_map.137
  1.4 13.5 %all-to-all-start = ((bf16[32,16,128]{2,1,0:T(8,128)(2,1)}), bf16[32,16,128]{2,1,0:T(8,128)(2,1)S(1)}, u32[]{:S(2)}, u32[]{:S(2)}) async-start(bf16[32,16,128]{2,1,0:T(8,128)(2,1)} %get-tuple-element.20), calls=%async_computation | async-start | bytes 262144 | tf_op jit(solution)/shard_map/all_to_all | solution.py:31
  14.8 2.0 %shard_map.136.meta_ref = s32[48]{0:T(128)S(1)} custom-call(s32[128]{0:T(128)} %len_hbm.1, s32[128,128]{1,0:T(8,128)} %table_hbm.1), custom_call_target="tpu_custom_call" | custom-call | tf_op jit(solution)/shard_map/pallas_call | solution.py:53
  16.8 8.0 %all-to-all-done = bf16[32,16,128]{2,1,0:T(8,128)(2,1)S(1)} async-done(((bf16[32,16,128]{2,1,0:T(8,128)(2,1)}), bf16[32,16,128]{2,1,0:T(8,128)(2,1)S(1)}, u32[]{:S(2)}, u32[]{:S(2)}) %all-to-all-start) | async-done | bytes 131104 | tf_op jit(solution)/shard_map/all_to_all | solution.py:31
  24.8 3.7 %all-gather = bf16[64,16,128]{2,1,0:T(8,128)(2,1)S(1)} all-gather(bf16[32,16,128]{2,1,0:T(8,128)(2,1)S(1)} %all-to-all-done), channel_id=2, replica_groups=mesh['yh'=4,'yl'=2,'zl'=4,'core'=2,'zh'=2,'x'=4] {'core'}, dimensions={0}, use_global_device_ids=true | all-gather | bytes 393216 | tf_op jit(solution)/shard_map/all_gather | solution.py:362
  28.4 1.1 copy-done.3
  29.6 1.1 copy-done.4
  30.7 2.2 %shard_map.138 = bf16[64,24,128]{2,1,0:T(8,128)(2,1)} custom-call(s32[48]{0:T(128)S(1)} %shard_map.136.meta_ref, bf16[2,32,16,128]{3,2,1,0:T(8,128)(2,1)S(1)} %bitcast.9, bf16[24,128,128]{2,1,0:T(8,128)(2,1)S(1)} %copy-done.3, bf16[24,128,128]{2,1,0:T(8,128)(2,1)S(1)} %copy-done.4), custom_call_target="tpu_custom_call" | custom-call | tf_op jit(solution)/shard_map/pallas_call | solution.py:53
  33.0 4.6 %all-to-all-start.1 = ((bf16[64,24,128]{2,1,0:T(8,128)(2,1)}), bf16[64,24,128]{2,1,0:T(8,128)(2,1)S(1)}, u32[]{:S(2)}, u32[]{:S(2)}) async-start(bf16[64,24,128]{2,1,0:T(8,128)(2,1)} %shard_map.138), calls=%async_computation.1 | async-start | bytes 786432 | tf_op jit(solution)/shard_map/all_to_all | solution.py:31
  38.2 1.1 shard_map.139
  39.3 0.8 copy-done.10
  40.1 0.8 copy-done.11
  40.9 0.8 copy-done.12
  41.7 2.5 %collective-permute-start = (bf16[14,128,128]{2,1,0:T(8,128)(2,1)}, bf16[14,128,128]{2,1,0:T(8,128)(2,1)}, u32[]{:S(2)}, u32[]{:S(2)}) collective-permute-start(bf16[14,128,128]{2,1,0:T(8,128)(2,1)} %get-tuple-element.24), channel_id=1, source_target_pairs={{0,8},{8,0},{1,9},{9,1},{2,10},{10,2},{3,11},{11,3},{4,12},{12,4},... | collective-permute-start | bytes 1376264 | tf_op jit(solution)/shard_map/ppermute | solution.py:344
  44.2 1.9 %collective-permute-start.1 = (bf16[1024,128]{1,0:T(8,128)(2,1)}, bf16[1024,128]{1,0:T(8,128)(2,1)}, u32[]{:S(2)}, u32[]{:S(2)}) collective-permute-start(bf16[1024,128]{1,0:T(8,128)(2,1)} %w_ref.2), channel_id=1, source_target_pairs={{0,8},{8,0},{1,9},{9,1},{2,10},{10,2},{3,11},{11,3},{4,12},{12,4},... | collective-permute-start | bytes 786440 | tf_op jit(solution)/shard_map/ppermute | solution.py:345
  46.1 6.6 %all-to-all-done.1.part_ref = bf16[64,24,128]{2,1,0:T(8,128)(2,1)S(1)} async-done(((bf16[64,24,128]{2,1,0:T(8,128)(2,1)}), bf16[64,24,128]{2,1,0:T(8,128)(2,1)S(1)}, u32[]{:S(2)}, u32[]{:S(2)}) %all-to-all-start.1) | async-done | bytes 393248 | tf_op jit(solution)/shard_map/all_to_all | solution.py:31
  52.7 0.7 copy-done.8
  53.4 1.6 shard_map.140
  55.0 4.5 %all-to-all-start.2 = ((bf16[32,16,128]{2,1,0:T(8,128)(2,1)}), bf16[32,16,128]{2,1,0:T(8,128)(2,1)S(1)}, u32[]{:S(2)}, u32[]{:S(2)}) async-start(bf16[32,16,128]{2,1,0:T(8,128)(2,1)} %shard_map.140), calls=%async_computation.2 | async-start | bytes 262144 | tf_op jit(solution)/shard_map/all_to_all | solution.py:31
  59.5 2.7 %collective-permute-start.2 = (bf16[16,128,128]{2,1,0:T(8,128)(2,1)}, bf16[16,128,128]{2,1,0:T(8,128)(2,1)S(1)}, u32[]{:S(2)}, u32[]{:S(2)}) collective-permute-start(bf16[16,128,128]{2,1,0:T(8,128)(2,1)} %copy-done.12), channel_id=1, source_target_pairs={{0,8},{8,0},{64,72},{72,64},{1,9},{9,1},{65,73},{73,65},{2,10},{10... | collective-permute-start | bytes 1572872 | tf_op jit(solution)/shard_map/ppermute | solution.py:341
  62.2 3.4 %collective-permute-start.3 = (bf16[16,128,128]{2,1,0:T(8,128)(2,1)}, bf16[16,128,128]{2,1,0:T(8,128)(2,1)}, u32[]{:S(2)}, u32[]{:S(2)}) collective-permute-start(bf16[16,128,128]{2,1,0:T(8,128)(2,1)} %copy-done.11), channel_id=1, source_target_pairs={{0,64},{8,72},{64,0},{72,8},{1,65},{9,73},{65,1},{73,9},{2,66},{10... | collective-permute-start | bytes 1572872 | tf_op jit(solution)/shard_map/ppermute | solution.py:341
  65.6 2.0 %collective-permute-start.4 = (bf16[16,128,128]{2,1,0:T(8,128)(2,1)}, bf16[16,128,128]{2,1,0:T(8,128)(2,1)}, u32[]{:S(2)}, u32[]{:S(2)}) collective-permute-start(bf16[16,128,128]{2,1,0:T(8,128)(2,1)} %copy-done.10), channel_id=1, source_target_pairs={{0,72},{8,64},{64,8},{72,0},{1,73},{9,65},{65,9},{73,1},{2,74},{10... | collective-permute-start | bytes 1572872 | tf_op jit(solution)/shard_map/ppermute | solution.py:341
  67.7 1.7 %all-to-all-done.2.att_ref = bf16[32,16,128]{2,1,0:T(8,128)(2,1)S(1)} async-done(((bf16[32,16,128]{2,1,0:T(8,128)(2,1)}), bf16[32,16,128]{2,1,0:T(8,128)(2,1)S(1)}, u32[]{:S(2)}, u32[]{:S(2)}) %all-to-all-start.2) | async-done | bytes 131104 | tf_op jit(solution)/shard_map/all_to_all | solution.py:31
  69.4 1.3 shard_map.141
  70.7 19.6 %all_to_all.35.part_ref = bf16[8,128,128]{2,1,0:T(8,128)(2,1)S(1)} all-to-all(bf16[8,128,128]{2,1,0:T(8,128)(2,1)S(1)} %bitcast.10), channel_id=1, replica_groups=mesh['yh'=4,'yl'=2,'zl'=4,'core'=2,'zh'=2,'x'=4] {'zh','x'}, dimensions={0} | all-to-all | bytes 524288 | tf_op jit(solution)/shard_map/all_to_all | solution.py:31
  90.3 8.8 %all-gather.1 = bf16[512,128]{1,0:T(8,128)(2,1)S(1)} all-gather(bf16[128,128]{1,0:T(8,128)(2,1)S(1)} %shard_map.142), channel_id=3, replica_groups=mesh['yh'=4,'yl'=2,'zl'=4,'core'=2,'zh'=2,'x'=4] {'yl','core'}, dimensions={0}, use_global_device_ids=true | all-gather | bytes 163840 | tf_op jit(solution)/shard_map/all_gather | solution.py:382
  99.1 1.9 %shard_map.143 = (bf16[16,120,128]{2,1,0:T(8,128)(2,1)S(1)}, bf16[128,128]{1,0:T(8,128)(2,1)S(1)}) custom-call(bf16[2,2,2,64,128]{4,3,2,1,0:T(8,128)(2,1)S(1)} %bitcast.11, bf16[2,128,128]{2,1,0:T(8,128)(2,1)S(1)} %get-tuple-element.26.mine_ref, bf16[128,3584]{1,0:T(8,128)(2,1)S(1)} %copy-done, bf16[128,3584]{1,0:T(8,128)(2,1)S(1)} %copy-done.1, ...), custom_call_target="tpu_custom_call" | custom-call | tf_op jit(solution)/shard_map/pallas_call | solution.py:53
  100.9 24.5 %all_to_all.36.part_ref = bf16[16,120,128]{2,1,0:T(8,128)(2,1)S(1)} all-to-all(bf16[16,120,128]{2,1,0:T(8,128)(2,1)S(1)} %get-tuple-element.30), channel_id=1, replica_groups=mesh['yh'=4,'yl'=2,'zl'=4,'core'=2,'zh'=2,'x'=4] {'yh','zl'}, dimensions={0} | all-to-all | bytes 983040 | tf_op jit(solution)/shard_map/all_to_all | solution.py:31
  125.7 20.7 %all_to_all.37 = bf16[32,56,128]{2,1,0:T(8,128)(2,1)S(1)} all-to-all(bf16[32,56,128]{2,1,0:T(8,128)(2,1)S(1)} %shard_map.144), channel_id=1, replica_groups=mesh['yh'=4,'yl'=2,'zl'=4,'core'=2,'zh'=2,'x'=4] {'yh','yl','zl'}, dimensions={0} | all-to-all | bytes 917504 | tf_op jit(solution)/shard_map/all_to_all | solution.py:31
  146.4 2.2 %shard_map.145 = (bf16[2,128,128]{2,1,0:T(8,128)(2,1)S(1)}, bf16[128,128]{1,0:T(8,128)(2,1)S(1)}) custom-call(bf16[4,2,4,56,128]{4,3,2,1,0:T(8,128)(2,1)S(1)} %bitcast.8, bf16[3584,128]{1,0:T(8,128)(2,1)S(1)} %copy-done.2, bf16[14,128,128]{2,1,0:T(8,128)(2,1)} %collective-permute-done.met_ref, bf16[128,128]{1,0:T(8,128)(2,1)S(1)} %get-tuple-element.32.hidden_ref, ...), custom_call_target="tpu_custom_call" | custom-call | tf_op jit(solution)/shard_map/pallas_call | solution.py:53
  148.6 16.6 %all_to_all.38.part_ref = bf16[16,16,128]{2,1,0:T(8,128)(2,1)S(1)} all-to-all(bf16[16,16,128]{2,1,0:T(8,128)(2,1)S(1)} %bitcast.12), channel_id=1, replica_groups=mesh['yh'=4,'yl'=2,'zl'=4,'core'=2,'zh'=2,'x'=4] {'core','zh','x'}, dimensions={0} | all-to-all | bytes 131072 | tf_op jit(solution)/shard_map/all_to_all | solution.py:31
  (27 shorter events, 1.5 us)
Async XLA Ops:
  0.0 0.7 copy-start.6
  1.4 23.4 %all-to-all-start = ((bf16[32,16,128]{2,1,0:T(8,128)(2,1)}), bf16[32,16,128]{2,1,0:T(8,128)(2,1)S(1)}, u32[]{:S(2)}, u32[]{:S(2)}) async-start(bf16[32,16,128]{2,1,0:T(8,128)(2,1)} %get-tuple-element.20), calls=%async_computation | async-start | bytes 262144 | tf_op jit(solution)/shard_map/all_to_all | solution.py:31
  28.4 1.1 copy-start.3
  29.6 1.1 copy-start.4
  30.7 6.8 %copy-start = (bf16[128,3584]{1,0:T(8,128)(2,1)S(1)}, bf16[128,3584]{1,0:T(8,128)(2,1)}, u32[]{:S(2)}) copy-start(bf16[128,3584]{1,0:T(8,128)(2,1)} %gate_ref.3) | copy-start | bytes 2752516
  30.7 6.8 %copy-start.1 = (bf16[128,3584]{1,0:T(8,128)(2,1)S(1)}, bf16[128,3584]{1,0:T(8,128)(2,1)}, u32[]{:S(2)}) copy-start(bf16[128,3584]{1,0:T(8,128)(2,1)} %up_ref.3) | copy-start | bytes 2752516
  30.7 6.8 %copy-start.2 = (bf16[3584,128]{1,0:T(8,128)(2,1)S(1)}, bf16[3584,128]{1,0:T(8,128)(2,1)}, u32[]{:S(2)}) copy-start(bf16[3584,128]{1,0:T(8,128)(2,1)} %w_ref.3) | copy-start | bytes 2752516
  33.0 4.6 %copy-start.5 = (bf16[128,128]{1,0:T(8,128)(2,1)S(1)}, bf16[128,128]{1,0:T(8,128)(2,1)}, u32[]{:S(2)}) copy-start(bf16[128,128]{1,0:T(8,128)(2,1)} %resid_ref.1) | copy-start | bytes 98308
  33.0 19.7 %all-to-all-start.1 = ((bf16[64,24,128]{2,1,0:T(8,128)(2,1)}), bf16[64,24,128]{2,1,0:T(8,128)(2,1)S(1)}, u32[]{:S(2)}, u32[]{:S(2)}) async-start(bf16[64,24,128]{2,1,0:T(8,128)(2,1)} %shard_map.138), calls=%async_computation.1 | async-start | bytes 786432 | tf_op jit(solution)/shard_map/all_to_all | solution.py:31
  37.5 0.7 copy-start.7
  39.3 0.8 copy-start.10
  40.1 0.8 copy-start.11
  40.9 0.8 copy-start.12
  41.7 13.3 %collective-permute-start = (bf16[14,128,128]{2,1,0:T(8,128)(2,1)}, bf16[14,128,128]{2,1,0:T(8,128)(2,1)}, u32[]{:S(2)}, u32[]{:S(2)}) collective-permute-start(bf16[14,128,128]{2,1,0:T(8,128)(2,1)} %get-tuple-element.24), channel_id=1, source_target_pairs={{0,8},{8,0},{1,9},{9,1},{2,10},{10,2},{3,11},{11,3},{4,12},{12,4},... | collective-permute-start | bytes 1376264 | tf_op jit(solution)/shard_map/ppermute | solution.py:344
  44.2 23.5 %collective-permute-start.1 = (bf16[1024,128]{1,0:T(8,128)(2,1)}, bf16[1024,128]{1,0:T(8,128)(2,1)}, u32[]{:S(2)}, u32[]{:S(2)}) collective-permute-start(bf16[1024,128]{1,0:T(8,128)(2,1)} %w_ref.2), channel_id=1, source_target_pairs={{0,8},{8,0},{1,9},{9,1},{2,10},{10,2},{3,11},{11,3},{4,12},{12,4},... | collective-permute-start | bytes 786440 | tf_op jit(solution)/shard_map/ppermute | solution.py:345
  52.7 0.7 copy-start.8
  52.7 0.7 copy-start.9
  55.0 14.4 %all-to-all-start.2 = ((bf16[32,16,128]{2,1,0:T(8,128)(2,1)}), bf16[32,16,128]{2,1,0:T(8,128)(2,1)S(1)}, u32[]{:S(2)}, u32[]{:S(2)}) async-start(bf16[32,16,128]{2,1,0:T(8,128)(2,1)} %shard_map.140), calls=%async_computation.2 | async-start | bytes 262144 | tf_op jit(solution)/shard_map/all_to_all | solution.py:31
  59.5 39.6 %collective-permute-start.2 = (bf16[16,128,128]{2,1,0:T(8,128)(2,1)}, bf16[16,128,128]{2,1,0:T(8,128)(2,1)S(1)}, u32[]{:S(2)}, u32[]{:S(2)}) collective-permute-start(bf16[16,128,128]{2,1,0:T(8,128)(2,1)} %copy-done.12), channel_id=1, source_target_pairs={{0,8},{8,0},{64,72},{72,64},{1,9},{9,1},{65,73},{73,65},{2,10},{10... | collective-permute-start | bytes 1572872 | tf_op jit(solution)/shard_map/ppermute | solution.py:341
  62.2 36.9 %collective-permute-start.3 = (bf16[16,128,128]{2,1,0:T(8,128)(2,1)}, bf16[16,128,128]{2,1,0:T(8,128)(2,1)}, u32[]{:S(2)}, u32[]{:S(2)}) collective-permute-start(bf16[16,128,128]{2,1,0:T(8,128)(2,1)} %copy-done.11), channel_id=1, source_target_pairs={{0,64},{8,72},{64,0},{72,8},{1,65},{9,73},{65,1},{73,9},{2,66},{10... | collective-permute-start | bytes 1572872 | tf_op jit(solution)/shard_map/ppermute | solution.py:341
  65.6 33.5 %collective-permute-start.4 = (bf16[16,128,128]{2,1,0:T(8,128)(2,1)}, bf16[16,128,128]{2,1,0:T(8,128)(2,1)}, u32[]{:S(2)}, u32[]{:S(2)}) collective-permute-start(bf16[16,128,128]{2,1,0:T(8,128)(2,1)} %copy-done.10), channel_id=1, source_target_pairs={{0,72},{8,64},{64,8},{72,0},{1,73},{9,65},{65,9},{73,1},{2,74},{10... | collective-permute-start | bytes 1572872 | tf_op jit(solution)/shard_map/ppermute | solution.py:341

commit v9 on v8

--- a/solution.py
+++ b/solution.py
@@ -12,6 +12,7 @@
 GROUP = 8
 LANES = 128
 EPS = 1e-05
+CHUNKS = 6
 NEG = -1e30
 VMEM_LIMIT = 16 * 2**20
 CTX = ("yh", "yl", "zl", "core")
@@ -90,7 +91,9 @@
         meta_ref[slots + s] = len_ref[owner] - (found % cols) * LANES
 
 
-def cut_body(ring, gate_ref, up_ref, down_ref, resid_ref, gain_ref, mine, core_ref, *out_refs):
+def cut_body(
+    ring, gate_ref, up_ref, down_ref, resid_ref, gain_ref, mine, core_ref, met2_ref, met3_ref
+):
     me = lax.axis_index(TEAM)
     reqs = resid_ref.shape[0]
     place = lax.broadcasted_iota(jnp.int32, (reqs, reqs), 0)
@@ -99,27 +102,39 @@
     gain = jnp.broadcast_to(gain_ref[...].astype(F32), (LANES, LANES)).astype(BF16)
     mine[0, :reqs] = resid
     mine[1] = gain
-    blocks = (out_refs[0].shape[0] - 2) // 2
+    blocks = (met2_ref.shape[0] - 2) // 2
     other = 1 - lax.axis_index("core")
     for z in range(2):
         start = pl.multiple_of((2 * z + other) * blocks * LANES, LANES)
         rows = down_ref[pl.ds(start, blocks * LANES), :]
         core_ref[z * blocks : (z + 1) * blocks] = rows.reshape(blocks, LANES, LANES)
-    for flip, out_ref in enumerate(out_refs, 1):
+    for flip, out_ref, base in ((1, core_ref, 2 * blocks), (2, met2_ref, 0), (3, met3_ref, 0)):
         start = (me ^ flip) * blocks * LANES
         for b in range(blocks):
             cols = pl.ds(pl.multiple_of(start + b * LANES, LANES), LANES)
-            out_ref[b] = gate_ref[:, cols]
-            out_ref[blocks + b] = up_ref[:, cols]
-        out_ref[2 * blocks, :reqs] = resid
-        out_ref[2 * blocks + 1] = gain
-
-
-def attend_body(meta_ref, q_ref, k_ref, v_ref, out_ref, top_ref, sum_ref, acc_ref):
+            out_ref[base + b] = gate_ref[:, cols]
+            out_ref[base + blocks + b] = up_ref[:, cols]
+        out_ref[base + 2 * blocks, :reqs] = resid
+        out_ref[base + 2 * blocks + 1] = gain
+
+
+def attend_body(
+    meta_ref, q_ref, k_hbm, v_hbm, out_ref, top_ref, sum_ref, acc_ref, k_ref, v_ref, sems
+):
     slots, page = k_ref.shape[0], k_ref.shape[1]
+    part = slots // CHUNKS
+    fetches = []
+    for w, (a, b) in enumerate(((k_hbm, k_ref), (v_hbm, v_ref))):
+        for i in range(CHUNKS):
+            span = pl.ds(i * part, part)
+            fetches.append(pltpu.make_async_copy(a.at[span], b.at[span], sems.at[w, i]))
+    for fetch in fetches:
+        fetch.start()
     top_ref[...] = jnp.full(top_ref.shape, NEG, F32)
     sum_ref[...] = jnp.zeros(sum_ref.shape, F32)
     acc_ref[...] = jnp.zeros(acc_ref.shape, F32)
+    for fetch in fetches:
+        fetch.wait()
     lane = lane_ids((GROUP, page))
     owners, scores = [], []
     for s in range(slots):
@@ -213,11 +228,12 @@
     team = 2 * pay_ref.shape[0]
     reqs = 2 * pay_ref.shape[3]
     mets = (met1_ref, met2_ref, met3_ref)
-    blocks = (met1_ref.shape[0] - 2) // 2
+    blocks = (met2_ref.shape[0] - 2) // 2
+    bases = (met1_ref.shape[0] - met2_ref.shape[0], 0, 0)
     square = jnp.zeros((reqs, 1), F32)
     gained = []
     for flip in range(team):
-        ref, at = (mine_ref, 0) if flip == 0 else (mets[flip - 1], 2 * blocks)
+        ref, at = (mine_ref, 0) if flip == 0 else (mets[flip - 1], bases[flip - 1] + 2 * blocks)
         owner = me ^ flip
         chip, core = owner // 2, owner % 2
         projected = jnp.concatenate([pay_ref[chip, c, core].astype(F32) for c in range(2)], axis=0)
@@ -232,7 +248,7 @@
     for b in range(2 * blocks):
         ref, at = (gate_ref, b) if b < blocks else (up_ref, b - blocks)
         cols = pl.ds(pl.multiple_of((me * blocks + at) * LANES, LANES), LANES)
-        w = jnp.concatenate([ref[:, cols]] + [met_ref[b] for met_ref in mets], axis=0)
+        w = jnp.concatenate([ref[:, cols]] + [met_ref[base + b] for met_ref, base in zip(mets, bases)], axis=0)
         x = jnp.dot(gained, w, preferred_element_type=F32)
         tiles.append(x.reshape(reqs // 8, 8, LANES))
     for i in range(blocks):
@@ -277,7 +293,7 @@
             acts.append(act[:, b * 8 : b * 8 + 8].reshape(reqs, LANES).astype(BF16))
         own.append(w_ref[pl.ds(pl.multiple_of((2 * z + core) * height, LANES), height), :])
     acts = jnp.concatenate(acts, axis=1)
-    met = met_ref[...].reshape(2 * height, LANES)
+    met = met_ref[: 2 * blocks].reshape(2 * height, LANES)
     totals = [
         jnp.dot(acts, w, preferred_element_type=F32).astype(BF16)
         for w in (jnp.concatenate(own, axis=0), met)
@@ -331,15 +347,15 @@
         ]
 
     bundle = shape((2 * blocks + 2, LANES, LANES), BF16)
-    core_bundle = shape((2 * blocks, LANES, LANES), BF16)
+    core_bundle = shape((4 * blocks + 2, LANES, LANES), BF16)
     mine, given_core, *given = call(
         functools.partial(cut_body, ring),
-        (shape((2, LANES, LANES), BF16), core_bundle) + (bundle,) * 3,
+        (shape((2, LANES, LANES), BF16), core_bundle, bundle, bundle),
         [VMEM] * 5,
     )(gate_weight, up_weight, down_weight, resid, norm_gain.reshape(1, width))
     met = [
         lax.ppermute(block, TEAM, [(i, i ^ flip) for i in range(team)])
-        for flip, block in enumerate(given, 1)
+        for flip, block in enumerate(given, 2)
     ]
     met_core = lax.ppermute(given_core, "core", [(0, 1), (1, 0)])
     met_out = lax.ppermute(out_weight, "core", [(0, 1), (1, 0)])
@@ -361,7 +377,8 @@
     all_queries = exchange(packed, RING)
     all_queries = lax.all_gather(all_queries, "core", axis=0, tiled=False)
     scratch = [pltpu.VMEM((reqs, GROUP, LANES), F32)] * 3
-    parts = call(attend_body, shape((ctx, 3 * GROUP, HD), BF16), [SMEM] + [VMEM] * 3, scratch)(
+    scratch += [pltpu.VMEM(key_cache.shape, BF16)] * 2 + [pltpu.SemaphoreType.DMA((2, CHUNKS))]
+    parts = call(attend_body, shape((ctx, 3 * GROUP, HD), BF16), [SMEM, VMEM, HBM, HBM], scratch)(
         meta, all_queries, key_cache, value_cache
     )
     parts = exchange(parts, CTX)
@@ -369,8 +386,8 @@
     local = call(combine_body, shape((ring, 2 * GROUP, HD), BF16), [VMEM] * 4)(
         parts, my_queries, fresh_keys, fresh_values
     )
-    local, met_core = lax.optimization_barrier((local, met_core))
     attended = exchange(local, RING)
+    attended, met_core = lax.optimization_barrier((attended, met_core))
     projected = call(
         project_body,
         shape((grp, 2, reqs // 2, width), BF16),
@@ -385,7 +402,7 @@
         widen_body,
         (shape((rest, 2 * units + 8, LANES), BF16), shape((reqs, width), BF16)),
         [VMEM] * 7,
-    )(pay.reshape(team // 2, 2, 2, reqs // 2, width), mine, gate_weight, up_weight, *met)
+    )(pay.reshape(team // 2, 2, 2, reqs // 2, width), mine, gate_weight, up_weight, met_core, *met)
     wide = exchange(wide, REST)
     active = call(
         functools.partial(activate_body, width * ctx), shape((ring, units, LANES), BF16), [VMEM]

time: 167 us -> 161 us (0.964)
  blocking collectives: 93.8 us -> 90.2 us
  waiting for transfers between devices: 16.3 us -> 18.9 us
  local copies, waits for them, and re-layouts: 6.67 us -> 4.34 us
  starting transfers between devices: 35 us -> 33.1 us
    all_to_all x4, blocking collectives: 81.3 us -> 77.6 us  [exchange(): return lax.all_to_all(x, axes, 0, 0, tiled=True)]
    all_to_all x3, waiting for transfers between devices: 16.3 us -> 18.9 us  [exchange(): return lax.all_to_all(x, axes, 0, 0, tiled=True)]
    unnamed x26 -> x24, local copies, waits for them, and re-layouts: 6.67 us -> 4.34 us
    ppermute x3 -> x2, starting transfers between devices: 8.16 us -> 6.24 us  [shards(): lax.ppermute(block, TEAM, [(i, i ^ flip) for i in range(team)])]
  transfers between devices with their start and end apart: 8 -> 7, of which waited for: 3 -> 3; matrix products, arithmetic and copies ran while one was open for 0% -> 0% of each run, Pallas kernels for 4% -> 4%
where the time goes in v9:
time: 161 us
  blocking collectives  90.2 us (56%)
  starting transfers between devices  33.1 us (21%)
  waiting for transfers between devices  18.9 us (12%)
  Pallas kernels  13.9 us (9%)
  local copies, waits for them, and re-layouts  4.34 us (3%)
    all_to_all x4, blocking collectives, exchange(): return lax.all_to_all(x, axes, 0, 0, tiled=True)  77.6 us
    all_to_all x3, starting transfers between devices, exchange(): return lax.all_to_all(x, axes, 0, 0, tiled=True)  22.5 us
    all_to_all x3, waiting for transfers between devices, exchange(): return lax.all_to_all(x, axes, 0, 0, tiled=True)  18.9 us
    pallas_call x11, Pallas kernels, run(): return kernel(*placed)  13.9 us
    all_gather x1, blocking collectives, shards(): pay = lax.all_gather(pay, TEAM, axis=0, tiled=False)  8.95 us
    ppermute x2, starting transfers between devices, shards(): lax.ppermute(block, TEAM, [(i, i ^ flip) for i in range(team)])  6.24 us
    unnamed x24, local copies, waits for them, and re-layouts  4.34 us
    all_gather x1, blocking collectives, shards(): all_queries = lax.all_gather(all_queries, 'core', axis=0, tiled=False)  3.68 us
  transfers between devices with their start and end apart: 7, of which 3 were waited for; matrix products, arithmetic and copies ran while one was open for 0% of the time, Pallas kernels for 4%

profile of v9, /device:TPU:1, one launch (start us, length us, event | category | flops | bytes accessed | tf_op | source)
XLA Modules:
  0.0 160.6 jit_solution(201876222044357372)
XLA Ops:
  0.0 0.7 copy-done.6
  0.7 0.7 shard_map.137
  1.3 13.5 %all-to-all-start = ((bf16[32,16,128]{2,1,0:T(8,128)(2,1)}), bf16[32,16,128]{2,1,0:T(8,128)(2,1)S(1)}, u32[]{:S(2)}, u32[]{:S(2)}) async-start(bf16[32,16,128]{2,1,0:T(8,128)(2,1)} %get-tuple-element.19), calls=%async_computation | async-start | bytes 262144 | tf_op jit(solution)/shard_map/all_to_all | solution.py:32
  14.8 2.0 %shard_map.136.meta_ref = s32[48]{0:T(128)S(1)} custom-call(s32[128]{0:T(128)} %len_hbm.1, s32[128,128]{1,0:T(8,128)} %table_hbm.1), custom_call_target="tpu_custom_call" | custom-call | tf_op jit(solution)/shard_map/pallas_call | solution.py:54
  16.8 8.0 %all-to-all-done = bf16[32,16,128]{2,1,0:T(8,128)(2,1)S(1)} async-done(((bf16[32,16,128]{2,1,0:T(8,128)(2,1)}), bf16[32,16,128]{2,1,0:T(8,128)(2,1)S(1)}, u32[]{:S(2)}, u32[]{:S(2)}) %all-to-all-start) | async-done | bytes 131104 | tf_op jit(solution)/shard_map/all_to_all | solution.py:32
  24.8 3.7 %all-gather = bf16[64,16,128]{2,1,0:T(8,128)(2,1)S(1)} all-gather(bf16[32,16,128]{2,1,0:T(8,128)(2,1)S(1)} %all-to-all-done), channel_id=2, replica_groups=mesh['yh'=4,'yl'=2,'zl'=4,'core'=2,'zh'=2,'x'=4] {'core'}, dimensions={0}, use_global_device_ids=true | all-gather | bytes 393216 | tf_op jit(solution)/shard_map/all_gather | solution.py:378
  28.4 3.3 %shard_map.138 = bf16[64,24,128]{2,1,0:T(8,128)(2,1)S(1)} custom-call(s32[48]{0:T(128)S(1)} %shard_map.136.meta_ref, bf16[2,32,16,128]{3,2,1,0:T(8,128)(2,1)S(1)} %bitcast.9, bf16[24,128,128]{2,1,0:T(8,128)(2,1)} %k_hbm.1, bf16[24,128,128]{2,1,0:T(8,128)(2,1)} %v_hbm.1), custom_call_target="tpu_custom_call" | custom-call | tf_op jit(solution)/shard_map/pallas_call | solution.py:54
  31.8 0.7 copy-done.4
  32.5 4.6 %all-to-all-start.1 = ((bf16[64,24,128]{2,1,0:T(8,128)(2,1)}), bf16[64,24,128]{2,1,0:T(8,128)(2,1)S(1)}, u32[]{:S(2)}, u32[]{:S(2)}) async-start(bf16[64,24,128]{2,1,0:T(8,128)(2,1)} %copy-done.4), calls=%async_computation.1 | async-start | bytes 786432 | tf_op jit(solution)/shard_map/all_to_all | solution.py:32
  37.2 0.6 copy-done.7
  37.8 1.3 shard_map.139
  39.0 0.8 copy-done.10
  39.8 0.8 copy-done.11
  40.7 2.5 %collective-permute-start = (bf16[30,128,128]{2,1,0:T(8,128)(2,1)}, bf16[30,128,128]{2,1,0:T(8,128)(2,1)S(1)}, u32[]{:S(2)}, u32[]{:S(2)}) collective-permute-start(bf16[30,128,128]{2,1,0:T(8,128)(2,1)} %get-tuple-element.23), channel_id=1, source_target_pairs={{0,8},{8,0},{1,9},{9,1},{2,10},{10,2},{3,11},{11,3},{4,12},{12,4},... | collective-permute-start | bytes 2949128 | tf_op jit(solution)/shard_map/ppermute | solution.py:360
  43.1 1.9 %collective-permute-start.1 = (bf16[1024,128]{1,0:T(8,128)(2,1)}, bf16[1024,128]{1,0:T(8,128)(2,1)}, u32[]{:S(2)}, u32[]{:S(2)}) collective-permute-start(bf16[1024,128]{1,0:T(8,128)(2,1)} %w_ref.2), channel_id=1, source_target_pairs={{0,8},{8,0},{1,9},{9,1},{2,10},{10,2},{3,11},{11,3},{4,12},{12,4},... | collective-permute-start | bytes 786440 | tf_op jit(solution)/shard_map/ppermute | solution.py:361
  45.1 7.2 %all-to-all-done.1.part_ref = bf16[64,24,128]{2,1,0:T(8,128)(2,1)S(1)} async-done(((bf16[64,24,128]{2,1,0:T(8,128)(2,1)}), bf16[64,24,128]{2,1,0:T(8,128)(2,1)S(1)}, u32[]{:S(2)}, u32[]{:S(2)}) %all-to-all-start.1) | async-done | bytes 393248 | tf_op jit(solution)/shard_map/all_to_all | solution.py:32
  52.3 0.7 copy-done.8
  53.0 1.6 %shard_map.140 = bf16[32,16,128]{2,1,0:T(8,128)(2,1)} custom-call(bf16[64,24,128]{2,1,0:T(8,128)(2,1)S(1)} %all-to-all-done.1.part_ref, bf16[16,128]{1,0:T(8,128)(2,1)S(1)} %get-tuple-element.22.q_ref, bf16[2,128]{1,0:T(2,128)(2,1)S(1)} %copy-done.8, bf16[2,128]{1,0:T(2,128)(2,1)S(1)} %copy-done.9), custom_call_target="tpu_custom_call" | custom-call | tf_op jit(solution)/shard_map/pallas_call | solution.py:54
  54.6 4.5 %all-to-all-start.2 = ((bf16[32,16,128]{2,1,0:T(8,128)(2,1)}), bf16[32,16,128]{2,1,0:T(8,128)(2,1)S(1)}, u32[]{:S(2)}, u32[]{:S(2)}) async-start(bf16[32,16,128]{2,1,0:T(8,128)(2,1)} %shard_map.140), calls=%async_computation.2 | async-start | bytes 262144 | tf_op jit(solution)/shard_map/all_to_all | solution.py:32
  59.1 3.1 %collective-permute-start.2 = (bf16[16,128,128]{2,1,0:T(8,128)(2,1)}, bf16[16,128,128]{2,1,0:T(8,128)(2,1)S(1)}, u32[]{:S(2)}, u32[]{:S(2)}) collective-permute-start(bf16[16,128,128]{2,1,0:T(8,128)(2,1)} %copy-done.11), channel_id=1, source_target_pairs={{0,64},{8,72},{64,0},{72,8},{1,65},{9,73},{65,1},{73,9},{2,66},{10... | collective-permute-start | bytes 1572872 | tf_op jit(solution)/shard_map/ppermute | solution.py:357
  62.2 3.1 %collective-permute-start.3 = (bf16[16,128,128]{2,1,0:T(8,128)(2,1)}, bf16[16,128,128]{2,1,0:T(8,128)(2,1)}, u32[]{:S(2)}, u32[]{:S(2)}) collective-permute-start(bf16[16,128,128]{2,1,0:T(8,128)(2,1)} %copy-done.10), channel_id=1, source_target_pairs={{0,72},{8,64},{64,8},{72,0},{1,73},{9,65},{65,9},{73,1},{2,74},{10... | collective-permute-start | bytes 1572872 | tf_op jit(solution)/shard_map/ppermute | solution.py:357
  65.3 3.7 %all-to-all-done.2.att_ref = bf16[32,16,128]{2,1,0:T(8,128)(2,1)S(1)} async-done(((bf16[32,16,128]{2,1,0:T(8,128)(2,1)}), bf16[32,16,128]{2,1,0:T(8,128)(2,1)S(1)}, u32[]{:S(2)}, u32[]{:S(2)}) %all-to-all-start.2) | async-done | bytes 131104 | tf_op jit(solution)/shard_map/all_to_all | solution.py:32
  69.0 1.4 shard_map.141
  70.4 19.6 %all_to_all.35.part_ref = bf16[8,128,128]{2,1,0:T(8,128)(2,1)S(1)} all-to-all(bf16[8,128,128]{2,1,0:T(8,128)(2,1)S(1)} %bitcast.10), channel_id=1, replica_groups=mesh['yh'=4,'yl'=2,'zl'=4,'core'=2,'zh'=2,'x'=4] {'zh','x'}, dimensions={0} | all-to-all | bytes 524288 | tf_op jit(solution)/shard_map/all_to_all | solution.py:32
  90.0 8.9 %all-gather.1 = bf16[512,128]{1,0:T(8,128)(2,1)S(1)} all-gather(bf16[128,128]{1,0:T(8,128)(2,1)S(1)} %shard_map.142), channel_id=3, replica_groups=mesh['yh'=4,'yl'=2,'zl'=4,'core'=2,'zh'=2,'x'=4] {'yl','core'}, dimensions={0}, use_global_device_ids=true | all-gather | bytes 163840 | tf_op jit(solution)/shard_map/all_gather | solution.py:399
  98.9 1.7 %shard_map.143 = (bf16[16,120,128]{2,1,0:T(8,128)(2,1)S(1)}, bf16[128,128]{1,0:T(8,128)(2,1)S(1)}) custom-call(bf16[2,2,2,64,128]{4,3,2,1,0:T(8,128)(2,1)S(1)} %bitcast.11, bf16[2,128,128]{2,1,0:T(8,128)(2,1)S(1)} %get-tuple-element.25.mine_ref, bf16[128,3584]{1,0:T(8,128)(2,1)S(1)} %copy-done.1, bf16[128,3584]{1,0:T(8,128)(2,1)S(1)} %copy-done.3, ...), custom_call_target="tpu_custom_call" | custom-call | tf_op jit(solution)/shard_map/pallas_call | solution.py:54
  100.6 21.3 %all_to_all.36.part_ref = bf16[16,120,128]{2,1,0:T(8,128)(2,1)S(1)} all-to-all(bf16[16,120,128]{2,1,0:T(8,128)(2,1)S(1)} %get-tuple-element.29), channel_id=1, replica_groups=mesh['yh'=4,'yl'=2,'zl'=4,'core'=2,'zh'=2,'x'=4] {'yh','zl'}, dimensions={0} | all-to-all | bytes 983040 | tf_op jit(solution)/shard_map/all_to_all | solution.py:32
  121.9 0.2 shard_map.144
  122.1 21.4 %all_to_all.37 = bf16[32,56,128]{2,1,0:T(8,128)(2,1)S(1)} all-to-all(bf16[32,56,128]{2,1,0:T(8,128)(2,1)S(1)} %shard_map.144), channel_id=1, replica_groups=mesh['yh'=4,'yl'=2,'zl'=4,'core'=2,'zh'=2,'x'=4] {'yh','yl','zl'}, dimensions={0} | all-to-all | bytes 917504 | tf_op jit(solution)/shard_map/all_to_all | solution.py:32
  143.5 1.2 shard_map.145
  144.7 15.4 %all_to_all.38.part_ref = bf16[16,16,128]{2,1,0:T(8,128)(2,1)S(1)} all-to-all(bf16[16,16,128]{2,1,0:T(8,128)(2,1)S(1)} %bitcast.12), channel_id=1, replica_groups=mesh['yh'=4,'yl'=2,'zl'=4,'core'=2,'zh'=2,'x'=4] {'core','zh','x'}, dimensions={0} | all-to-all | bytes 131072 | tf_op jit(solution)/shard_map/all_to_all | solution.py:32
  160.0 0.6 shard_map.146
  (23 shorter events, 0.1 us)
Async XLA Ops:
  0.0 0.7 copy-start.6
  1.3 23.4 %all-to-all-start = ((bf16[32,16,128]{2,1,0:T(8,128)(2,1)}), bf16[32,16,128]{2,1,0:T(8,128)(2,1)S(1)}, u32[]{:S(2)}, u32[]{:S(2)}) async-start(bf16[32,16,128]{2,1,0:T(8,128)(2,1)} %get-tuple-element.19), calls=%async_computation | async-start | bytes 262144 | tf_op jit(solution)/shard_map/all_to_all | solution.py:32
  28.4 8.7 %copy-start = (bf16[3584,128]{1,0:T(8,128)(2,1)S(1)}, bf16[3584,128]{1,0:T(8,128)(2,1)}, u32[]{:S(2)}) copy-start(bf16[3584,128]{1,0:T(8,128)(2,1)} %w_ref.3) | copy-start | bytes 2752516
  28.4 8.7 %copy-start.1 = (bf16[128,3584]{1,0:T(8,128)(2,1)S(1)}, bf16[128,3584]{1,0:T(8,128)(2,1)}, u32[]{:S(2)}) copy-start(bf16[128,3584]{1,0:T(8,128)(2,1)} %gate_ref.3) | copy-start | bytes 2752516
  28.4 8.7 %copy-start.2 = (bf16[128,3584]{1,0:T(8,128)(2,1)S(1)}, bf16[128,3584]{1,0:T(8,128)(2,1)}, u32[]{:S(2)}) copy-start(bf16[128,3584]{1,0:T(8,128)(2,1)} %up_ref.3) | copy-start | bytes 2752516
  31.8 0.7 copy-start.4
  32.5 4.6 %copy-start.5 = (bf16[128,128]{1,0:T(8,128)(2,1)S(1)}, bf16[128,128]{1,0:T(8,128)(2,1)}, u32[]{:S(2)}) copy-start(bf16[128,128]{1,0:T(8,128)(2,1)} %resid_ref.1) | copy-start | bytes 98308
  32.5 19.7 %all-to-all-start.1 = ((bf16[64,24,128]{2,1,0:T(8,128)(2,1)}), bf16[64,24,128]{2,1,0:T(8,128)(2,1)S(1)}, u32[]{:S(2)}, u32[]{:S(2)}) async-start(bf16[64,24,128]{2,1,0:T(8,128)(2,1)} %copy-done.4), calls=%async_computation.1 | async-start | bytes 786432 | tf_op jit(solution)/shard_map/all_to_all | solution.py:32
  37.1 0.7 copy-start.7
  39.0 0.8 copy-start.10
  39.8 0.8 copy-start.11
  40.7 24.7 %collective-permute-start = (bf16[30,128,128]{2,1,0:T(8,128)(2,1)}, bf16[30,128,128]{2,1,0:T(8,128)(2,1)S(1)}, u32[]{:S(2)}, u32[]{:S(2)}) collective-permute-start(bf16[30,128,128]{2,1,0:T(8,128)(2,1)} %get-tuple-element.23), channel_id=1, source_target_pairs={{0,8},{8,0},{1,9},{9,1},{2,10},{10,2},{3,11},{11,3},{4,12},{12,4},... | collective-permute-start | bytes 2949128 | tf_op jit(solution)/shard_map/ppermute | solution.py:360
  43.1 25.9 %collective-permute-start.1 = (bf16[1024,128]{1,0:T(8,128)(2,1)}, bf16[1024,128]{1,0:T(8,128)(2,1)}, u32[]{:S(2)}, u32[]{:S(2)}) collective-permute-start(bf16[1024,128]{1,0:T(8,128)(2,1)} %w_ref.2), channel_id=1, source_target_pairs={{0,8},{8,0},{1,9},{9,1},{2,10},{10,2},{3,11},{11,3},{4,12},{12,4},... | collective-permute-start | bytes 786440 | tf_op jit(solution)/shard_map/ppermute | solution.py:361
  52.3 0.7 copy-start.8
  52.3 0.7 copy-start.9
  54.6 14.4 %all-to-all-start.2 = ((bf16[32,16,128]{2,1,0:T(8,128)(2,1)}), bf16[32,16,128]{2,1,0:T(8,128)(2,1)S(1)}, u32[]{:S(2)}, u32[]{:S(2)}) async-start(bf16[32,16,128]{2,1,0:T(8,128)(2,1)} %shard_map.140), calls=%async_computation.2 | async-start | bytes 262144 | tf_op jit(solution)/shard_map/all_to_all | solution.py:32
  59.1 39.8 %collective-permute-start.2 = (bf16[16,128,128]{2,1,0:T(8,128)(2,1)}, bf16[16,128,128]{2,1,0:T(8,128)(2,1)S(1)}, u32[]{:S(2)}, u32[]{:S(2)}) collective-permute-start(bf16[16,128,128]{2,1,0:T(8,128)(2,1)} %copy-done.11), channel_id=1, source_target_pairs={{0,64},{8,72},{64,0},{72,8},{1,65},{9,73},{65,1},{73,9},{2,66},{10... | collective-permute-start | bytes 1572872 | tf_op jit(solution)/shard_map/ppermute | solution.py:357
  62.2 36.7 %collective-permute-start.3 = (bf16[16,128,128]{2,1,0:T(8,128)(2,1)}, bf16[16,128,128]{2,1,0:T(8,128)(2,1)}, u32[]{:S(2)}, u32[]{:S(2)}) collective-permute-start(bf16[16,128,128]{2,1,0:T(8,128)(2,1)} %copy-done.10), channel_id=1, source_target_pairs={{0,72},{8,64},{64,8},{72,0},{1,73},{9,65},{65,9},{73,1},{2,74},{10... | collective-permute-start | bytes 1572872 | tf_op jit(solution)/shard_map/ppermute | solution.py:357
  69.0 29.9 %copy-start.3 = (bf16[128,3584]{1,0:T(8,128)(2,1)S(1)}, bf16[128,3584]{1,0:T(8,128)(2,1)}, u32[]{:S(2)}) copy-start(bf16[128,3584]{1,0:T(8,128)(2,1)} %up_ref.3) | copy-start | bytes 2752516

commit v10 on v9

--- a/solution.py
+++ b/solution.py
@@ -61,7 +61,10 @@
     return (at >> 1) * 4 + core * 2 + (at & 1)
 
 
-def pack_body(q_ref, out_ref, mine_ref):
+def pack_body(q_hbm, out_ref, mine_ref, q_ref, sem):
+    fetch = pltpu.make_async_copy(q_hbm, q_ref, sem)
+    fetch.start()
+    fetch.wait()
     wide = q_ref[...].astype(F32)
     rows = [
         wide[r : r + 1, h * HD : (h + 1) * HD] for r in range(wide.shape[0]) for h in range(GROUP)
@@ -119,7 +122,23 @@
 
 
 def attend_body(
-    meta_ref, q_ref, k_hbm, v_hbm, out_ref, top_ref, sum_ref, acc_ref, k_ref, v_ref, sems
+    meta_ref,
+    q_ref,
+    k_hbm,
+    v_hbm,
+    fk_hbm,
+    fv_hbm,
+    out_ref,
+    fresh_ref,
+    top_ref,
+    sum_ref,
+    acc_ref,
+    k_ref,
+    v_ref,
+    fk_ref,
+    fv_ref,
+    sems,
+    fresh_sems,
 ):
     slots, page = k_ref.shape[0], k_ref.shape[1]
     part = slots // CHUNKS
@@ -128,6 +147,8 @@
         for i in range(CHUNKS):
             span = pl.ds(i * part, part)
             fetches.append(pltpu.make_async_copy(a.at[span], b.at[span], sems.at[w, i]))
+    fetches.append(pltpu.make_async_copy(fk_hbm, fk_ref, fresh_sems.at[0]))
+    fetches.append(pltpu.make_async_copy(fv_hbm, fv_ref, fresh_sems.at[1]))
     for fetch in fetches:
         fetch.start()
     top_ref[...] = jnp.full(top_ref.shape, NEG, F32)
@@ -135,6 +156,8 @@
     acc_ref[...] = jnp.zeros(acc_ref.shape, F32)
     for fetch in fetches:
         fetch.wait()
+    fresh_ref[0] = fk_ref[...].astype(F32)
+    fresh_ref[1] = fv_ref[...].astype(F32)
     lane = lane_ids((GROUP, page))
     owners, scores = [], []
     for s in range(slots):
@@ -171,12 +194,12 @@
         out_ref[d] = block.astype(BF16)
 
 
-def combine_body(part_ref, q_ref, fk_ref, fv_ref, out_ref):
+def combine_body(part_ref, q_ref, fresh_ref, out_ref):
     count = part_ref.shape[0]
     best = jnp.full((GROUP, LANES), NEG, F32)
     for d in range(count):
         best = jnp.maximum(best, part_ref[d].astype(F32)[2 * GROUP :])
-    fk, fv = fk_ref[...].astype(F32), fv_ref[...].astype(F32)
+    fk, fv = fresh_ref[0], fresh_ref[1]
     q = q_ref[...].astype(F32)
     tops, totals, accs = [], [], []
     for par in range(2):
@@ -372,19 +395,26 @@
     )(lengths, block_table)
 
     packed, my_queries = call(
-        pack_body, (shape((ring, 2 * GROUP, HD), BF16), shape((2 * GROUP, HD), BF16)), [VMEM]
+        pack_body,
+        (shape((ring, 2 * GROUP, HD), BF16), shape((2 * GROUP, HD), BF16)),
+        [HBM],
+        [pltpu.VMEM(queries.shape, BF16), pltpu.SemaphoreType.DMA(())],
     )(queries)
     all_queries = exchange(packed, RING)
     all_queries = lax.all_gather(all_queries, "core", axis=0, tiled=False)
     scratch = [pltpu.VMEM((reqs, GROUP, LANES), F32)] * 3
-    scratch += [pltpu.VMEM(key_cache.shape, BF16)] * 2 + [pltpu.SemaphoreType.DMA((2, CHUNKS))]
-    parts = call(attend_body, shape((ctx, 3 * GROUP, HD), BF16), [SMEM, VMEM, HBM, HBM], scratch)(
-        meta, all_queries, key_cache, value_cache
-    )
+    scratch += [pltpu.VMEM(key_cache.shape, BF16)] * 2 + [pltpu.VMEM(fresh_keys.shape, BF16)] * 2
+    scratch += [pltpu.SemaphoreType.DMA((2, CHUNKS)), pltpu.SemaphoreType.DMA((2,))]
+    parts, fresh = call(
+        attend_body,
+        (pltpu.HBM((ctx, 3 * GROUP, HD), BF16), shape((2,) + fresh_keys.shape, F32)),
+        [SMEM, VMEM] + [HBM] * 4,
+        scratch,
+    )(meta, all_queries, key_cache, value_cache, fresh_keys, fresh_values)
     parts = exchange(parts, CTX)
     parts, mine = lax.optimization_barrier((parts, mine))
-    local = call(combine_body, shape((ring, 2 * GROUP, HD), BF16), [VMEM] * 4)(
-        parts, my_queries, fresh_keys, fresh_values
+    local = call(combine_body, shape((ring, 2 * GROUP, HD), BF16), [VMEM] * 3)(
+        parts, my_queries, fresh
     )
     attended = exchange(local, RING)
     attended, met_core = lax.optimization_barrier((attended, met_core))

time: 161 us -> 161 us (level)
  local copies, waits for them, and re-layouts: 4.34 us -> 2.27 us
    unnamed x24 -> x16, local copies, waits for them, and re-layouts: 4.34 us -> 2.27 us
where the time goes in v10:
time: 161 us; the launch traced here: 160 us
  blocking collectives  90.3 us (56%)
  starting transfers between devices  33 us (20%)
  waiting for transfers between devices  18.9 us (12%)
  Pallas kernels  15.1 us (9%)
  local copies, waits for them, and re-layouts  2.27 us (1%)
    all_to_all x4, blocking collectives, exchange(): return lax.all_to_all(x, axes, 0, 0, tiled=True)  77.6 us
    all_to_all x3, starting transfers between devices, exchange(): return lax.all_to_all(x, axes, 0, 0, tiled=True)  22.4 us
    all_to_all x3, waiting for transfers between devices, exchange(): return lax.all_to_all(x, axes, 0, 0, tiled=True)  18.8 us
    pallas_call x11, Pallas kernels, run(): return kernel(*placed)  15.1 us
    all_gather x1, blocking collectives, shards(): pay = lax.all_gather(pay, TEAM, axis=0, tiled=False)  8.95 us
    ppermute x2, starting transfers between devices, shards(): lax.ppermute(block, TEAM, [(i, i ^ flip) for i in range(team)])  6.24 us
    all_gather x1, blocking collectives, shards(): all_queries = lax.all_gather(all_queries, 'core', axis=0, tiled=False)  3.81 us
  transfers between devices with their start and end apart: 7, of which 3 were waited for; matrix products, arithmetic and copies ran while one was open for 0% of the time, Pallas kernels for 4%

profile of v10, /device:TPU:1, one launch (start us, length us, event | category | flops | bytes accessed | tf_op | source)
XLA Modules:
  0.0 159.8 jit_solution(3216975866831894675)
XLA Ops:
  0.0 1.4 shard_map.137
  1.4 13.5 %all-to-all-start = ((bf16[32,16,128]{2,1,0:T(8,128)(2,1)}), bf16[32,16,128]{2,1,0:T(8,128)(2,1)S(1)}, u32[]{:S(2)}, u32[]{:S(2)}) async-start(bf16[32,16,128]{2,1,0:T(8,128)(2,1)} %get-tuple-element.21), calls=%async_computation | async-start | bytes 262144 | tf_op jit(solution)/shard_map/all_to_all | solution.py:32
  14.9 2.0 %shard_map.136.meta_ref = s32[48]{0:T(128)S(1)} custom-call(s32[128]{0:T(128)} %len_hbm.1, s32[128,128]{1,0:T(8,128)} %table_hbm.1), custom_call_target="tpu_custom_call" | custom-call | tf_op jit(solution)/shard_map/pallas_call | solution.py:54
  16.8 8.0 %all-to-all-done = bf16[32,16,128]{2,1,0:T(8,128)(2,1)S(1)} async-done(((bf16[32,16,128]{2,1,0:T(8,128)(2,1)}), bf16[32,16,128]{2,1,0:T(8,128)(2,1)S(1)}, u32[]{:S(2)}, u32[]{:S(2)}) %all-to-all-start) | async-done | bytes 131104 | tf_op jit(solution)/shard_map/all_to_all | solution.py:32
  24.8 3.8 %all-gather = bf16[64,16,128]{2,1,0:T(8,128)(2,1)S(1)} all-gather(bf16[32,16,128]{2,1,0:T(8,128)(2,1)S(1)} %all-to-all-done), channel_id=2, replica_groups=mesh['yh'=4,'yl'=2,'zl'=4,'core'=2,'zh'=2,'x'=4] {'core'}, dimensions={0}, use_global_device_ids=true | all-gather | bytes 393216 | tf_op jit(solution)/shard_map/all_gather | solution.py:404
  28.6 3.8 %shard_map.138 = (bf16[64,24,128]{2,1,0:T(8,128)(2,1)}, f32[2,2,128]{2,1,0:T(2,128)S(1)}) custom-call(s32[48]{0:T(128)S(1)} %shard_map.136.meta_ref, bf16[2,32,16,128]{3,2,1,0:T(8,128)(2,1)S(1)} %bitcast.10, bf16[24,128,128]{2,1,0:T(8,128)(2,1)} %k_hbm.1, bf16[24,128,128]{2,1,0:T(8,128)(2,1)} %v_hbm.1, bf16[2,128]{1,0:T(2,128)(2,1)} %fk_hbm.1, ...), custom_call_target="tpu_custom_call" | custom-call | tf_op jit(solution)/shard_map/pallas_call | solution.py:54
  32.5 0.0 copy-start.4
  32.5 4.4 %all-to-all-start.1 = ((bf16[64,24,128]{2,1,0:T(8,128)(2,1)}), bf16[64,24,128]{2,1,0:T(8,128)(2,1)S(1)}, u32[]{:S(2)}, u32[]{:S(2)}) async-start(bf16[64,24,128]{2,1,0:T(8,128)(2,1)} %get-tuple-element.22), calls=%async_computation.1 | async-start | bytes 786432 | tf_op jit(solution)/shard_map/all_to_all | solution.py:32
  36.9 0.0 copy-start.5
  37.0 0.6 copy-done.5
  37.6 1.3 shard_map.139
  38.8 0.8 copy-done.6
  39.6 0.8 copy-done.7
  40.5 2.5 %collective-permute-start = (bf16[30,128,128]{2,1,0:T(8,128)(2,1)}, bf16[30,128,128]{2,1,0:T(8,128)(2,1)S(1)}, u32[]{:S(2)}, u32[]{:S(2)}) collective-permute-start(bf16[30,128,128]{2,1,0:T(8,128)(2,1)} %get-tuple-element.27), channel_id=1, source_target_pairs={{0,8},{8,0},{1,9},{9,1},{2,10},{10,2},{3,11},{11,3},{4,12},{12,4},... | collective-permute-start | bytes 2949128 | tf_op jit(solution)/shard_map/ppermute | solution.py:383
  42.9 1.9 %collective-permute-start.1 = (bf16[1024,128]{1,0:T(8,128)(2,1)}, bf16[1024,128]{1,0:T(8,128)(2,1)}, u32[]{:S(2)}, u32[]{:S(2)}) collective-permute-start(bf16[1024,128]{1,0:T(8,128)(2,1)} %w_ref.2), channel_id=1, source_target_pairs={{0,8},{8,0},{1,9},{9,1},{2,10},{10,2},{3,11},{11,3},{4,12},{12,4},... | collective-permute-start | bytes 786440 | tf_op jit(solution)/shard_map/ppermute | solution.py:384
  44.9 7.2 %all-to-all-done.1.part_ref = bf16[64,24,128]{2,1,0:T(8,128)(2,1)S(1)} async-done(((bf16[64,24,128]{2,1,0:T(8,128)(2,1)}), bf16[64,24,128]{2,1,0:T(8,128)(2,1)S(1)}, u32[]{:S(2)}, u32[]{:S(2)}) %all-to-all-start.1) | async-done | bytes 393248 | tf_op jit(solution)/shard_map/all_to_all | solution.py:32
  52.1 1.6 %shard_map.140 = bf16[32,16,128]{2,1,0:T(8,128)(2,1)} custom-call(bf16[64,24,128]{2,1,0:T(8,128)(2,1)S(1)} %all-to-all-done.1.part_ref, bf16[16,128]{1,0:T(8,128)(2,1)S(1)} %get-tuple-element.25.q_ref, f32[2,2,128]{2,1,0:T(2,128)S(1)} %get-tuple-element.26.fresh_ref), custom_call_target="tpu_custom_call" | custom-call | tf_op jit(solution)/shard_map/pallas_call | solution.py:54
  53.7 4.5 %all-to-all-start.2 = ((bf16[32,16,128]{2,1,0:T(8,128)(2,1)}), bf16[32,16,128]{2,1,0:T(8,128)(2,1)S(1)}, u32[]{:S(2)}, u32[]{:S(2)}) async-start(bf16[32,16,128]{2,1,0:T(8,128)(2,1)} %shard_map.140), calls=%async_computation.2 | async-start | bytes 262144 | tf_op jit(solution)/shard_map/all_to_all | solution.py:32
  58.2 3.1 %collective-permute-start.2 = (bf16[16,128,128]{2,1,0:T(8,128)(2,1)}, bf16[16,128,128]{2,1,0:T(8,128)(2,1)S(1)}, u32[]{:S(2)}, u32[]{:S(2)}) collective-permute-start(bf16[16,128,128]{2,1,0:T(8,128)(2,1)} %copy-done.7), channel_id=1, source_target_pairs={{0,64},{8,72},{64,0},{72,8},{1,65},{9,73},{65,1},{73,9},{2,66},{10... | collective-permute-start | bytes 1572872 | tf_op jit(solution)/shard_map/ppermute | solution.py:380
  61.3 3.1 %collective-permute-start.3 = (bf16[16,128,128]{2,1,0:T(8,128)(2,1)}, bf16[16,128,128]{2,1,0:T(8,128)(2,1)}, u32[]{:S(2)}, u32[]{:S(2)}) collective-permute-start(bf16[16,128,128]{2,1,0:T(8,128)(2,1)} %copy-done.6), channel_id=1, source_target_pairs={{0,72},{8,64},{64,8},{72,0},{1,73},{9,65},{65,9},{73,1},{2,74},{10... | collective-permute-start | bytes 1572872 | tf_op jit(solution)/shard_map/ppermute | solution.py:380
  64.4 0.0 collective-permute-done.met1_ref.met_ref
  64.4 3.7 %all-to-all-done.2.att_ref = bf16[32,16,128]{2,1,0:T(8,128)(2,1)S(1)} async-done(((bf16[32,16,128]{2,1,0:T(8,128)(2,1)}), bf16[32,16,128]{2,1,0:T(8,128)(2,1)S(1)}, u32[]{:S(2)}, u32[]{:S(2)}) %all-to-all-start.2) | async-done | bytes 131104 | tf_op jit(solution)/shard_map/all_to_all | solution.py:32
  68.1 1.4 shard_map.141
  69.5 19.5 %all_to_all.35.part_ref = bf16[8,128,128]{2,1,0:T(8,128)(2,1)S(1)} all-to-all(bf16[8,128,128]{2,1,0:T(8,128)(2,1)S(1)} %bitcast.9), channel_id=1, replica_groups=mesh['yh'=4,'yl'=2,'zl'=4,'core'=2,'zh'=2,'x'=4] {'zh','x'}, dimensions={0} | all-to-all | bytes 524288 | tf_op jit(solution)/shard_map/all_to_all | solution.py:32
  89.1 8.9 %all-gather.1 = bf16[512,128]{1,0:T(8,128)(2,1)S(1)} all-gather(bf16[128,128]{1,0:T(8,128)(2,1)S(1)} %shard_map.142), channel_id=3, replica_groups=mesh['yh'=4,'yl'=2,'zl'=4,'core'=2,'zh'=2,'x'=4] {'yl','core'}, dimensions={0}, use_global_device_ids=true | all-gather | bytes 163840 | tf_op jit(solution)/shard_map/all_gather | solution.py:429
  98.0 1.7 %shard_map.143 = (bf16[16,120,128]{2,1,0:T(8,128)(2,1)S(1)}, bf16[128,128]{1,0:T(8,128)(2,1)S(1)}) custom-call(bf16[2,2,2,64,128]{4,3,2,1,0:T(8,128)(2,1)S(1)} %bitcast.11, bf16[2,128,128]{2,1,0:T(8,128)(2,1)S(1)} %get-tuple-element.29.mine_ref, bf16[128,3584]{1,0:T(8,128)(2,1)S(1)} %copy-done.1, bf16[128,3584]{1,0:T(8,128)(2,1)S(1)} %copy-done.3, ...), custom_call_target="tpu_custom_call" | custom-call | tf_op jit(solution)/shard_map/pallas_call | solution.py:54
  99.7 21.3 %all_to_all.36.part_ref = bf16[16,120,128]{2,1,0:T(8,128)(2,1)S(1)} all-to-all(bf16[16,120,128]{2,1,0:T(8,128)(2,1)S(1)} %get-tuple-element.33), channel_id=1, replica_groups=mesh['yh'=4,'yl'=2,'zl'=4,'core'=2,'zh'=2,'x'=4] {'yh','zl'}, dimensions={0} | all-to-all | bytes 983040 | tf_op jit(solution)/shard_map/all_to_all | solution.py:32
  121.1 0.2 shard_map.144
  121.3 21.4 %all_to_all.37 = bf16[32,56,128]{2,1,0:T(8,128)(2,1)S(1)} all-to-all(bf16[32,56,128]{2,1,0:T(8,128)(2,1)S(1)} %shard_map.144), channel_id=1, replica_groups=mesh['yh'=4,'yl'=2,'zl'=4,'core'=2,'zh'=2,'x'=4] {'yh','yl','zl'}, dimensions={0} | all-to-all | bytes 917504 | tf_op jit(solution)/shard_map/all_to_all | solution.py:32
  142.6 1.2 shard_map.145
  143.8 15.4 %all_to_all.38.part_ref = bf16[16,16,128]{2,1,0:T(8,128)(2,1)S(1)} all-to-all(bf16[16,16,128]{2,1,0:T(8,128)(2,1)S(1)} %bitcast.12), channel_id=1, replica_groups=mesh['yh'=4,'yl'=2,'zl'=4,'core'=2,'zh'=2,'x'=4] {'core','zh','x'}, dimensions={0} | all-to-all | bytes 131072 | tf_op jit(solution)/shard_map/all_to_all | solution.py:32
  159.1 0.6 shard_map.146
  (15 shorter events, 0.1 us)
Async XLA Ops:
  1.4 23.4 %all-to-all-start = ((bf16[32,16,128]{2,1,0:T(8,128)(2,1)}), bf16[32,16,128]{2,1,0:T(8,128)(2,1)S(1)}, u32[]{:S(2)}, u32[]{:S(2)}) async-start(bf16[32,16,128]{2,1,0:T(8,128)(2,1)} %get-tuple-element.21), calls=%async_computation | async-start | bytes 262144 | tf_op jit(solution)/shard_map/all_to_all | solution.py:32
  24.8 12.1 %copy-start.2 = (bf16[128,3584]{1,0:T(8,128)(2,1)S(1)}, bf16[128,3584]{1,0:T(8,128)(2,1)}, u32[]{:S(2)}) copy-start(bf16[128,3584]{1,0:T(8,128)(2,1)} %up_ref.3) | copy-start | bytes 2752516
  28.6 8.3 %copy-start = (bf16[3584,128]{1,0:T(8,128)(2,1)S(1)}, bf16[3584,128]{1,0:T(8,128)(2,1)}, u32[]{:S(2)}) copy-start(bf16[3584,128]{1,0:T(8,128)(2,1)} %w_ref.3) | copy-start | bytes 2752516
  28.6 8.3 %copy-start.1 = (bf16[128,3584]{1,0:T(8,128)(2,1)S(1)}, bf16[128,3584]{1,0:T(8,128)(2,1)}, u32[]{:S(2)}) copy-start(bf16[128,3584]{1,0:T(8,128)(2,1)} %gate_ref.3) | copy-start | bytes 2752516
  32.5 4.5 %copy-start.4 = (bf16[128,128]{1,0:T(8,128)(2,1)S(1)}, bf16[128,128]{1,0:T(8,128)(2,1)}, u32[]{:S(2)}) copy-start(bf16[128,128]{1,0:T(8,128)(2,1)} %resid_ref.1) | copy-start | bytes 98308
  32.5 19.6 %all-to-all-start.1 = ((bf16[64,24,128]{2,1,0:T(8,128)(2,1)}), bf16[64,24,128]{2,1,0:T(8,128)(2,1)S(1)}, u32[]{:S(2)}, u32[]{:S(2)}) async-start(bf16[64,24,128]{2,1,0:T(8,128)(2,1)} %get-tuple-element.22), calls=%async_computation.1 | async-start | bytes 786432 | tf_op jit(solution)/shard_map/all_to_all | solution.py:32
  36.9 0.7 copy-start.5
  38.8 0.8 copy-start.6
  39.6 0.8 copy-start.7
  40.5 24.0 %collective-permute-start = (bf16[30,128,128]{2,1,0:T(8,128)(2,1)}, bf16[30,128,128]{2,1,0:T(8,128)(2,1)S(1)}, u32[]{:S(2)}, u32[]{:S(2)}) collective-permute-start(bf16[30,128,128]{2,1,0:T(8,128)(2,1)} %get-tuple-element.27), channel_id=1, source_target_pairs={{0,8},{8,0},{1,9},{9,1},{2,10},{10,2},{3,11},{11,3},{4,12},{12,4},... | collective-permute-start | bytes 2949128 | tf_op jit(solution)/shard_map/ppermute | solution.py:383
  42.9 25.2 %collective-permute-start.1 = (bf16[1024,128]{1,0:T(8,128)(2,1)}, bf16[1024,128]{1,0:T(8,128)(2,1)}, u32[]{:S(2)}, u32[]{:S(2)}) collective-permute-start(bf16[1024,128]{1,0:T(8,128)(2,1)} %w_ref.2), channel_id=1, source_target_pairs={{0,8},{8,0},{1,9},{9,1},{2,10},{10,2},{3,11},{11,3},{4,12},{12,4},... | collective-permute-start | bytes 786440 | tf_op jit(solution)/shard_map/ppermute | solution.py:384
  53.7 14.4 %all-to-all-start.2 = ((bf16[32,16,128]{2,1,0:T(8,128)(2,1)}), bf16[32,16,128]{2,1,0:T(8,128)(2,1)S(1)}, u32[]{:S(2)}, u32[]{:S(2)}) async-start(bf16[32,16,128]{2,1,0:T(8,128)(2,1)} %shard_map.140), calls=%async_computation.2 | async-start | bytes 262144 | tf_op jit(solution)/shard_map/all_to_all | solution.py:32
  58.2 39.8 %collective-permute-start.2 = (bf16[16,128,128]{2,1,0:T(8,128)(2,1)}, bf16[16,128,128]{2,1,0:T(8,128)(2,1)S(1)}, u32[]{:S(2)}, u32[]{:S(2)}) collective-permute-start(bf16[16,128,128]{2,1,0:T(8,128)(2,1)} %copy-done.7), channel_id=1, source_target_pairs={{0,64},{8,72},{64,0},{72,8},{1,65},{9,73},{65,1},{73,9},{2,66},{10... | collective-permute-start | bytes 1572872 | tf_op jit(solution)/shard_map/ppermute | solution.py:380
  61.3 36.7 %collective-permute-start.3 = (bf16[16,128,128]{2,1,0:T(8,128)(2,1)}, bf16[16,128,128]{2,1,0:T(8,128)(2,1)}, u32[]{:S(2)}, u32[]{:S(2)}) collective-permute-start(bf16[16,128,128]{2,1,0:T(8,128)(2,1)} %copy-done.6), channel_id=1, source_target_pairs={{0,72},{8,64},{64,8},{72,0},{1,73},{9,65},{65,9},{73,1},{2,74},{10... | collective-permute-start | bytes 1572872 | tf_op jit(solution)/shard_map/ppermute | solution.py:380
  68.1 29.9 %copy-start.3 = (bf16[128,3584]{1,0:T(8,128)(2,1)S(1)}, bf16[128,3584]{1,0:T(8,128)(2,1)}, u32[]{:S(2)}) copy-start(bf16[128,3584]{1,0:T(8,128)(2,1)} %up_ref.3) | copy-start | bytes 2752516

commit v11 on v10

--- a/solution.py
+++ b/solution.py
@@ -369,8 +369,8 @@
             for flip, block in enumerate(blocks_out, 1)
         ]
 
-    bundle = shape((2 * blocks + 2, LANES, LANES), BF16)
-    core_bundle = shape((4 * blocks + 2, LANES, LANES), BF16)
+    bundle = pltpu.HBM((2 * blocks + 2, LANES, LANES), BF16)
+    core_bundle = pltpu.HBM((4 * blocks + 2, LANES, LANES), BF16)
     mine, given_core, *given = call(
         functools.partial(cut_body, ring),
         (shape((2, LANES, LANES), BF16), core_bundle, bundle, bundle),
@@ -417,7 +417,7 @@
         parts, my_queries, fresh
     )
     attended = exchange(local, RING)
-    attended, met_core = lax.optimization_barrier((attended, met_core))
+    attended, met_core, met[0] = lax.optimization_barrier((attended, met_core, met[0]))
     projected = call(
         project_body,
         shape((grp, 2, reqs // 2, width), BF16),

time: 161 us -> 159 us (0.988)
  blocking collectives: 90.3 us -> 88.3 us
  local copies, waits for them, and re-layouts: 2.27 us -> 0.63 us
    all_to_all x4, blocking collectives: 77.6 us -> 75.7 us  [exchange(): return lax.all_to_all(x, axes, 0, 0, tiled=True)]
    unnamed x16 -> x12, local copies, waits for them, and re-layouts: 2.27 us -> 0.63 us
where the time goes in v11:
time: 159 us; the launch traced here: 158 us
  blocking collectives  88.3 us (56%)
  starting transfers between devices  34.5 us (22%)
  waiting for transfers between devices  18.9 us (12%)
  Pallas kernels  15.4 us (10%)
    all_to_all x4, blocking collectives, exchange(): return lax.all_to_all(x, axes, 0, 0, tiled=True)  75.7 us
    all_to_all x3, starting transfers between devices, exchange(): return lax.all_to_all(x, axes, 0, 0, tiled=True)  22.2 us
    all_to_all x3, waiting for transfers between devices, exchange(): return lax.all_to_all(x, axes, 0, 0, tiled=True)  18.9 us
    pallas_call x11, Pallas kernels, run(): return kernel(*placed)  15.4 us
    all_gather x1, blocking collectives, shards(): pay = lax.all_gather(pay, TEAM, axis=0, tiled=False)  8.82 us
    ppermute x2, starting transfers between devices, shards(): lax.ppermute(block, TEAM, [(i, i ^ flip) for i in range(team)])  7.42 us
    all_gather x1, blocking collectives, shards(): all_queries = lax.all_gather(all_queries, 'core', axis=0, tiled=False)  3.81 us
  transfers between devices with their start and end apart: 7, of which 3 were waited for; matrix products, arithmetic and copies ran while one was open for 0% of the time, Pallas kernels for 4%

profile of v11, /device:TPU:1, one launch (start us, length us, event | category | flops | bytes accessed | tf_op | source)
XLA Modules:
  0.0 157.9 jit_solution(13402337370056383703)
XLA Ops:
  0.0 1.4 shard_map.137
  1.4 13.5 %all-to-all-start = ((bf16[32,16,128]{2,1,0:T(8,128)(2,1)}), bf16[32,16,128]{2,1,0:T(8,128)(2,1)S(1)}, u32[]{:S(2)}, u32[]{:S(2)}) async-start(bf16[32,16,128]{2,1,0:T(8,128)(2,1)} %get-tuple-element.22), calls=%async_computation | async-start | bytes 262144 | tf_op jit(solution)/shard_map/all_to_all | solution.py:32
  14.9 2.0 %shard_map.136.meta_ref = s32[48]{0:T(128)S(1)} custom-call(s32[128]{0:T(128)} %len_hbm.1, s32[128,128]{1,0:T(8,128)} %table_hbm.1), custom_call_target="tpu_custom_call" | custom-call | tf_op jit(solution)/shard_map/pallas_call | solution.py:54
  16.8 8.0 %all-to-all-done = bf16[32,16,128]{2,1,0:T(8,128)(2,1)S(1)} async-done(((bf16[32,16,128]{2,1,0:T(8,128)(2,1)}), bf16[32,16,128]{2,1,0:T(8,128)(2,1)S(1)}, u32[]{:S(2)}, u32[]{:S(2)}) %all-to-all-start) | async-done | bytes 131104 | tf_op jit(solution)/shard_map/all_to_all | solution.py:32
  24.8 3.8 %all-gather = bf16[64,16,128]{2,1,0:T(8,128)(2,1)S(1)} all-gather(bf16[32,16,128]{2,1,0:T(8,128)(2,1)S(1)} %all-to-all-done), channel_id=2, replica_groups=mesh['yh'=4,'yl'=2,'zl'=4,'core'=2,'zh'=2,'x'=4] {'core'}, dimensions={0}, use_global_device_ids=true | all-gather | bytes 393216 | tf_op jit(solution)/shard_map/all_gather | solution.py:404
  28.6 3.8 %shard_map.138 = (bf16[64,24,128]{2,1,0:T(8,128)(2,1)}, f32[2,2,128]{2,1,0:T(2,128)S(1)}) custom-call(s32[48]{0:T(128)S(1)} %shard_map.136.meta_ref, bf16[2,32,16,128]{3,2,1,0:T(8,128)(2,1)S(1)} %bitcast.10, bf16[24,128,128]{2,1,0:T(8,128)(2,1)} %k_hbm.1, bf16[24,128,128]{2,1,0:T(8,128)(2,1)} %v_hbm.1, bf16[2,128]{1,0:T(2,128)(2,1)} %fk_hbm.1, ...), custom_call_target="tpu_custom_call" | custom-call | tf_op jit(solution)/shard_map/pallas_call | solution.py:54
  32.5 0.0 copy-start.4
  32.5 4.4 %all-to-all-start.1 = ((bf16[64,24,128]{2,1,0:T(8,128)(2,1)}), bf16[64,24,128]{2,1,0:T(8,128)(2,1)S(1)}, u32[]{:S(2)}, u32[]{:S(2)}) async-start(bf16[64,24,128]{2,1,0:T(8,128)(2,1)} %get-tuple-element.23), calls=%async_computation.1 | async-start | bytes 786432 | tf_op jit(solution)/shard_map/all_to_all | solution.py:32
  36.9 0.0 copy-start.5
  37.0 0.6 copy-done.5
  37.6 1.5 shard_map.139
  39.1 2.5 %collective-permute-start = (bf16[30,128,128]{2,1,0:T(8,128)(2,1)}, bf16[30,128,128]{2,1,0:T(8,128)(2,1)S(1)}, u32[]{:S(2)}, u32[]{:S(2)}) collective-permute-start(bf16[30,128,128]{2,1,0:T(8,128)(2,1)} %get-tuple-element.28), channel_id=1, source_target_pairs={{0,8},{8,0},{1,9},{9,1},{2,10},{10,2},{3,11},{11,3},{4,12},{12,4},... | collective-permute-start | bytes 2949128 | tf_op jit(solution)/shard_map/ppermute | solution.py:383
  41.6 3.1 %collective-permute-start.1 = (bf16[16,128,128]{2,1,0:T(8,128)(2,1)}, bf16[16,128,128]{2,1,0:T(8,128)(2,1)}, u32[]{:S(2)}, u32[]{:S(2)}) collective-permute-start(bf16[16,128,128]{2,1,0:T(8,128)(2,1)} %get-tuple-element.29), channel_id=1, source_target_pairs={{0,64},{8,72},{64,0},{72,8},{1,65},{9,73},{65,1},{73,9},{2,66},{10... | collective-permute-start | bytes 1572872 | tf_op jit(solution)/shard_map/ppermute | solution.py:380
  44.7 2.4 %collective-permute-start.2 = (bf16[1024,128]{1,0:T(8,128)(2,1)}, bf16[1024,128]{1,0:T(8,128)(2,1)}, u32[]{:S(2)}, u32[]{:S(2)}) collective-permute-start(bf16[1024,128]{1,0:T(8,128)(2,1)} %w_ref.2), channel_id=1, source_target_pairs={{0,8},{8,0},{1,9},{9,1},{2,10},{10,2},{3,11},{11,3},{4,12},{12,4},... | collective-permute-start | bytes 786440 | tf_op jit(solution)/shard_map/ppermute | solution.py:384
  47.1 5.3 %all-to-all-done.1.part_ref = bf16[64,24,128]{2,1,0:T(8,128)(2,1)S(1)} async-done(((bf16[64,24,128]{2,1,0:T(8,128)(2,1)}), bf16[64,24,128]{2,1,0:T(8,128)(2,1)S(1)}, u32[]{:S(2)}, u32[]{:S(2)}) %all-to-all-start.1) | async-done | bytes 393248 | tf_op jit(solution)/shard_map/all_to_all | solution.py:32
  52.4 1.6 %shard_map.140 = bf16[32,16,128]{2,1,0:T(8,128)(2,1)} custom-call(bf16[64,24,128]{2,1,0:T(8,128)(2,1)S(1)} %all-to-all-done.1.part_ref, bf16[16,128]{1,0:T(8,128)(2,1)S(1)} %get-tuple-element.26.q_ref, f32[2,2,128]{2,1,0:T(2,128)S(1)} %get-tuple-element.27.fresh_ref), custom_call_target="tpu_custom_call" | custom-call | tf_op jit(solution)/shard_map/pallas_call | solution.py:54
  54.0 4.3 %all-to-all-start.2 = ((bf16[32,16,128]{2,1,0:T(8,128)(2,1)}), bf16[32,16,128]{2,1,0:T(8,128)(2,1)S(1)}, u32[]{:S(2)}, u32[]{:S(2)}) async-start(bf16[32,16,128]{2,1,0:T(8,128)(2,1)} %shard_map.140), calls=%async_computation.2 | async-start | bytes 262144 | tf_op jit(solution)/shard_map/all_to_all | solution.py:32
  58.3 4.3 %collective-permute-start.3 = (bf16[16,128,128]{2,1,0:T(8,128)(2,1)}, bf16[16,128,128]{2,1,0:T(8,128)(2,1)S(1)}, u32[]{:S(2)}, u32[]{:S(2)}) collective-permute-start(bf16[16,128,128]{2,1,0:T(8,128)(2,1)} %get-tuple-element.34), channel_id=1, source_target_pairs={{0,72},{8,64},{64,8},{72,0},{1,73},{9,65},{65,9},{73,1},{2,74},{10... | collective-permute-start | bytes 1572872 | tf_op jit(solution)/shard_map/ppermute | solution.py:380
  62.6 0.0 collective-permute-done.met1_ref.met_ref
  62.6 5.6 %all-to-all-done.2.att_ref = bf16[32,16,128]{2,1,0:T(8,128)(2,1)S(1)} async-done(((bf16[32,16,128]{2,1,0:T(8,128)(2,1)}), bf16[32,16,128]{2,1,0:T(8,128)(2,1)S(1)}, u32[]{:S(2)}, u32[]{:S(2)}) %all-to-all-start.2) | async-done | bytes 131104 | tf_op jit(solution)/shard_map/all_to_all | solution.py:32
  68.3 0.0 collective-permute-done.2.met_ref
  68.3 1.4 shard_map.141
  69.6 19.5 %all_to_all.35.part_ref = bf16[8,128,128]{2,1,0:T(8,128)(2,1)S(1)} all-to-all(bf16[8,128,128]{2,1,0:T(8,128)(2,1)S(1)} %bitcast.9), channel_id=1, replica_groups=mesh['yh'=4,'yl'=2,'zl'=4,'core'=2,'zh'=2,'x'=4] {'zh','x'}, dimensions={0} | all-to-all | bytes 524288 | tf_op jit(solution)/shard_map/all_to_all | solution.py:32
  89.2 8.8 %all-gather.1 = bf16[512,128]{1,0:T(8,128)(2,1)S(1)} all-gather(bf16[128,128]{1,0:T(8,128)(2,1)S(1)} %shard_map.142), channel_id=3, replica_groups=mesh['yh'=4,'yl'=2,'zl'=4,'core'=2,'zh'=2,'x'=4] {'yl','core'}, dimensions={0}, use_global_device_ids=true | all-gather | bytes 163840 | tf_op jit(solution)/shard_map/all_gather | solution.py:429
  98.0 0.0 collective-permute-done.3.met3_ref
  98.0 1.7 %shard_map.143 = (bf16[16,120,128]{2,1,0:T(8,128)(2,1)S(1)}, bf16[128,128]{1,0:T(8,128)(2,1)S(1)}) custom-call(bf16[2,2,2,64,128]{4,3,2,1,0:T(8,128)(2,1)S(1)} %bitcast.11, bf16[2,128,128]{2,1,0:T(8,128)(2,1)S(1)} %get-tuple-element.31.mine_ref, bf16[128,3584]{1,0:T(8,128)(2,1)S(1)} %copy-done.1, bf16[128,3584]{1,0:T(8,128)(2,1)S(1)} %copy-done.3, ...), custom_call_target="tpu_custom_call" | custom-call | tf_op jit(solution)/shard_map/pallas_call | solution.py:54
  99.7 17.2 %all_to_all.36.part_ref = bf16[16,120,128]{2,1,0:T(8,128)(2,1)S(1)} all-to-all(bf16[16,120,128]{2,1,0:T(8,128)(2,1)S(1)} %get-tuple-element.35), channel_id=1, replica_groups=mesh['yh'=4,'yl'=2,'zl'=4,'core'=2,'zh'=2,'x'=4] {'yh','zl'}, dimensions={0} | all-to-all | bytes 983040 | tf_op jit(solution)/shard_map/all_to_all | solution.py:32
  117.0 0.2 shard_map.144
  117.2 23.6 %all_to_all.37 = bf16[32,56,128]{2,1,0:T(8,128)(2,1)S(1)} all-to-all(bf16[32,56,128]{2,1,0:T(8,128)(2,1)S(1)} %shard_map.144), channel_id=1, replica_groups=mesh['yh'=4,'yl'=2,'zl'=4,'core'=2,'zh'=2,'x'=4] {'yh','yl','zl'}, dimensions={0} | all-to-all | bytes 917504 | tf_op jit(solution)/shard_map/all_to_all | solution.py:32
  140.8 1.2 shard_map.145
  141.9 15.3 %all_to_all.38.part_ref = bf16[16,16,128]{2,1,0:T(8,128)(2,1)S(1)} all-to-all(bf16[16,16,128]{2,1,0:T(8,128)(2,1)S(1)} %bitcast.12), channel_id=1, replica_groups=mesh['yh'=4,'yl'=2,'zl'=4,'core'=2,'zh'=2,'x'=4] {'core','zh','x'}, dimensions={0} | all-to-all | bytes 131072 | tf_op jit(solution)/shard_map/all_to_all | solution.py:32
  157.2 0.6 shard_map.146
  (11 shorter events, 0.1 us)
Async XLA Ops:
  1.4 23.4 %all-to-all-start = ((bf16[32,16,128]{2,1,0:T(8,128)(2,1)}), bf16[32,16,128]{2,1,0:T(8,128)(2,1)S(1)}, u32[]{:S(2)}, u32[]{:S(2)}) async-start(bf16[32,16,128]{2,1,0:T(8,128)(2,1)} %get-tuple-element.22), calls=%async_computation | async-start | bytes 262144 | tf_op jit(solution)/shard_map/all_to_all | solution.py:32
  24.8 12.1 %copy-start.2 = (bf16[128,3584]{1,0:T(8,128)(2,1)S(1)}, bf16[128,3584]{1,0:T(8,128)(2,1)}, u32[]{:S(2)}) copy-start(bf16[128,3584]{1,0:T(8,128)(2,1)} %up_ref.3) | copy-start | bytes 2752516
  28.6 8.3 %copy-start = (bf16[3584,128]{1,0:T(8,128)(2,1)S(1)}, bf16[3584,128]{1,0:T(8,128)(2,1)}, u32[]{:S(2)}) copy-start(bf16[3584,128]{1,0:T(8,128)(2,1)} %w_ref.3) | copy-start | bytes 2752516
  28.6 8.3 %copy-start.1 = (bf16[128,3584]{1,0:T(8,128)(2,1)S(1)}, bf16[128,3584]{1,0:T(8,128)(2,1)}, u32[]{:S(2)}) copy-start(bf16[128,3584]{1,0:T(8,128)(2,1)} %gate_ref.3) | copy-start | bytes 2752516
  32.5 4.5 %copy-start.4 = (bf16[128,128]{1,0:T(8,128)(2,1)S(1)}, bf16[128,128]{1,0:T(8,128)(2,1)}, u32[]{:S(2)}) copy-start(bf16[128,128]{1,0:T(8,128)(2,1)} %resid_ref.1) | copy-start | bytes 98308
  32.5 19.9 %all-to-all-start.1 = ((bf16[64,24,128]{2,1,0:T(8,128)(2,1)}), bf16[64,24,128]{2,1,0:T(8,128)(2,1)S(1)}, u32[]{:S(2)}, u32[]{:S(2)}) async-start(bf16[64,24,128]{2,1,0:T(8,128)(2,1)} %get-tuple-element.23), calls=%async_computation.1 | async-start | bytes 786432 | tf_op jit(solution)/shard_map/all_to_all | solution.py:32
  36.9 0.7 copy-start.5
  39.1 23.5 %collective-permute-start = (bf16[30,128,128]{2,1,0:T(8,128)(2,1)}, bf16[30,128,128]{2,1,0:T(8,128)(2,1)S(1)}, u32[]{:S(2)}, u32[]{:S(2)}) collective-permute-start(bf16[30,128,128]{2,1,0:T(8,128)(2,1)} %get-tuple-element.28), channel_id=1, source_target_pairs={{0,8},{8,0},{1,9},{9,1},{2,10},{10,2},{3,11},{11,3},{4,12},{12,4},... | collective-permute-start | bytes 2949128 | tf_op jit(solution)/shard_map/ppermute | solution.py:383
  41.6 21.1 %collective-permute-start.1 = (bf16[16,128,128]{2,1,0:T(8,128)(2,1)}, bf16[16,128,128]{2,1,0:T(8,128)(2,1)}, u32[]{:S(2)}, u32[]{:S(2)}) collective-permute-start(bf16[16,128,128]{2,1,0:T(8,128)(2,1)} %get-tuple-element.29), channel_id=1, source_target_pairs={{0,64},{8,72},{64,0},{72,8},{1,65},{9,73},{65,1},{73,9},{2,66},{10... | collective-permute-start | bytes 1572872 | tf_op jit(solution)/shard_map/ppermute | solution.py:380
  44.7 23.6 %collective-permute-start.2 = (bf16[1024,128]{1,0:T(8,128)(2,1)}, bf16[1024,128]{1,0:T(8,128)(2,1)}, u32[]{:S(2)}, u32[]{:S(2)}) collective-permute-start(bf16[1024,128]{1,0:T(8,128)(2,1)} %w_ref.2), channel_id=1, source_target_pairs={{0,8},{8,0},{1,9},{9,1},{2,10},{10,2},{3,11},{11,3},{4,12},{12,4},... | collective-permute-start | bytes 786440 | tf_op jit(solution)/shard_map/ppermute | solution.py:384
  54.0 14.3 %all-to-all-start.2 = ((bf16[32,16,128]{2,1,0:T(8,128)(2,1)}), bf16[32,16,128]{2,1,0:T(8,128)(2,1)S(1)}, u32[]{:S(2)}, u32[]{:S(2)}) async-start(bf16[32,16,128]{2,1,0:T(8,128)(2,1)} %shard_map.140), calls=%async_computation.2 | async-start | bytes 262144 | tf_op jit(solution)/shard_map/all_to_all | solution.py:32
  58.3 39.7 %collective-permute-start.3 = (bf16[16,128,128]{2,1,0:T(8,128)(2,1)}, bf16[16,128,128]{2,1,0:T(8,128)(2,1)S(1)}, u32[]{:S(2)}, u32[]{:S(2)}) collective-permute-start(bf16[16,128,128]{2,1,0:T(8,128)(2,1)} %get-tuple-element.34), channel_id=1, source_target_pairs={{0,72},{8,64},{64,8},{72,0},{1,73},{9,65},{65,9},{73,1},{2,74},{10... | collective-permute-start | bytes 1572872 | tf_op jit(solution)/shard_map/ppermute | solution.py:380
  68.3 29.8 %copy-start.3 = (bf16[128,3584]{1,0:T(8,128)(2,1)S(1)}, bf16[128,3584]{1,0:T(8,128)(2,1)}, u32[]{:S(2)}) copy-start(bf16[128,3584]{1,0:T(8,128)(2,1)} %up_ref.3) | copy-start | bytes 2752516

commit v12 on v11

--- a/solution.py
+++ b/solution.py
@@ -154,10 +154,8 @@
     top_ref[...] = jnp.full(top_ref.shape, NEG, F32)
     sum_ref[...] = jnp.zeros(sum_ref.shape, F32)
     acc_ref[...] = jnp.zeros(acc_ref.shape, F32)
-    for fetch in fetches:
+    for fetch in fetches[:CHUNKS]:
         fetch.wait()
-    fresh_ref[0] = fk_ref[...].astype(F32)
-    fresh_ref[1] = fv_ref[...].astype(F32)
     lane = lane_ids((GROUP, page))
     owners, scores = [], []
     for s in range(slots):
@@ -171,6 +169,10 @@
         top_ref[owner] = jnp.maximum(top_ref[owner], jnp.broadcast_to(best, (GROUP, LANES)))
         owners.append(owner)
         scores.append(score)
+    for fetch in fetches[CHUNKS:]:
+        fetch.wait()
+    fresh_ref[0] = fk_ref[...].astype(F32)
+    fresh_ref[1] = fv_ref[...].astype(F32)
     for s in range(slots):
         owner = owners[s]
         shift = top_ref[owner].astype(BF16).astype(F32)

time: 159 us -> 158 us (level)
  no operation moved by 1% of the time
where the time goes in v12:
time: 158 us
  blocking collectives  88.3 us (56%)
  starting transfers between devices  34.5 us (22%)
  waiting for transfers between devices  18.9 us (12%)
  Pallas kernels  15.2 us (10%)
    all_to_all x4, blocking collectives, exchange(): return lax.all_to_all(x, axes, 0, 0, tiled=True)  75.7 us
    all_to_all x3, starting transfers between devices, exchange(): return lax.all_to_all(x, axes, 0, 0, tiled=True)  22.2 us
    all_to_all x3, waiting for transfers between devices, exchange(): return lax.all_to_all(x, axes, 0, 0, tiled=True)  18.9 us
    pallas_call x11, Pallas kernels, run(): return kernel(*placed)  15.2 us
    all_gather x1, blocking collectives, shards(): pay = lax.all_gather(pay, TEAM, axis=0, tiled=False)  8.82 us
    ppermute x2, starting transfers between devices, shards(): lax.ppermute(block, TEAM, [(i, i ^ flip) for i in range(team)])  7.42 us
    all_gather x1, blocking collectives, shards(): all_queries = lax.all_gather(all_queries, 'core', axis=0, tiled=False)  3.81 us
  transfers between devices with their start and end apart: 7, of which 3 were waited for; matrix products, arithmetic and copies ran while one was open for 0% of the time, Pallas kernels for 4%

profile of v12, /device:TPU:1, one launch (start us, length us, event | category | flops | bytes accessed | tf_op | source)
XLA Modules:
  0.0 157.7 jit_solution(5634255639199168476)
XLA Ops:
  0.0 1.4 shard_map.137
  1.4 13.5 %all-to-all-start = ((bf16[32,16,128]{2,1,0:T(8,128)(2,1)}), bf16[32,16,128]{2,1,0:T(8,128)(2,1)S(1)}, u32[]{:S(2)}, u32[]{:S(2)}) async-start(bf16[32,16,128]{2,1,0:T(8,128)(2,1)} %get-tuple-element.22), calls=%async_computation | async-start | bytes 262144 | tf_op jit(solution)/shard_map/all_to_all | solution.py:32
  14.9 2.0 %shard_map.136.meta_ref = s32[48]{0:T(128)S(1)} custom-call(s32[128]{0:T(128)} %len_hbm.1, s32[128,128]{1,0:T(8,128)} %table_hbm.1), custom_call_target="tpu_custom_call" | custom-call | tf_op jit(solution)/shard_map/pallas_call | solution.py:54
  16.8 8.0 %all-to-all-done = bf16[32,16,128]{2,1,0:T(8,128)(2,1)S(1)} async-done(((bf16[32,16,128]{2,1,0:T(8,128)(2,1)}), bf16[32,16,128]{2,1,0:T(8,128)(2,1)S(1)}, u32[]{:S(2)}, u32[]{:S(2)}) %all-to-all-start) | async-done | bytes 131104 | tf_op jit(solution)/shard_map/all_to_all | solution.py:32
  24.8 3.8 %all-gather = bf16[64,16,128]{2,1,0:T(8,128)(2,1)S(1)} all-gather(bf16[32,16,128]{2,1,0:T(8,128)(2,1)S(1)} %all-to-all-done), channel_id=2, replica_groups=mesh['yh'=4,'yl'=2,'zl'=4,'core'=2,'zh'=2,'x'=4] {'core'}, dimensions={0}, use_global_device_ids=true | all-gather | bytes 393216 | tf_op jit(solution)/shard_map/all_gather | solution.py:406
  28.6 3.6 %shard_map.138 = (bf16[64,24,128]{2,1,0:T(8,128)(2,1)}, f32[2,2,128]{2,1,0:T(2,128)S(1)}) custom-call(s32[48]{0:T(128)S(1)} %shard_map.136.meta_ref, bf16[2,32,16,128]{3,2,1,0:T(8,128)(2,1)S(1)} %bitcast.10, bf16[24,128,128]{2,1,0:T(8,128)(2,1)} %k_hbm.1, bf16[24,128,128]{2,1,0:T(8,128)(2,1)} %v_hbm.1, bf16[2,128]{1,0:T(2,128)(2,1)} %fk_hbm.1, ...), custom_call_target="tpu_custom_call" | custom-call | tf_op jit(solution)/shard_map/pallas_call | solution.py:54
  32.2 0.0 copy-start.4
  32.2 4.4 %all-to-all-start.1 = ((bf16[64,24,128]{2,1,0:T(8,128)(2,1)}), bf16[64,24,128]{2,1,0:T(8,128)(2,1)S(1)}, u32[]{:S(2)}, u32[]{:S(2)}) async-start(bf16[64,24,128]{2,1,0:T(8,128)(2,1)} %get-tuple-element.23), calls=%async_computation.1 | async-start | bytes 786432 | tf_op jit(solution)/shard_map/all_to_all | solution.py:32
  36.7 0.0 copy-start.5
  36.7 0.6 copy-done.5
  37.3 1.5 shard_map.139
  38.9 2.5 %collective-permute-start = (bf16[30,128,128]{2,1,0:T(8,128)(2,1)}, bf16[30,128,128]{2,1,0:T(8,128)(2,1)S(1)}, u32[]{:S(2)}, u32[]{:S(2)}) collective-permute-start(bf16[30,128,128]{2,1,0:T(8,128)(2,1)} %get-tuple-element.28), channel_id=1, source_target_pairs={{0,8},{8,0},{1,9},{9,1},{2,10},{10,2},{3,11},{11,3},{4,12},{12,4},... | collective-permute-start | bytes 2949128 | tf_op jit(solution)/shard_map/ppermute | solution.py:385
  41.3 3.1 %collective-permute-start.1 = (bf16[16,128,128]{2,1,0:T(8,128)(2,1)}, bf16[16,128,128]{2,1,0:T(8,128)(2,1)}, u32[]{:S(2)}, u32[]{:S(2)}) collective-permute-start(bf16[16,128,128]{2,1,0:T(8,128)(2,1)} %get-tuple-element.29), channel_id=1, source_target_pairs={{0,64},{8,72},{64,0},{72,8},{1,65},{9,73},{65,1},{73,9},{2,66},{10... | collective-permute-start | bytes 1572872 | tf_op jit(solution)/shard_map/ppermute | solution.py:382
  44.5 2.4 %collective-permute-start.2 = (bf16[1024,128]{1,0:T(8,128)(2,1)}, bf16[1024,128]{1,0:T(8,128)(2,1)}, u32[]{:S(2)}, u32[]{:S(2)}) collective-permute-start(bf16[1024,128]{1,0:T(8,128)(2,1)} %w_ref.2), channel_id=1, source_target_pairs={{0,8},{8,0},{1,9},{9,1},{2,10},{10,2},{3,11},{11,3},{4,12},{12,4},... | collective-permute-start | bytes 786440 | tf_op jit(solution)/shard_map/ppermute | solution.py:386
  46.8 5.3 %all-to-all-done.1.part_ref = bf16[64,24,128]{2,1,0:T(8,128)(2,1)S(1)} async-done(((bf16[64,24,128]{2,1,0:T(8,128)(2,1)}), bf16[64,24,128]{2,1,0:T(8,128)(2,1)S(1)}, u32[]{:S(2)}, u32[]{:S(2)}) %all-to-all-start.1) | async-done | bytes 393248 | tf_op jit(solution)/shard_map/all_to_all | solution.py:32
  52.2 1.6 %shard_map.140 = bf16[32,16,128]{2,1,0:T(8,128)(2,1)} custom-call(bf16[64,24,128]{2,1,0:T(8,128)(2,1)S(1)} %all-to-all-done.1.part_ref, bf16[16,128]{1,0:T(8,128)(2,1)S(1)} %get-tuple-element.26.q_ref, f32[2,2,128]{2,1,0:T(2,128)S(1)} %get-tuple-element.27.fresh_ref), custom_call_target="tpu_custom_call" | custom-call | tf_op jit(solution)/shard_map/pallas_call | solution.py:54
  53.8 4.3 %all-to-all-start.2 = ((bf16[32,16,128]{2,1,0:T(8,128)(2,1)}), bf16[32,16,128]{2,1,0:T(8,128)(2,1)S(1)}, u32[]{:S(2)}, u32[]{:S(2)}) async-start(bf16[32,16,128]{2,1,0:T(8,128)(2,1)} %shard_map.140), calls=%async_computation.2 | async-start | bytes 262144 | tf_op jit(solution)/shard_map/all_to_all | solution.py:32
  58.1 4.3 %collective-permute-start.3 = (bf16[16,128,128]{2,1,0:T(8,128)(2,1)}, bf16[16,128,128]{2,1,0:T(8,128)(2,1)S(1)}, u32[]{:S(2)}, u32[]{:S(2)}) collective-permute-start(bf16[16,128,128]{2,1,0:T(8,128)(2,1)} %get-tuple-element.34), channel_id=1, source_target_pairs={{0,72},{8,64},{64,8},{72,0},{1,73},{9,65},{65,9},{73,1},{2,74},{10... | collective-permute-start | bytes 1572872 | tf_op jit(solution)/shard_map/ppermute | solution.py:382
  62.4 0.0 collective-permute-done.1.met2_ref
  62.4 5.6 %all-to-all-done.2.att_ref = bf16[32,16,128]{2,1,0:T(8,128)(2,1)S(1)} async-done(((bf16[32,16,128]{2,1,0:T(8,128)(2,1)}), bf16[32,16,128]{2,1,0:T(8,128)(2,1)S(1)}, u32[]{:S(2)}, u32[]{:S(2)}) %all-to-all-start.2) | async-done | bytes 131104 | tf_op jit(solution)/shard_map/all_to_all | solution.py:32
  68.0 0.0 collective-permute-done.2.met_ref
  68.0 1.4 shard_map.141
  69.4 19.5 %all_to_all.35.part_ref = bf16[8,128,128]{2,1,0:T(8,128)(2,1)S(1)} all-to-all(bf16[8,128,128]{2,1,0:T(8,128)(2,1)S(1)} %bitcast.9), channel_id=1, replica_groups=mesh['yh'=4,'yl'=2,'zl'=4,'core'=2,'zh'=2,'x'=4] {'zh','x'}, dimensions={0} | all-to-all | bytes 524288 | tf_op jit(solution)/shard_map/all_to_all | solution.py:32
  89.0 8.8 %all-gather.1 = bf16[512,128]{1,0:T(8,128)(2,1)S(1)} all-gather(bf16[128,128]{1,0:T(8,128)(2,1)S(1)} %shard_map.142), channel_id=3, replica_groups=mesh['yh'=4,'yl'=2,'zl'=4,'core'=2,'zh'=2,'x'=4] {'yl','core'}, dimensions={0}, use_global_device_ids=true | all-gather | bytes 163840 | tf_op jit(solution)/shard_map/all_gather | solution.py:431
  97.8 0.0 collective-permute-done.3.met3_ref
  97.8 1.7 %shard_map.143 = (bf16[16,120,128]{2,1,0:T(8,128)(2,1)S(1)}, bf16[128,128]{1,0:T(8,128)(2,1)S(1)}) custom-call(bf16[2,2,2,64,128]{4,3,2,1,0:T(8,128)(2,1)S(1)} %bitcast.11, bf16[2,128,128]{2,1,0:T(8,128)(2,1)S(1)} %get-tuple-element.31.mine_ref, bf16[128,3584]{1,0:T(8,128)(2,1)S(1)} %copy-done.1, bf16[128,3584]{1,0:T(8,128)(2,1)S(1)} %copy-done.3, ...), custom_call_target="tpu_custom_call" | custom-call | tf_op jit(solution)/shard_map/pallas_call | solution.py:54
  99.5 17.2 %all_to_all.36.part_ref = bf16[16,120,128]{2,1,0:T(8,128)(2,1)S(1)} all-to-all(bf16[16,120,128]{2,1,0:T(8,128)(2,1)S(1)} %get-tuple-element.35), channel_id=1, replica_groups=mesh['yh'=4,'yl'=2,'zl'=4,'core'=2,'zh'=2,'x'=4] {'yh','zl'}, dimensions={0} | all-to-all | bytes 983040 | tf_op jit(solution)/shard_map/all_to_all | solution.py:32
  116.8 0.2 shard_map.144
  117.0 23.6 %all_to_all.37 = bf16[32,56,128]{2,1,0:T(8,128)(2,1)S(1)} all-to-all(bf16[32,56,128]{2,1,0:T(8,128)(2,1)S(1)} %shard_map.144), channel_id=1, replica_groups=mesh['yh'=4,'yl'=2,'zl'=4,'core'=2,'zh'=2,'x'=4] {'yh','yl','zl'}, dimensions={0} | all-to-all | bytes 917504 | tf_op jit(solution)/shard_map/all_to_all | solution.py:32
  140.6 1.2 shard_map.145
  141.7 15.3 %all_to_all.38.part_ref = bf16[16,16,128]{2,1,0:T(8,128)(2,1)S(1)} all-to-all(bf16[16,16,128]{2,1,0:T(8,128)(2,1)S(1)} %bitcast.12), channel_id=1, replica_groups=mesh['yh'=4,'yl'=2,'zl'=4,'core'=2,'zh'=2,'x'=4] {'core','zh','x'}, dimensions={0} | all-to-all | bytes 131072 | tf_op jit(solution)/shard_map/all_to_all | solution.py:32
  157.0 0.6 shard_map.146
  (11 shorter events, 0.1 us)
Async XLA Ops:
  1.4 23.4 %all-to-all-start = ((bf16[32,16,128]{2,1,0:T(8,128)(2,1)}), bf16[32,16,128]{2,1,0:T(8,128)(2,1)S(1)}, u32[]{:S(2)}, u32[]{:S(2)}) async-start(bf16[32,16,128]{2,1,0:T(8,128)(2,1)} %get-tuple-element.22), calls=%async_computation | async-start | bytes 262144 | tf_op jit(solution)/shard_map/all_to_all | solution.py:32
  24.8 11.9 %copy-start.2 = (bf16[128,3584]{1,0:T(8,128)(2,1)S(1)}, bf16[128,3584]{1,0:T(8,128)(2,1)}, u32[]{:S(2)}) copy-start(bf16[128,3584]{1,0:T(8,128)(2,1)} %up_ref.3) | copy-start | bytes 2752516
  28.6 8.1 %copy-start = (bf16[3584,128]{1,0:T(8,128)(2,1)S(1)}, bf16[3584,128]{1,0:T(8,128)(2,1)}, u32[]{:S(2)}) copy-start(bf16[3584,128]{1,0:T(8,128)(2,1)} %w_ref.3) | copy-start | bytes 2752516
  28.6 8.1 %copy-start.1 = (bf16[128,3584]{1,0:T(8,128)(2,1)S(1)}, bf16[128,3584]{1,0:T(8,128)(2,1)}, u32[]{:S(2)}) copy-start(bf16[128,3584]{1,0:T(8,128)(2,1)} %gate_ref.3) | copy-start | bytes 2752516
  32.2 4.5 %copy-start.4 = (bf16[128,128]{1,0:T(8,128)(2,1)S(1)}, bf16[128,128]{1,0:T(8,128)(2,1)}, u32[]{:S(2)}) copy-start(bf16[128,128]{1,0:T(8,128)(2,1)} %resid_ref.1) | copy-start | bytes 98308
  32.2 19.9 %all-to-all-start.1 = ((bf16[64,24,128]{2,1,0:T(8,128)(2,1)}), bf16[64,24,128]{2,1,0:T(8,128)(2,1)S(1)}, u32[]{:S(2)}, u32[]{:S(2)}) async-start(bf16[64,24,128]{2,1,0:T(8,128)(2,1)} %get-tuple-element.23), calls=%async_computation.1 | async-start | bytes 786432 | tf_op jit(solution)/shard_map/all_to_all | solution.py:32
  36.7 0.7 copy-start.5
  38.9 23.5 %collective-permute-start = (bf16[30,128,128]{2,1,0:T(8,128)(2,1)}, bf16[30,128,128]{2,1,0:T(8,128)(2,1)S(1)}, u32[]{:S(2)}, u32[]{:S(2)}) collective-permute-start(bf16[30,128,128]{2,1,0:T(8,128)(2,1)} %get-tuple-element.28), channel_id=1, source_target_pairs={{0,8},{8,0},{1,9},{9,1},{2,10},{10,2},{3,11},{11,3},{4,12},{12,4},... | collective-permute-start | bytes 2949128 | tf_op jit(solution)/shard_map/ppermute | solution.py:385
  41.3 21.1 %collective-permute-start.1 = (bf16[16,128,128]{2,1,0:T(8,128)(2,1)}, bf16[16,128,128]{2,1,0:T(8,128)(2,1)}, u32[]{:S(2)}, u32[]{:S(2)}) collective-permute-start(bf16[16,128,128]{2,1,0:T(8,128)(2,1)} %get-tuple-element.29), channel_id=1, source_target_pairs={{0,64},{8,72},{64,0},{72,8},{1,65},{9,73},{65,1},{73,9},{2,66},{10... | collective-permute-start | bytes 1572872 | tf_op jit(solution)/shard_map/ppermute | solution.py:382
  44.5 23.6 %collective-permute-start.2 = (bf16[1024,128]{1,0:T(8,128)(2,1)}, bf16[1024,128]{1,0:T(8,128)(2,1)}, u32[]{:S(2)}, u32[]{:S(2)}) collective-permute-start(bf16[1024,128]{1,0:T(8,128)(2,1)} %w_ref.2), channel_id=1, source_target_pairs={{0,8},{8,0},{1,9},{9,1},{2,10},{10,2},{3,11},{11,3},{4,12},{12,4},... | collective-permute-start | bytes 786440 | tf_op jit(solution)/shard_map/ppermute | solution.py:386
  53.8 14.3 %all-to-all-start.2 = ((bf16[32,16,128]{2,1,0:T(8,128)(2,1)}), bf16[32,16,128]{2,1,0:T(8,128)(2,1)S(1)}, u32[]{:S(2)}, u32[]{:S(2)}) async-start(bf16[32,16,128]{2,1,0:T(8,128)(2,1)} %shard_map.140), calls=%async_computation.2 | async-start | bytes 262144 | tf_op jit(solution)/shard_map/all_to_all | solution.py:32
  58.1 39.7 %collective-permute-start.3 = (bf16[16,128,128]{2,1,0:T(8,128)(2,1)}, bf16[16,128,128]{2,1,0:T(8,128)(2,1)S(1)}, u32[]{:S(2)}, u32[]{:S(2)}) collective-permute-start(bf16[16,128,128]{2,1,0:T(8,128)(2,1)} %get-tuple-element.34), channel_id=1, source_target_pairs={{0,72},{8,64},{64,8},{72,0},{1,73},{9,65},{65,9},{73,1},{2,74},{10... | collective-permute-start | bytes 1572872 | tf_op jit(solution)/shard_map/ppermute | solution.py:382
  68.0 29.8 %copy-start.3 = (bf16[128,3584]{1,0:T(8,128)(2,1)S(1)}, bf16[128,3584]{1,0:T(8,128)(2,1)}, u32[]{:S(2)}) copy-start(bf16[128,3584]{1,0:T(8,128)(2,1)} %up_ref.3) | copy-start | bytes 2752516
